TPU v7x, 256 devices: a whole 4x4x8 slice. The times are simulated.
256 devices in a mesh: chain: 64 (over z, y, core), col: 4 (over x).
Axes of the slice: x: 4, y: 4, z: 8, core: 2. Of those that a mesh axis runs over, the one named last changes fastest.
Arguments:
- rhs: bfloat16 [4, 64, 32, 128], P(None, 'chain'), may hold values from -6 to 6
- pattern: int32 [4, 64, 24], P(None, 'chain', 'col'), may hold values from 0 to 255, as said below
- factor: bfloat16 [4, 64, 24, 128, 128], P(None, 'chain', 'col'), may hold values from -0.1875 to 0.1875
- inverse: bfloat16 [4, 64, 128, 128], P(None, 'chain'), as said below
- level_size: int32 [6], replicated, may hold values from 1 to 64, 256 in all
Outputs:
- half_solved: bfloat16 [4, 64, 32, 128], P(None, 'chain')
- solved: bfloat16 [4, 64, 32, 128], P(None, 'chain')
Inputs may be any that keep to these rules, and one draw needn't show every extreme that they name: Among the pattern entries held by one index of chain and one index of col (all 4 of its block rows), at most 2 name block rows on any one index of chain (block row mod 64); in every such group exactly 2 name block rows on one index of chain that is common to all groups of that index of col. A block row may name a block row more than once. `inverse`: each block is lower triangular with a diagonal between 0.3 and 2.
All inputs are finite; a program needn't handle non-finite values.
Results may differ from a plain program's by a relative error of at most 0.013.
Values may be sent and summed in bfloat16 or wider, within the bound.
No kernel may reach another device: no remote copies, remote signals or barrier semaphores. Data moves between devices by JAX's collectives and lax.ppermute only.
A program may use at most 64 MiB of HBM per device.

v0:
```python
import jax
import jax.numpy as jnp
from jax import lax
from jax.sharding import PartitionSpec as P


def level_index(positions, ends):
    return jnp.sum((positions[..., None] >= ends).astype(jnp.int32), axis=-1)


def per_device(rhs, pattern, factor, inverse, level_size):
    lane_count = lax.axis_size("chain")
    chain_pos = lax.axis_index("chain")
    row_count = rhs.shape[0]
    probe_count = rhs.shape[2]
    width = rhs.shape[3]
    entries = pattern.shape[2]
    level_count = level_size.shape[0]
    total = row_count * lane_count
    ends = jnp.cumsum(level_size)
    starts = ends - level_size
    own_rows = jnp.arange(row_count, dtype=jnp.int32) * lane_count + chain_pos
    own_level = level_index(own_rows, ends)
    columns = pattern[:, 0, :]
    column_level = level_index(columns, ends)
    keep = column_level < own_level[:, None]
    blocks = factor[:, 0]
    inverse_rows = inverse[:, 0]
    right = rhs[:, 0]
    slot_ids = jnp.arange(row_count, dtype=jnp.int32)
    lane_ids = jnp.arange(lane_count, dtype=jnp.int32)

    def locate(level):
        picked = own_level == level
        own_slot = jnp.sum(jnp.where(picked, slot_ids, 0))
        return (picked, own_slot, jnp.any(picked))

    def forward_level(level, carry):
        store, half_local = carry
        picked, own_slot, is_live = locate(level)
        wanted = keep[own_slot] & is_live
        chosen = jnp.where(
            wanted[:, None, None], store[columns[own_slot]], jnp.zeros((), jnp.bfloat16)
        )
        partial_value = jnp.einsum(
            "jpb,jcb->pc", chosen, blocks[own_slot], preferred_element_type=jnp.float32
        )
        summed = lax.psum(partial_value, "col")
        rest = (right[own_slot].astype(jnp.float32) - summed).astype(jnp.bfloat16)
        segment = jnp.dot(
            rest, inverse_rows[own_slot].T, preferred_element_type=jnp.float32
        ).astype(jnp.bfloat16)
        segment = jnp.where(is_live, segment, jnp.zeros((), jnp.bfloat16))
        front = lax.all_gather(segment[None], "chain", axis=0, tiled=True)
        half_local = jnp.where(picked[:, None, None], segment[None], half_local)
        start = starts[level]
        ordered = front[(start + lane_ids) % lane_count]
        store = lax.dynamic_update_slice_in_dim(store, ordered, start, 0)
        return (store, half_local)

    store = jnp.zeros((total + lane_count, probe_count, width), jnp.bfloat16)
    half_local = jnp.zeros((row_count, probe_count, width), jnp.bfloat16)
    store, half_local = lax.fori_loop(0, level_count, forward_level, (store, half_local))
    solved_local = jnp.zeros((row_count, probe_count, width), jnp.bfloat16)

    def backward_level(counter, carry):
        pending, solved_now = carry
        level = level_count - 1 - counter
        picked, own_slot, is_live = locate(level)
        target = (column_level == level) & keep
        hits = ((columns % lane_count)[None] == lane_ids[:, None, None]) & target[None]
        hits = hits.astype(jnp.float32).reshape(lane_count, row_count * entries)
        terms = jnp.dot(
            hits,
            pending.reshape(row_count * entries, probe_count * width),
            precision=lax.Precision.HIGHEST,
            preferred_element_type=jnp.float32,
        )
        terms = terms.reshape(lane_count, probe_count, width)
        own_half = half_local[own_slot]
        mine = lax.psum_scatter(terms, "chain", scatter_dimension=0, tiled=True)[0]
        summed = lax.psum(mine, "col")
        rest = (own_half.astype(jnp.float32) - summed).astype(jnp.bfloat16)
        segment = jnp.dot(rest, inverse_rows[own_slot], preferred_element_type=jnp.float32).astype(
            jnp.bfloat16
        )
        segment = jnp.where(is_live, segment, jnp.zeros((), jnp.bfloat16))
        solved_now = jnp.where(picked[:, None, None], segment[None], solved_now)
        fresh = jnp.einsum(
            "pc,jcb->jpb", segment, blocks[own_slot], preferred_element_type=jnp.float32
        )
        fresh = jnp.where(keep[own_slot][:, None, None], fresh, 0.0)
        pending = jnp.where(picked[:, None, None, None], fresh[None], pending)
        return (pending, solved_now)

    pending = jnp.zeros((row_count, entries, probe_count, width), jnp.float32)
    pending, solved_local = lax.fori_loop(0, level_count, backward_level, (pending, solved_local))
    return (half_local[:, None], solved_local[:, None])


def solution(mesh):
    return jax.shard_map(
        per_device,
        mesh=mesh,
        in_specs=(
            P(None, "chain", None, None),
            P(None, "chain", "col"),
            P(None, "chain", "col", None, None),
            P(None, "chain", None, None),
            P(),
        ),
        out_specs=(P(None, "chain", None, None), P(None, "chain", None, None)),
        check_vma=False,
    )
```

profile of v0, /device:TPU:1, one launch (start us, length us, event | category | flops | bytes accessed | tf_op | source)
XLA Modules:
  0.0 1427.0 jit_solution(11156799697766740432)
XLA Ops:
  11.9 464.5 %while.38 = (s32[]{:T(128)}, bf16[320,32,128]{2,1,0:T(8,128)(2,1)}, bf16[4,32,128]{2,1,0:T(8,128)(2,1)S(1)}, s32[4]{0:T(128)S(1)}, bf16[4,32,128]{2,1,0:T(8,128)...) while((s32[]{:T(128)}, bf16[320,32,128]{2,1,0:T(8,128)(2,1)}, ...), condition=%wide.region_7.8_spmd.clone, body=%wide.region_3.7_spmd.clone.sunk | while | flops 7425007 | bytes 3173509 | solution.py:63
  15.8 2.3 gather_fusion
  18.3 14.2 psum.34
  34.0 57.6 %all-gather.3 = bf16[2048,128]{1,0:T(8,128)(2,1)S(1)} all-gather(bf16[32,128]{1,0:T(8,128)(2,1)S(1)} %fusion.91), channel_id=2, replica_groups=mesh['chain'=64,'col'=4] {'chain'}, dimensions={0}, use_global_device_ids=true | all-gather | bytes 532480 | tf_op jit(solution)/shard_map/while/body/eval_jaxpr/all_gather | solution.py:54
  100.2 2.3 gather_fusion
  102.7 11.1 psum.34
  115.3 52.3 %all-gather.3 = bf16[2048,128]{1,0:T(8,128)(2,1)S(1)} all-gather(bf16[32,128]{1,0:T(8,128)(2,1)S(1)} %fusion.91), channel_id=2, replica_groups=mesh['chain'=64,'col'=4] {'chain'}, dimensions={0}, use_global_device_ids=true | all-gather | bytes 532480 | tf_op jit(solution)/shard_map/while/body/eval_jaxpr/all_gather | solution.py:54
  176.2 2.3 gather_fusion
  178.7 11.7 psum.34
  191.9 51.7 %all-gather.3 = bf16[2048,128]{1,0:T(8,128)(2,1)S(1)} all-gather(bf16[32,128]{1,0:T(8,128)(2,1)S(1)} %fusion.91), channel_id=2, replica_groups=mesh['chain'=64,'col'=4] {'chain'}, dimensions={0}, use_global_device_ids=true | all-gather | bytes 532480 | tf_op jit(solution)/shard_map/while/body/eval_jaxpr/all_gather | solution.py:54
  252.2 2.3 gather_fusion
  254.7 11.1 psum.34
  267.3 52.3 %all-gather.3 = bf16[2048,128]{1,0:T(8,128)(2,1)S(1)} all-gather(bf16[32,128]{1,0:T(8,128)(2,1)S(1)} %fusion.91), channel_id=2, replica_groups=mesh['chain'=64,'col'=4] {'chain'}, dimensions={0}, use_global_device_ids=true | all-gather | bytes 532480 | tf_op jit(solution)/shard_map/while/body/eval_jaxpr/all_gather | solution.py:54
  328.3 2.3 gather_fusion
  330.8 11.7 psum.34
  343.9 51.7 %all-gather.3 = bf16[2048,128]{1,0:T(8,128)(2,1)S(1)} all-gather(bf16[32,128]{1,0:T(8,128)(2,1)S(1)} %fusion.91), channel_id=2, replica_groups=mesh['chain'=64,'col'=4] {'chain'}, dimensions={0}, use_global_device_ids=true | all-gather | bytes 532480 | tf_op jit(solution)/shard_map/while/body/eval_jaxpr/all_gather | solution.py:54
  404.2 2.3 gather_fusion
  406.7 11.1 psum.34
  419.3 52.4 %all-gather.3 = bf16[2048,128]{1,0:T(8,128)(2,1)S(1)} all-gather(bf16[32,128]{1,0:T(8,128)(2,1)S(1)} %fusion.91), channel_id=2, replica_groups=mesh['chain'=64,'col'=4] {'chain'}, dimensions={0}, use_global_device_ids=true | all-gather | bytes 532480 | tf_op jit(solution)/shard_map/while/body/eval_jaxpr/all_gather | solution.py:54
  476.8 942.8 %while.39 = (s32[]{:T(128)}, f32[4,6,32,128]{3,2,1,0:T(8,128)S(1)}, bf16[4,32,128]{2,1,0:T(8,128)(2,1)S(1)}, s32[4]{0:T(128)S(1)}, pred[4,6]{1,0:T(4,128)(4,1)S(...) while((s32[]{:T(128)}, f32[4,6,32,128]{3,2,1,0:T(8,128)S(1)}, ...), condition=%wide.wide.region_13.14_spmd.clone, body=%wide.wide.region_8.13_spmd.clone.sunk | while | flops 83217712 | bytes 8882577 | solution.py:97
  482.3 128.6 %reduce-scatter.7.cloned.1.call-done = f32[1,32,128]{2,1,0:T(8,128)} async-done(((f32[64,32,128]{2,1,0:T(8,128)}), f32[1,32,128]{2,1,0:T(8,128)}) %reduce-scatter.7.cloned.1.call-update) | async-done | bytes 16400 | tf_op jit(solution)/shard_map/while
  610.9 13.4 psum.35
  631.1 138.5 %reduce-scatter.7.cloned.1.call-done = f32[1,32,128]{2,1,0:T(8,128)} async-done(((f32[64,32,128]{2,1,0:T(8,128)}), f32[1,32,128]{2,1,0:T(8,128)}) %reduce-scatter.7.cloned.1.call-update) | async-done | bytes 16400 | tf_op jit(solution)/shard_map/while
  769.6 13.7 psum.35
  790.1 138.8 %reduce-scatter.7.cloned.1.call-done = f32[1,32,128]{2,1,0:T(8,128)} async-done(((f32[64,32,128]{2,1,0:T(8,128)}), f32[1,32,128]{2,1,0:T(8,128)}) %reduce-scatter.7.cloned.1.call-update) | async-done | bytes 16400 | tf_op jit(solution)/shard_map/while
  928.9 13.7 psum.35
  949.4 138.2 %reduce-scatter.7.cloned.1.call-done = f32[1,32,128]{2,1,0:T(8,128)} async-done(((f32[64,32,128]{2,1,0:T(8,128)}), f32[1,32,128]{2,1,0:T(8,128)}) %reduce-scatter.7.cloned.1.call-update) | async-done | bytes 16400 | tf_op jit(solution)/shard_map/while
  1087.6 13.7 psum.35
  1108.0 137.9 %reduce-scatter.7.cloned.1.call-done = f32[1,32,128]{2,1,0:T(8,128)} async-done(((f32[64,32,128]{2,1,0:T(8,128)}), f32[1,32,128]{2,1,0:T(8,128)}) %reduce-scatter.7.cloned.1.call-update) | async-done | bytes 16400 | tf_op jit(solution)/shard_map/while
  1245.9 13.7 psum.35
  1266.4 138.7 %reduce-scatter.7.cloned.1.call-done = f32[1,32,128]{2,1,0:T(8,128)} async-done(((f32[64,32,128]{2,1,0:T(8,128)}), f32[1,32,128]{2,1,0:T(8,128)}) %reduce-scatter.7.cloned.1.call-update) | async-done | bytes 16400 | tf_op jit(solution)/shard_map/while
  1405.0 13.3 psum.35
  (194 shorter events, 74.4 us)
Async XLA Ops:
  7.2 4.8 copy-start.4
  7.2 4.8 copy-start
  7.2 4.8 copy-start.3
  476.8 134.1 %reduce-scatter.7.cloned.1.call-start = ((), (), s32[]{:S(2)}) async-start(), calls=%async_computation.1 | async-start | bytes 1064960 | tf_op jit(solution)/shard_map/while
  625.5 144.2 %reduce-scatter.7.cloned.1.call-start = ((), (), s32[]{:S(2)}) async-start(), calls=%async_computation.1 | async-start | bytes 1064960 | tf_op jit(solution)/shard_map/while
  784.5 144.4 %reduce-scatter.7.cloned.1.call-start = ((), (), s32[]{:S(2)}) async-start(), calls=%async_computation.1 | async-start | bytes 1064960 | tf_op jit(solution)/shard_map/while
  943.8 143.8 %reduce-scatter.7.cloned.1.call-start = ((), (), s32[]{:S(2)}) async-start(), calls=%async_computation.1 | async-start | bytes 1064960 | tf_op jit(solution)/shard_map/while
  1102.4 143.5 %reduce-scatter.7.cloned.1.call-start = ((), (), s32[]{:S(2)}) async-start(), calls=%async_computation.1 | async-start | bytes 1064960 | tf_op jit(solution)/shard_map/while
  1260.8 144.3 %reduce-scatter.7.cloned.1.call-start = ((), (), s32[]{:S(2)}) async-start(), calls=%async_computation.1 | async-start | bytes 1064960 | tf_op jit(solution)/shard_map/while
  1419.5 0.6 copy-start.1
  1419.5 0.6 copy-start.2
Sparse Core Ops, SparseCore 0:
  481.6 129.2 reduce-scatter.6
  630.3 139.2 reduce-scatter.6
  789.3 139.5 reduce-scatter.6
  948.3 139.2 reduce-scatter.6
  1106.9 138.9 reduce-scatter.6
  1265.3 139.7 reduce-scatter.6
where the time goes:
time: 1440 us; the launch traced here: 1430 us
  waiting for transfers between devices  821 us (57%)
  blocking collectives  470 us (33%)
  local copies, waits for them, and re-layouts  40.2 us (3%)
  loops' own time  33.6 us (2%)
  other arithmetic  27.2 us (2%)
  matrix products  20.5 us (1%)
    while x12, waiting for transfers between devices  821 us
    all_gather x6, blocking collectives, forward_level(): front = lax.all_gather(segment[None], 'chain', axis=0, tiled=True)  318 us
    psum x6, blocking collectives, backward_level(): summed = lax.psum(mine, 'col')  81.5 us
    psum x6, blocking collectives, forward_level(): summed = lax.psum(partial_value, 'col')  71 us
  transfers between devices with their start and end apart: 6, of which 6 were waited for; matrix products, arithmetic and copies ran while one was open for 1% of the time, Pallas kernels for 0%

commit v1 on v0

v1 whole, which is shorter than its diff:
```python
import functools
import jax
import jax.numpy as jnp
from jax import lax
from jax.experimental import pallas as pl
from jax.experimental.pallas import tpu as pltpu
from jax.sharding import PartitionSpec as P

BF16 = jnp.bfloat16
F32 = jnp.float32
NT = (((1,), (1,)), ((), ()))
NN = (((1,), (0,)), ((), ()))


def locate(level, sizes, lanes, rows):
    lane = lax.axis_index("chain")
    start = jnp.int32(0)
    for k in range(level):
        start = start + sizes[k]
    slot = (start - lane + (lanes - 1)) // lanes
    live = (slot < rows) & (slot * lanes + lane < start + sizes[level])
    return jnp.minimum(slot, rows - 1), live


def start_all(copies):
    for c in copies:
        c.start()


def wait_all(copies):
    for c in copies:
        c.wait()


def factor_copies(cols, entries, slot, fac, fbuf, sems, base):
    return [
        pltpu.make_async_copy(
            fac.at[q, pl.ds(slot * entries, entries)],
            fbuf.at[pl.ds(q * entries, entries)],
            sems.at[base + q],
        )
        for q in range(cols)
    ]


def wide(fbuf, total):
    return jnp.concatenate([fbuf[j] for j in range(total)], axis=1)


def half_segment(level, lanes, total, slot, index, rest, inv, fbuf, store):
    if level > 0:
        chosen = jnp.concatenate(
            [
                store[jnp.minimum(index[slot * total + j], level * lanes)]
                for j in range(total)
            ],
            axis=1,
        )
        summed = lax.dot_general(
            chosen, wide(fbuf, total), NT, preferred_element_type=F32
        )
        rest = (rest.astype(F32) - summed).astype(BF16)
    return lax.dot_general(rest, inv, NT, preferred_element_type=F32).astype(BF16)


def forward_first(lanes, rows, sizes, right, inverse, out, rbuf, ibuf, sems):
    slot, _ = locate(0, sizes, lanes, rows)
    copies = [
        pltpu.make_async_copy(right.at[slot], rbuf, sems.at[0]),
        pltpu.make_async_copy(inverse.at[slot], ibuf, sems.at[1]),
    ]
    start_all(copies)
    wait_all(copies)
    segment = half_segment(0, lanes, 0, slot, None, rbuf[...], ibuf[...], None, None)
    out[...] = jnp.broadcast_to(segment[None], out.shape)


def forward_level(level, lanes, rows, cols, entries, *refs):
    sizes, index, right, inverse, fac = refs[:5]
    earlier = refs[5 : 5 + level]
    out, rbuf, ibuf, fbuf, store, sems = refs[5 + level :]
    total = cols * entries
    slot, _ = locate(level, sizes, lanes, rows)
    copies = [
        pltpu.make_async_copy(right.at[slot], rbuf, sems.at[0]),
        pltpu.make_async_copy(inverse.at[slot], ibuf, sems.at[1]),
    ]
    copies += [
        pltpu.make_async_copy(
            earlier[k], store.at[pl.ds(k * lanes, lanes)], sems.at[2 + k]
        )
        for k in range(level)
    ]
    copies += factor_copies(cols, entries, slot, fac, fbuf, sems, 2 + level)
    start_all(copies)
    store[level * lanes] = jnp.zeros(store.shape[1:], BF16)
    wait_all(copies)
    segment = half_segment(
        level, lanes, total, slot, index, rbuf[...], ibuf[...], fbuf, store
    )
    out[...] = jnp.broadcast_to(segment[None], out.shape)


def add_terms(level, lanes, total, slot, live, index, segment, fbuf, acc):
    segment = jnp.where(live, segment.astype(F32), 0.0).astype(BF16)
    terms = lax.dot_general(segment, wide(fbuf, total), NN, preferred_element_type=F32)
    width = segment.shape[1]
    for j in range(total):
        at = jnp.minimum(index[slot * total + j], level * lanes)
        acc[at] = acc[at] + terms[:, j * width : (j + 1) * width]


def turn_level(level, lanes, rows, cols, entries, *refs):
    sizes, index, right, inverse, fac = refs[:5]
    earlier = refs[5 : 5 + level]
    half, solved, kept, out, rbuf, ibuf, fbuf, store, acc, sems = refs[5 + level :]
    total = cols * entries
    slot, live = locate(level, sizes, lanes, rows)
    copies = [
        pltpu.make_async_copy(right.at[slot], rbuf, sems.at[0]),
        pltpu.make_async_copy(inverse.at[slot], ibuf, sems.at[1]),
    ]
    copies += [
        pltpu.make_async_copy(
            earlier[k], store.at[pl.ds(k * lanes, lanes)], sems.at[2 + k]
        )
        for k in range(level)
    ]
    copies += factor_copies(cols, entries, slot, fac, fbuf, sems, 2 + level)
    start_all(copies)
    store[level * lanes] = jnp.zeros(store.shape[1:], BF16)
    acc[...] = jnp.zeros(acc.shape, F32)
    wait_all(copies)
    segment = half_segment(
        level, lanes, total, slot, index, rbuf[...], ibuf[...], fbuf, store
    )
    half[...] = segment
    segment = lax.dot_general(
        segment, ibuf[...], NN, preferred_element_type=F32
    ).astype(BF16)
    solved[...] = segment
    add_terms(level, lanes, total, slot, live, index, segment, fbuf, acc)
    below = (level - 1) * lanes
    save = pltpu.make_async_copy(acc.at[pl.ds(0, below)], kept, sems.at[0])
    save.start()
    out[...] = acc[pl.ds(below, lanes)].astype(BF16)
    save.wait()


def backward_level(level, lanes, rows, cols, entries, *refs):
    sizes, index, inverse, fac, fronts, arrived, pending = refs[:7]
    refs = refs[7:]
    solved, refs = refs[0], refs[1:]
    kept = None
    if level > 1:
        kept, refs = refs[0], refs[1:]
    out, hbuf, ibuf, fbuf, tbuf, acc, sems = refs
    total = cols * entries
    slot, live = locate(level, sizes, lanes, rows)
    first = [
        pltpu.make_async_copy(arrived, tbuf, sems.at[0]),
        pltpu.make_async_copy(inverse.at[slot], ibuf, sems.at[1]),
        pltpu.make_async_copy(
            fronts.at[lax.axis_index("chain")], hbuf, sems.at[2]
        ),
    ]
    later = factor_copies(cols, entries, slot, fac, fbuf, sems, 3)
    later.append(
        pltpu.make_async_copy(
            pending, acc.at[pl.ds(0, level * lanes)], sems.at[3 + cols]
        )
    )
    start_all(first + later)
    wait_all(first)
    summed = jnp.sum(tbuf[...].astype(F32), axis=0)
    rest = (hbuf[...].astype(F32) - summed).astype(BF16)
    segment = lax.dot_general(rest, ibuf[...], NN, preferred_element_type=F32).astype(
        BF16
    )
    solved[...] = segment
    wait_all(later)
    add_terms(level, lanes, total, slot, live, index, segment, fbuf, acc)
    below = (level - 1) * lanes
    if kept is not None:
        save = pltpu.make_async_copy(acc.at[pl.ds(0, below)], kept, sems.at[0])
        save.start()
    out[...] = acc[pl.ds(below, lanes)].astype(BF16)
    if kept is not None:
        save.wait()


def finish(levels, lanes, rows, cols, *refs):
    sizes, inverse, arrived = refs[:3]
    fronts = refs[3 : 3 + levels - 1]
    refs = refs[3 + levels - 1 :]
    half_last = refs[0]
    done = refs[1:levels]
    out, hbuf, sbuf, ibuf, tbuf, sems = refs[levels:]
    lane = lax.axis_index("chain")
    slot, _ = locate(0, sizes, lanes, rows)
    first = [
        pltpu.make_async_copy(arrived, tbuf, sems.at[0]),
        pltpu.make_async_copy(inverse.at[slot], ibuf, sems.at[1]),
    ]
    first += [
        pltpu.make_async_copy(fronts[k].at[lane], hbuf.at[k], sems.at[2 + k])
        for k in range(levels - 1)
    ]
    first.append(
        pltpu.make_async_copy(half_last, hbuf.at[levels - 1], sems.at[1 + levels])
    )
    first += [
        pltpu.make_async_copy(done[k - 1], sbuf.at[k], sems.at[1 + levels + k])
        for k in range(1, levels)
    ]
    start_all(first)
    wait_all(first)
    summed = jnp.sum(tbuf[...].astype(F32), axis=0)
    rest = (hbuf[0].astype(F32) - summed).astype(BF16)
    sbuf[0] = lax.dot_general(rest, ibuf[...], NN, preferred_element_type=F32).astype(
        BF16
    )
    for r in range(rows):
        row = r * lanes + lane
        end = jnp.int32(0)
        level = jnp.int32(0)
        for k in range(levels):
            end = end + sizes[k]
            level = level + (row >= end).astype(jnp.int32)
        h, s = hbuf[level], sbuf[level]
        for q in range(cols):
            out[q, r] = h
            out[q, rows + r] = s


def per_device(rhs, pattern, factor, inverse, level_size):
    lanes = lax.axis_size("chain")
    cols = lax.axis_size("col")
    lane = lax.axis_index("chain")
    rows, _, probes, width = rhs.shape
    entries = pattern.shape[2]
    levels = level_size.shape[0]
    share = probes // cols
    total = cols * entries
    inverse = inverse[:, 0]
    right = lax.dynamic_index_in_dim(
        rhs.reshape(rows, cols, share, width), lax.axis_index("col"), 1, keepdims=False
    )

    smem = pl.BlockSpec(memory_space=pltpu.SMEM)
    hbm = pl.BlockSpec(memory_space=pl.ANY)
    vmem = pl.BlockSpec(memory_space=pltpu.VMEM)
    segment_shape = jax.ShapeDtypeStruct((share, width), BF16)
    front_shape = jax.ShapeDtypeStruct((lanes, share, width), BF16)
    params = pltpu.CompilerParams(vmem_limit_bytes=12 * 1024 * 1024)
    rbuf = pltpu.VMEM((share, width), BF16)
    ibuf = pltpu.VMEM((width, width), BF16)
    fbuf = pltpu.VMEM((total, width, width), BF16)

    def exchange(x):
        return lax.all_to_all(x, "chain", 0, 0, tiled=True)

    codes = jnp.pad(
        pattern.reshape(1, 1, rows * entries).astype(BF16),
        ((0, 0), (0, width - 1), (0, width - rows * entries)),
    )
    fac = lax.all_gather(
        jnp.concatenate([factor.reshape(rows * entries, width, width), codes]), "col"
    )
    columns = fac[:, rows * entries, 0, : rows * entries].astype(jnp.int32)
    columns = columns.reshape(cols, rows, entries).transpose(1, 0, 2)
    own_rows = jnp.arange(rows, dtype=jnp.int32) * lanes + lane
    own_level = jnp.zeros_like(own_rows)
    level = jnp.zeros_like(columns)
    end = jnp.int32(0)
    for k in range(levels):
        end = end + level_size[k]
        own_level += (own_rows >= end).astype(jnp.int32)
        level += (columns >= end).astype(jnp.int32)
    index = jnp.where(
        level < own_level[:, None, None],
        level * lanes + columns % lanes,
        levels * lanes,
    ).reshape(rows * total)

    first = pl.pallas_call(
        functools.partial(forward_first, lanes, rows),
        out_shape=front_shape,
        in_specs=[smem, hbm, hbm],
        out_specs=vmem,
        scratch_shapes=[rbuf, ibuf, pltpu.SemaphoreType.DMA((2,))],
        compiler_params=params,
        name="forward_first",
    )(level_size, right, inverse)
    fronts = [exchange(first)]
    for k in range(1, levels - 1):
        mine = pl.pallas_call(
            functools.partial(forward_level, k, lanes, rows, cols, entries),
            out_shape=front_shape,
            in_specs=[smem, smem, hbm, hbm, hbm] + [hbm] * k,
            out_specs=vmem,
            scratch_shapes=[
                rbuf,
                ibuf,
                fbuf,
                pltpu.VMEM((k * lanes + 1, share, width), BF16),
                pltpu.SemaphoreType.DMA((2 + k + cols,)),
            ],
            compiler_params=params,
            name=f"forward_level_{k}",
        )(level_size, index, right, inverse, fac, *fronts)
        fronts.append(exchange(mine))

    last = levels - 1
    half_last, solved, pending, terms = pl.pallas_call(
        functools.partial(turn_level, last, lanes, rows, cols, entries),
        out_shape=(
            segment_shape,
            segment_shape,
            jax.ShapeDtypeStruct(((last - 1) * lanes, share, width), F32),
            front_shape,
        ),
        in_specs=[smem, smem, hbm, hbm, hbm] + [hbm] * last,
        out_specs=(vmem, vmem, hbm, vmem),
        scratch_shapes=[
            rbuf,
            ibuf,
            fbuf,
            pltpu.VMEM((last * lanes + 1, share, width), BF16),
            pltpu.VMEM((last * lanes + 1, share, width), F32),
            pltpu.SemaphoreType.DMA((2 + last + cols,)),
        ],
        compiler_params=params,
        name="turn_level",
    )(level_size, index, right, inverse, fac, *fronts)
    done = [solved]
    for k in range(last - 1, 0, -1):
        arrived = exchange(terms)
        outs = [segment_shape]
        specs = [vmem]
        if k > 1:
            outs.append(jax.ShapeDtypeStruct(((k - 1) * lanes, share, width), F32))
            specs.append(hbm)
        got = pl.pallas_call(
            functools.partial(backward_level, k, lanes, rows, cols, entries),
            out_shape=(*outs, front_shape),
            in_specs=[smem, smem] + [hbm] * 5,
            out_specs=(*specs, vmem),
            scratch_shapes=[
                rbuf,
                ibuf,
                fbuf,
                pltpu.VMEM((lanes, share, width), BF16),
                pltpu.VMEM((k * lanes + 1, share, width), F32),
                pltpu.SemaphoreType.DMA((4 + cols,)),
            ],
            compiler_params=params,
            name=f"backward_level_{k}",
        )(level_size, index, inverse, fac, fronts[k], arrived, pending)
        solved, terms = got[0], got[-1]
        pending = got[1] if k > 1 else None
        done.insert(0, solved)
    arrived = exchange(terms)
    shares = pl.pallas_call(
        functools.partial(finish, levels, lanes, rows, cols),
        out_shape=jax.ShapeDtypeStruct((cols, 2 * rows, share, width), BF16),
        in_specs=[smem] + [hbm] * (2 + 2 * levels - 1),
        out_specs=vmem,
        scratch_shapes=[
            pltpu.VMEM((levels, share, width), BF16),
            pltpu.VMEM((levels, share, width), BF16),
            ibuf,
            pltpu.VMEM((lanes, share, width), BF16),
            pltpu.SemaphoreType.DMA((2 + 2 * levels,)),
        ],
        compiler_params=params,
        name="finish",
    )(level_size, inverse, arrived, *fronts, half_last, *done)
    whole = lax.all_to_all(shares, "col", 0, 0, tiled=True)
    whole = whole.transpose(1, 0, 2, 3).reshape(2, rows, 1, probes, width)
    return whole[0], whole[1]


def solution(mesh):
    return jax.shard_map(
        per_device,
        mesh=mesh,
        in_specs=(
            P(None, "chain", None, None),
            P(None, "chain", "col"),
            P(None, "chain", "col", None, None),
            P(None, "chain", None, None),
            P(),
        ),
        out_specs=(P(None, "chain", None, None), P(None, "chain", None, None)),
        check_vma=False,
    )
```

time: 1440 us -> 242 us (0.17)
  waiting for transfers between devices: 821 us -> 27.5 us
  blocking collectives: 470 us -> 148 us
  local copies, waits for them, and re-layouts: 40.2 us -> 3.54 us
  loops' own time: 33.6 us -> 0 us
  Pallas kernels: 0 us -> 26.3 us
  other arithmetic: 27.2 us -> 4.79 us
  matrix products: 20.5 us -> 0 us
    while x12 -> x0, waiting for transfers between devices: 821 us -> none
    all_gather x6 -> x0, blocking collectives: 318 us -> none  [forward_level(): front = lax.all_gather(segment[None], 'chain', axis=0, tiled=True)]
    psum x12 -> x0, blocking collectives: 152 us -> none  [the longest x6 81.5 us: backward_level(): summed = lax.psum(mine, 'col')]
    all_to_all x0 -> x10, blocking collectives: none -> 148 us  [the longest x9 141 us: exchange(): return lax.all_to_all(x, 'chain', 0, 0, tiled=True)]
    another operation x2 -> x0, loops' own time: 33.6 us -> none  [the longest x1 23.1 us: per_device(): lax.fori_loop(0, level_count, forward_level, (store, half_local))]
    all_gather x0 -> x1, waiting for transfers between devices: none -> 27.5 us  [per_device(): lax.all_gather(jnp.concatenate([factor.reshape(rows * entries, width, wid...]
    pallas_call x0 -> x11, Pallas kernels: none -> 26.3 us  [the longest x4 10.4 us: per_device(): pl.pallas_call(functools.partial(forward_level, k, lanes, rows, cols, ent...]
    dot_general x30 -> x0, matrix products: 20.5 us -> none  [the longest x6 8.82 us: forward_level(): jnp.dot(rest, inverse_rows[own_slot].T, preferred_element_type=jnp.float32)]
  transfers between devices with their start and end apart: 6 -> 2, of which waited for: 6 -> 1; matrix products, arithmetic and copies ran while one was open for 1% -> 1% of each run, Pallas kernels for 0% -> 1%
where the time goes in v1:
time: 242 us; the launch traced here: 241 us
  blocking collectives  148 us (61%)
  waiting for transfers between devices  27.5 us (11%)
  Pallas kernels  26.3 us (11%)
  between operations  18 us (7%)
  starting transfers between devices  13.2 us (5%)
  other arithmetic  4.79 us (2%)
  local copies, waits for them, and re-layouts  3.54 us (1%)
    all_to_all x9, blocking collectives, exchange(): return lax.all_to_all(x, 'chain', 0, 0, tiled=True)  141 us
    all_gather x1, waiting for transfers between devices, per_device(): lax.all_gather(jnp.concatenate([factor.reshape(rows * entries, width, wid...  27.5 us
    all_to_all x1, starting transfers between devices, exchange(): return lax.all_to_all(x, 'chain', 0, 0, tiled=True)  13.2 us
    pallas_call x4, Pallas kernels, per_device(): pl.pallas_call(functools.partial(forward_level, k, lanes, rows, cols, ent...  10.4 us
    pallas_call x4, Pallas kernels, per_device(): pl.pallas_call(functools.partial(backward_level, k, lanes, rows, cols, en...  9.58 us
    all_to_all x1, blocking collectives, per_device(): whole = lax.all_to_all(shares, 'col', 0, 0, tiled=True)  7.2 us
  transfers between devices with their start and end apart: 2, of which 1 were waited for; matrix products, arithmetic and copies ran while one was open for 1% of the time, Pallas kernels for 1%

profile of v1, /device:TPU:1, one launch (start us, length us, event | category | flops | bytes accessed | tf_op | source)
XLA Modules:
  0.0 241.5 jit_solution(5671161244248671454)
XLA Ops:
  7.2 0.7 convert_reduce_fusion
  8.1 2.1 fusion.1
  10.3 1.4 forward_first.1
  11.7 13.2 %all-to-all-start = ((bf16[64,8,128]{2,1,0:T(8,128)(2,1)}), bf16[64,8,128]{2,1,0:T(8,128)(2,1)S(1)}, u32[]{:S(2)}, u32[]{:S(2)}) async-start(bf16[64,8,128]{2,1,0:T(8,128)(2,1)} %forward_first.1), calls=%async_computation | async-start | bytes 262144 | tf_op jit(solution)/shard_map/all_to_all | solution.py:261
  24.9 0.7 fusion.12
  29.3 0.6 fusion.10
  29.9 27.5 %all-gather.3.cloned.1.call-done = bf16[100,128,128]{2,1,0:T(8,128)(2,1)} async-done(((bf16[25,128,128]{2,1,0:T(8,128)(2,1)}), bf16[100,128,128]{2,1,0:T(8,128)(2,1)}) %all-gather.3.cloned.1.call-update) | async-done | bytes 3276816 | tf_op jit(solution)/shard_map/all_gather | solution.py:267
  57.4 0.7 fusion.5
  58.2 0.6 fusion.4
  58.8 0.1 reshape.59.refs_1_
  58.9 1.9 copy-done.1
  60.9 2.3 forward_level_1.1
  63.2 21.6 %all_to_all.55.refs_6_.refs_4_ = bf16[64,8,128]{2,1,0:T(8,128)(2,1)S(1)} all-to-all(bf16[64,8,128]{2,1,0:T(8,128)(2,1)S(1)} %forward_level_1.1), channel_id=1, replica_groups=mesh['chain'=64,'col'=4] {'chain'}, dimensions={0} | all-to-all | bytes 262144 | tf_op jit(solution)/shard_map/all_to_all | solution.py:261
  84.8 2.5 %forward_level_2.1 = bf16[64,8,128]{2,1,0:T(8,128)(2,1)S(1)} custom-call(s32[6]{0:T(128)S(1)} %copy-done.4, s32[96]{0:T(128)S(1)} %reshape.59.refs_1_, bf16[4,8,128]{2,1,0:T(8,128)(2,1)S(1)} %dynamic-slice_bitcast_fusion.right.refs_2_, bf16[4,128,128]{2,1,0:T(8,128)(2,1)S(1)} %bitcast.60, bf16[4,25,128,128]{3,2,1,0:T(8,128)(2,1)S(1)} %bitcast.50, ...), custom_call_target="tpu_custom_call" | custom-call | tf_op jit(solution)/shard_map/forward_level_2/pallas_call | solution.py:297
  87.3 14.9 %all_to_all.56.refs_7_.refs_4_.refs_5_ = bf16[64,8,128]{2,1,0:T(8,128)(2,1)S(1)} all-to-all(bf16[64,8,128]{2,1,0:T(8,128)(2,1)S(1)} %forward_level_2.1), channel_id=1, replica_groups=mesh['chain'=64,'col'=4] {'chain'}, dimensions={0} | all-to-all | bytes 262144 | tf_op jit(solution)/shard_map/all_to_all | solution.py:261
  102.2 2.7 %forward_level_3.1 = bf16[64,8,128]{2,1,0:T(8,128)(2,1)S(1)} custom-call(s32[6]{0:T(128)S(1)} %copy-done.4, s32[96]{0:T(128)S(1)} %reshape.59.refs_1_, bf16[4,8,128]{2,1,0:T(8,128)(2,1)S(1)} %dynamic-slice_bitcast_fusion.right.refs_2_, bf16[4,128,128]{2,1,0:T(8,128)(2,1)S(1)} %bitcast.61, bf16[4,25,128,128]{3,2,1,0:T(8,128)(2,1)S(1)} %bitcast.51, ...), custom_call_target="tpu_custom_call" | custom-call | tf_op jit(solution)/shard_map/forward_level_3/pallas_call | solution.py:297
  105.0 14.9 %all_to_all.57.refs_8_.refs_4_.refs_6_ = bf16[64,8,128]{2,1,0:T(8,128)(2,1)S(1)} all-to-all(bf16[64,8,128]{2,1,0:T(8,128)(2,1)S(1)} %forward_level_3.1), channel_id=1, replica_groups=mesh['chain'=64,'col'=4] {'chain'}, dimensions={0} | all-to-all | bytes 262144 | tf_op jit(solution)/shard_map/all_to_all | solution.py:261
  119.9 2.9 %forward_level_4.1 = bf16[64,8,128]{2,1,0:T(8,128)(2,1)S(1)} custom-call(s32[6]{0:T(128)S(1)} %copy-done.4, s32[96]{0:T(128)S(1)} %reshape.59.refs_1_, bf16[4,8,128]{2,1,0:T(8,128)(2,1)S(1)} %dynamic-slice_bitcast_fusion.right.refs_2_, bf16[4,128,128]{2,1,0:T(8,128)(2,1)S(1)} %bitcast.62, bf16[4,25,128,128]{3,2,1,0:T(8,128)(2,1)S(1)} %bitcast.52, ...), custom_call_target="tpu_custom_call" | custom-call | tf_op jit(solution)/shard_map/forward_level_4/pallas_call | solution.py:297
  122.8 14.9 %all_to_all.58.refs_9_.refs_4_.refs_7_ = bf16[64,8,128]{2,1,0:T(8,128)(2,1)S(1)} all-to-all(bf16[64,8,128]{2,1,0:T(8,128)(2,1)S(1)} %forward_level_4.1), channel_id=1, replica_groups=mesh['chain'=64,'col'=4] {'chain'}, dimensions={0} | all-to-all | bytes 262144 | tf_op jit(solution)/shard_map/all_to_all | solution.py:261
  137.7 3.7 %turn_level.1 = (bf16[8,128]{1,0:T(8,128)(2,1)S(1)}, bf16[8,128]{1,0:T(8,128)(2,1)S(1)}, f32[256,8,128]{2,1,0:T(8,128)S(1)}, bf16[64,8,128]{2,1,0:T(8,128)(2,1)S(1)}) custom-call(s32[6]{0:T(128)S(1)} %copy-done.4, s32[96]{0:T(128)S(1)} %reshape.59.refs_1_, bf16[4,8,128]{2,1,0:T(8,128)(2,1)S(1)} %dynamic-slice_bitcast_fusion.right.refs_2_, ...), custom_call_target="tpu_custom_call" | custom-call | tf_op jit(solution)/shard_map/turn_level/pallas_call | solution.py:315
  141.4 14.9 %all_to_all.59.refs_5_ = bf16[64,8,128]{2,1,0:T(8,128)(2,1)S(1)} all-to-all(bf16[64,8,128]{2,1,0:T(8,128)(2,1)S(1)} %get-tuple-element.17), channel_id=1, replica_groups=mesh['chain'=64,'col'=4] {'chain'}, dimensions={0} | all-to-all | bytes 262144 | tf_op jit(solution)/shard_map/all_to_all | solution.py:261
  156.4 2.4 %backward_level_4.1 = (bf16[8,128]{1,0:T(8,128)(2,1)S(1)}, f32[192,8,128]{2,1,0:T(8,128)S(1)}, bf16[64,8,128]{2,1,0:T(8,128)(2,1)S(1)}) custom-call(s32[6]{0:T(128)S(1)} %copy-done.4, s32[96]{0:T(128)S(1)} %reshape.59.refs_1_, bf16[4,128,128]{2,1,0:T(8,128)(2,1)S(1)} %bitcast.64, bf16[4,25,128,128]{3,2,1,0:T(8,128)(2,1)S(1)} %bitcast.54, ...), custom_call_target="tpu_custom_call" | custom-call | tf_op jit(solution)/shard_map/backward_level_4/pallas_call | solution.py:344
  158.8 14.9 %all_to_all.60.refs_5_ = bf16[64,8,128]{2,1,0:T(8,128)(2,1)S(1)} all-to-all(bf16[64,8,128]{2,1,0:T(8,128)(2,1)S(1)} %get-tuple-element.19), channel_id=1, replica_groups=mesh['chain'=64,'col'=4] {'chain'}, dimensions={0} | all-to-all | bytes 262144 | tf_op jit(solution)/shard_map/all_to_all | solution.py:261
  173.7 2.4 backward_level_3.1
  176.1 14.9 %all_to_all.61.refs_5_ = bf16[64,8,128]{2,1,0:T(8,128)(2,1)S(1)} all-to-all(bf16[64,8,128]{2,1,0:T(8,128)(2,1)S(1)} %get-tuple-element.21), channel_id=1, replica_groups=mesh['chain'=64,'col'=4] {'chain'}, dimensions={0} | all-to-all | bytes 262144 | tf_op jit(solution)/shard_map/all_to_all | solution.py:261
  191.1 2.4 backward_level_2.1
  193.5 14.9 %all_to_all.62.refs_5_ = bf16[64,8,128]{2,1,0:T(8,128)(2,1)S(1)} all-to-all(bf16[64,8,128]{2,1,0:T(8,128)(2,1)S(1)} %get-tuple-element.23), channel_id=1, replica_groups=mesh['chain'=64,'col'=4] {'chain'}, dimensions={0} | all-to-all | bytes 262144 | tf_op jit(solution)/shard_map/all_to_all | solution.py:261
  208.4 2.4 backward_level_1.1
  210.7 14.9 %all_to_all.63.refs_2_ = bf16[64,8,128]{2,1,0:T(8,128)(2,1)S(1)} all-to-all(bf16[64,8,128]{2,1,0:T(8,128)(2,1)S(1)} %get-tuple-element.25), channel_id=1, replica_groups=mesh['chain'=64,'col'=4] {'chain'}, dimensions={0} | all-to-all | bytes 262144 | tf_op jit(solution)/shard_map/all_to_all | solution.py:261
  225.7 1.1 finish.1
  226.8 7.2 %all_to_all.64 = bf16[4,8,8,128]{3,2,1,0:T(8,128)(2,1)S(1)} all-to-all(bf16[4,8,8,128]{3,2,1,0:T(8,128)(2,1)S(1)} %finish.1), channel_id=1, replica_groups=mesh['chain'=64,'col'=4] {'col'}, dimensions={0} | all-to-all | bytes 131072 | tf_op jit(solution)/shard_map/all_to_all | solution.py:379
  234.0 0.6 copy_bitcast_fusion
  (17 shorter events, 0.3 us)
Async XLA Ops:
  7.2 3.1 %copy-start = (bf16[4,1,32,128]{3,2,1,0:T(8,128)(2,1)S(1)}, bf16[4,1,32,128]{3,2,1,0:T(8,128)(2,1)}, u32[]{:S(2)}) copy-start(bf16[4,1,32,128]{3,2,1,0:T(8,128)(2,1)} %param.5) | copy-start | bytes 98308
  7.2 3.1 %copy-start.4 = (s32[6]{0:T(128)S(1)}, s32[6]{0:T(128)}, u32[]{:S(2)}) copy-start(s32[6]{0:T(128)} %refs_0_.19) | copy-start | bytes 76
  7.2 3.1 %copy-start.3 = (bf16[4,1,128,128]{3,2,1,0:T(8,128)(2,1)S(1)}, bf16[4,1,128,128]{3,2,1,0:T(8,128)(2,1)}, u32[]{:S(2)}) copy-start(bf16[4,1,128,128]{3,2,1,0:T(8,128)(2,1)} %param.8) | copy-start | bytes 393220
  7.2 50.2 %all-gather.3.cloned.1.call-start = ((), (), s32[]{:S(2)}) async-start(), calls=%async_computation.11 | async-start | bytes 4096000 | tf_op jit(solution)/shard_map/all_gather | solution.py:267
  11.7 47.2 %all-to-all-start = ((bf16[64,8,128]{2,1,0:T(8,128)(2,1)}), bf16[64,8,128]{2,1,0:T(8,128)(2,1)S(1)}, u32[]{:S(2)}, u32[]{:S(2)}) async-start(bf16[64,8,128]{2,1,0:T(8,128)(2,1)} %forward_first.1), calls=%async_computation | async-start | bytes 262144 | tf_op jit(solution)/shard_map/all_to_all | solution.py:261
  58.9 1.9 copy-start.1
  137.7 18.7 %copy-start.2 = (bf16[100,128,128]{2,1,0:T(8,128)(2,1)S(1)}, bf16[100,128,128]{2,1,0:T(8,128)(2,1)}, u32[]{:S(2)}) copy-start(bf16[100,128,128]{2,1,0:T(8,128)(2,1)} %all-gather.3.cloned.1.call-done) | copy-start | bytes 9830404
Sparse Core Ops, SparseCore 0:
  10.4 46.9 all-gather.2

commit v2 on v0

v2 whole, which is shorter than its diff:
```python
import functools
import jax
import jax.numpy as jnp
from jax import lax
from jax.experimental import pallas as pl
from jax.experimental.pallas import tpu as pltpu
from jax.sharding import PartitionSpec as P

BF16 = jnp.bfloat16
F32 = jnp.float32
NT = (((1,), (1,)), ((), ()))
NN = (((1,), (0,)), ((), ()))
CODE_ROWS = 16


class Plan:
    def __init__(self, lanes, cols, rows, entries, share, width, levels):
        self.lanes, self.cols, self.rows, self.entries = lanes, cols, rows, entries
        self.share, self.width, self.levels = share, width, levels
        self.near = (rows + 1) // 2

    def slots(self, level):
        return max(0, self.rows - (self.levels - level)), min(level, self.rows - 1)


def locate(plan, level, sizes):
    lane = lax.axis_index("chain")
    start = jnp.int32(0)
    for k in range(level):
        start = start + sizes[k]
    slot = (start - lane + (plan.lanes - 1)) // plan.lanes
    live = (slot < plan.rows) & (
        slot * plan.lanes + lane < start + sizes[level]
    )
    low, high = plan.slots(level)
    return jnp.clip(slot, low, high), live


def block_at(plan, ref, slot, entry):
    at = pl.multiple_of((slot * plan.entries + entry) * plan.width, plan.width)
    return ref[pl.ds(at, plan.width), :]


def by_source(plan, level, slot, near, far, run):
    low, high = plan.slots(level)
    col = lax.axis_index("col")

    def near_entries():
        for s in range(plan.cols):
            for e in range(plan.entries):
                yield (
                    functools.partial(block_at, plan, near[s], slot, e),
                    (s * plan.rows + slot, e),
                )

    def far_entries():
        for q in range(plan.cols):
            s = lax.rem(col - q + plan.cols, plan.cols)
            for e in range(plan.entries):
                yield (
                    functools.partial(block_at, plan, far.at[q], slot - plan.near, e),
                    (s * plan.rows + slot, e),
                )

    if high < plan.near:
        run(list(near_entries()))
    elif low >= plan.near:
        run(list(far_entries()))
    else:

        @pl.when(slot < plan.near)
        def _():
            run(list(near_entries()))

        @pl.when(slot >= plan.near)
        def _():
            run(list(far_entries()))


def gather_store(plan, level, earlier, store):
    for k in range(level):
        store[pl.ds(k * plan.lanes, plan.lanes)] = earlier[k][...]
    store[level * plan.lanes] = jnp.zeros(store.shape[1:], BF16)


def half_segment(plan, level, slot, table, right, inverse, near, far, store, sums):
    def run(entries):
        chosen = jnp.concatenate(
            [store[jnp.minimum(table[at], level * plan.lanes)] for _, at in entries],
            axis=1,
        )
        weights = jnp.concatenate([load() for load, _ in entries], axis=1)
        sums[...] = lax.dot_general(chosen, weights, NT, preferred_element_type=F32)

    by_source(plan, level, slot, near, far, run)
    rest = right[slot, lax.axis_index("col")].astype(F32) - sums[...]
    return lax.dot_general(
        rest.astype(BF16), inverse[slot], NT, preferred_element_type=F32
    ).astype(BF16)


def add_terms(plan, level, slot, live, table, segment, near, far, acc):
    segment = jnp.where(live, segment.astype(F32), 0.0).astype(BF16)

    def run(entries):
        weights = jnp.concatenate([load() for load, _ in entries], axis=1)
        terms = lax.dot_general(segment, weights, NN, preferred_element_type=F32)
        for j, (_, place) in enumerate(entries):
            at = jnp.minimum(table[place], level * plan.lanes)
            acc[at] = acc[at] + terms[:, j * plan.width : (j + 1) * plan.width]

    by_source(plan, level, slot, near, far, run)


def forward_first(plan, *refs):
    pattern, factor, right, inverse, out, near, far, wide, code, sems = refs
    split = plan.near * plan.entries * plan.width
    left = plan.rows * plan.entries * plan.width - split
    copies = [
        pltpu.make_async_copy(
            factor.at[pl.ds(0, split)], near.at[pl.ds(0, split)], sems.at[0]
        ),
        pltpu.make_async_copy(factor.at[pl.ds(split, left)], far, sems.at[1]),
    ]
    for c in copies:
        c.start()
    wide[...] = jnp.zeros(wide.shape, F32)
    wide[pl.ds(0, plan.rows), pl.ds(0, plan.entries)] = pattern[:, 0, :].astype(F32)
    code[...] = wide[...].astype(BF16)
    last = pltpu.make_async_copy(code, near.at[pl.ds(split, CODE_ROWS)], sems.at[2])
    last.start()
    segment = lax.dot_general(
        right[0, lax.axis_index("col")], inverse[0], NT, preferred_element_type=F32
    ).astype(BF16)
    out[...] = jnp.broadcast_to(segment[None], out.shape)
    for c in copies:
        c.wait()
    last.wait()


def fill_table(plan, sizes, near, table):
    split = plan.near * plan.entries * plan.width
    lane = lax.axis_index("chain")
    columns = jnp.concatenate(
        [
            near[s][pl.ds(split, CODE_ROWS), :].astype(F32)[: plan.rows]
            for s in range(plan.cols)
        ],
        axis=0,
    ).astype(jnp.int32)
    places = lax.broadcasted_iota(jnp.int32, columns.shape, 0)
    own = lax.rem(places, plan.rows) * plan.lanes + lane
    level = jnp.zeros_like(columns)
    own_level = jnp.zeros_like(columns)
    end = jnp.int32(0)
    for k in range(plan.levels):
        end = end + sizes[k]
        level = level + (columns >= end).astype(jnp.int32)
        own_level = own_level + (own >= end).astype(jnp.int32)
    table[...] = jnp.where(
        level < own_level,
        level * plan.lanes + lax.rem(columns, plan.lanes),
        plan.levels * plan.lanes,
    )


def forward_second(plan, *refs):
    sizes, right, inverse, front = refs[:4]
    near = refs[4 : 4 + plan.cols]
    out, table, local, store, sums, sem = refs[4 + plan.cols :]
    fill_table(plan, sizes, near, table)
    copy = pltpu.make_async_copy(table, local, sem)
    copy.start()
    slot, _ = locate(plan, 1, sizes)
    gather_store(plan, 1, [front], store)
    copy.wait()
    segment = half_segment(
        plan, 1, slot, local, right, inverse, near, None, store, sums
    )
    out[...] = jnp.broadcast_to(segment[None], out.shape)


def forward_level(plan, level, *refs):
    sizes, table, right, inverse, far = refs[:5]
    near = refs[5 : 5 + plan.cols]
    earlier = refs[5 + plan.cols : 5 + plan.cols + level]
    out, store, sums = refs[5 + plan.cols + level :]
    slot, _ = locate(plan, level, sizes)
    gather_store(plan, level, earlier, store)
    segment = half_segment(
        plan, level, slot, table, right, inverse, near, far, store, sums
    )
    out[...] = jnp.broadcast_to(segment[None], out.shape)


def turn_level(plan, level, *refs):
    sizes, table, right, inverse, far = refs[:5]
    near = refs[5 : 5 + plan.cols]
    earlier = refs[5 + plan.cols : 5 + plan.cols + level]
    half, solved, acc, out, store, sums = refs[5 + plan.cols + level :]
    slot, live = locate(plan, level, sizes)
    gather_store(plan, level, earlier, store)
    acc[...] = jnp.zeros(acc.shape, F32)
    segment = half_segment(
        plan, level, slot, table, right, inverse, near, far, store, sums
    )
    half[...] = segment
    segment = lax.dot_general(
        segment, inverse[slot], NN, preferred_element_type=F32
    ).astype(BF16)
    solved[...] = segment
    add_terms(plan, level, slot, live, table, segment, near, far, acc)
    out[...] = acc[pl.ds((level - 1) * plan.lanes, plan.lanes)].astype(BF16)


def solve_back(slot, half, inverse, arrived):
    summed = jnp.sum(arrived[...].astype(F32), axis=0)
    rest = (half.astype(F32) - summed).astype(BF16)
    return lax.dot_general(
        rest, inverse[slot], NN, preferred_element_type=F32
    ).astype(BF16)


def backward_level(plan, level, *refs):
    sizes, table, inverse, front, arrived, _, far = refs[:7]
    near = refs[7 : 7 + plan.cols]
    solved, acc, out = refs[7 + plan.cols :]
    slot, live = locate(plan, level, sizes)
    segment = solve_back(slot, front[lax.axis_index("chain")], inverse, arrived)
    solved[...] = segment
    add_terms(plan, level, slot, live, table, segment, near, far, acc)
    out[...] = acc[pl.ds((level - 1) * plan.lanes, plan.lanes)].astype(BF16)


def finish(plan, *refs):
    levels = plan.levels
    sizes, inverse, arrived = refs[:3]
    fronts = refs[3 : 2 + levels]
    half_last = refs[2 + levels]
    done = refs[3 + levels : 2 + 2 * levels]
    out, hbuf, sbuf = refs[2 + 2 * levels :]
    lane = lax.axis_index("chain")
    for k in range(levels - 1):
        hbuf[k] = fronts[k][lane]
        sbuf[k + 1] = done[k][...]
    hbuf[levels - 1] = half_last[...]
    sbuf[0] = solve_back(0, hbuf[0], inverse, arrived)
    for r in range(plan.rows):
        row = r * plan.lanes + lane
        end = jnp.int32(0)
        level = jnp.int32(0)
        for k in range(levels):
            end = end + sizes[k]
            level = level + (row >= end).astype(jnp.int32)
        h, s = hbuf[level], sbuf[level]
        for q in range(plan.cols):
            out[q, r] = h
            out[q, plan.rows + r] = s


def per_device(rhs, pattern, factor, inverse, level_size):
    lanes = lax.axis_size("chain")
    cols = lax.axis_size("col")
    rows, _, probes, width = rhs.shape
    entries = pattern.shape[2]
    levels = level_size.shape[0]
    share = probes // cols
    plan = Plan(lanes, cols, rows, entries, share, width, levels)
    split = plan.near * entries * width
    left = rows * entries * width - split

    smem = pl.BlockSpec(memory_space=pltpu.SMEM)
    hbm = pl.BlockSpec(memory_space=pl.ANY)
    vmem = pl.BlockSpec(memory_space=pltpu.VMEM)
    segment_shape = pltpu.VMEM((share, width), BF16)
    front_shape = pltpu.VMEM((lanes, share, width), BF16)
    params = pltpu.CompilerParams(vmem_limit_bytes=12 * 1024 * 1024)
    sums = pltpu.VMEM((share, width), F32)

    def held(x):
        return pltpu.with_memory_space_constraint(x, pltpu.VMEM)

    def store(level):
        return pltpu.VMEM((level * lanes + 1, share, width), BF16)

    def exchange(x):
        return held(lax.all_to_all(x, "chain", 0, 0, tiled=True))

    inverse = held(inverse.reshape(rows, width, width))
    right = held(rhs.reshape(rows, cols, share, width))

    first, own, rest = pl.pallas_call(
        functools.partial(forward_first, plan),
        out_shape=(
            front_shape,
            pltpu.VMEM((split + CODE_ROWS, width), BF16),
            jax.ShapeDtypeStruct((left, width), BF16),
        ),
        in_specs=[vmem, hbm, vmem, vmem],
        out_specs=(vmem, vmem, hbm),
        scratch_shapes=[
            pltpu.VMEM((CODE_ROWS, width), F32),
            pltpu.VMEM((CODE_ROWS, width), BF16),
            pltpu.SemaphoreType.DMA((3,)),
        ],
        compiler_params=params,
        name="forward_first",
    )(pattern, factor.reshape(rows * entries * width, width), right, inverse)
    near = [held(own)] + [
        held(lax.ppermute(own, "col", [(i, (i + s) % cols) for i in range(cols)]))
        for s in range(1, cols)
    ]
    far = held(lax.all_gather(rest, "col"))
    fronts = [exchange(first)]

    mine, table = pl.pallas_call(
        functools.partial(forward_second, plan),
        out_shape=(front_shape, pltpu.VMEM((cols * rows, width), jnp.int32)),
        in_specs=[smem] + [vmem] * (3 + cols),
        out_specs=(vmem, vmem),
        scratch_shapes=[
            pltpu.SMEM((cols * rows, width), jnp.int32),
            store(1),
            sums,
            pltpu.SemaphoreType.DMA,
        ],
        compiler_params=params,
        name="forward_second",
    )(level_size, right, inverse, fronts[0], *near)
    fronts.append(exchange(mine))
    for k in range(2, levels - 1):
        mine = pl.pallas_call(
            functools.partial(forward_level, plan, k),
            out_shape=front_shape,
            in_specs=[smem, smem] + [vmem] * (3 + cols + k),
            out_specs=vmem,
            scratch_shapes=[store(k), sums],
            compiler_params=params,
            name=f"forward_level_{k}",
        )(level_size, table, right, inverse, far, *near, *fronts)
        fronts.append(exchange(mine))

    last = levels - 1
    acc_shape = pltpu.VMEM((last * lanes + 1, share, width), F32)
    half_last, solved, acc, terms = pl.pallas_call(
        functools.partial(turn_level, plan, last),
        out_shape=(segment_shape, segment_shape, acc_shape, front_shape),
        in_specs=[smem, smem] + [vmem] * (3 + cols + last),
        out_specs=(vmem,) * 4,
        scratch_shapes=[store(last), sums],
        compiler_params=params,
        name="turn_level",
    )(level_size, table, right, inverse, far, *near, *fronts)
    done = [held(solved)]
    for k in range(last - 1, 0, -1):
        solved, acc, terms = pl.pallas_call(
            functools.partial(backward_level, plan, k),
            out_shape=(segment_shape, acc_shape, front_shape),
            in_specs=[smem, smem] + [vmem] * (5 + cols),
            out_specs=(vmem,) * 3,
            input_output_aliases={5: 1},
            compiler_params=params,
            name=f"backward_level_{k}",
        )(
            level_size,
            table,
            inverse,
            fronts[k],
            exchange(terms),
            held(acc),
            far,
            *near,
        )
        done.insert(0, held(solved))
    shares = pl.pallas_call(
        functools.partial(finish, plan),
        out_shape=pltpu.VMEM((cols, 2 * rows, share, width), BF16),
        in_specs=[smem] + [vmem] * (1 + 2 * levels),
        out_specs=vmem,
        scratch_shapes=[
            pltpu.VMEM((levels, share, width), BF16),
            pltpu.VMEM((levels, share, width), BF16),
        ],
        compiler_params=params,
        name="finish",
    )(level_size, inverse, exchange(terms), *fronts, held(half_last), *done)
    whole = lax.all_to_all(shares, "col", 0, 0, tiled=True)
    whole = whole.transpose(1, 0, 2, 3).reshape(2, rows, 1, probes, width)
    return whole[0], whole[1]


def solution(mesh):
    return jax.shard_map(
        per_device,
        mesh=mesh,
        in_specs=(
            P(None, "chain", None, None),
            P(None, "chain", "col"),
            P(None, "chain", "col", None, None),
            P(None, "chain", None, None),
            P(),
        ),
        out_specs=(P(None, "chain", None, None), P(None, "chain", None, None)),
        check_vma=False,
    )
```

time: 1440 us -> 214 us (0.15)
  waiting for transfers between devices: 821 us -> 0.22 us
  blocking collectives: 470 us -> 175 us
  local copies, waits for them, and re-layouts: 40.2 us -> 5.53 us
  loops' own time: 33.6 us -> 0 us
  other arithmetic: 27.2 us -> 0 us
  matrix products: 20.5 us -> 0 us
    while x12 -> x0, waiting for transfers between devices: 821 us -> none
    all_gather x6 -> x0, blocking collectives: 318 us -> none  [forward_level(): front = lax.all_gather(segment[None], 'chain', axis=0, tiled=True)]
    all_to_all x0 -> x11, blocking collectives: none -> 175 us  [the longest x10 168 us: exchange(): return held(lax.all_to_all(x, 'chain', 0, 0, tiled=True))]
    psum x12 -> x0, blocking collectives: 152 us -> none  [the longest x6 81.5 us: backward_level(): summed = lax.psum(mine, 'col')]
    another operation x2 -> x0, loops' own time: 33.6 us -> none  [the longest x1 23.1 us: per_device(): lax.fori_loop(0, level_count, forward_level, (store, half_local))]
    dot_general x30 -> x0, matrix products: 20.5 us -> none  [the longest x6 8.82 us: forward_level(): jnp.dot(rest, inverse_rows[own_slot].T, preferred_element_type=jnp.float32)]
    gather x12 -> x0, local copies, waits for them, and re-layouts: 17.8 us -> none  [the longest x6 13.8 us: forward_level(): store[columns[own_slot]]]
  transfers between devices with their start and end apart: 6 -> 4, of which waited for: 6 -> 1; matrix products, arithmetic and copies ran while one was open for 1% -> 0% of each run, Pallas kernels for 0% -> 1%
where the time goes in v2:
time: 214 us; the launch traced here: 213 us
  blocking collectives  175 us (82%)
  between operations  14.1 us (7%)
  Pallas kernels  13.1 us (6%)
  local copies, waits for them, and re-layouts  5.53 us (3%)
  starting transfers between devices  4.55 us (2%)
    all_to_all x10, blocking collectives, exchange(): return held(lax.all_to_all(x, 'chain', 0, 0, tiled=True))  168 us
    all_to_all x1, blocking collectives, per_device(): whole = lax.all_to_all(shares, 'col', 0, 0, tiled=True)  6.99 us
    unnamed x19, local copies, waits for them, and re-layouts  5.53 us
    ppermute x3, starting transfers between devices, per_device(): lax.ppermute(own, 'col', [(i, (i + s) % cols) for i in range(cols)])  4.51 us
    pallas_call x4, Pallas kernels, per_device(): pl.pallas_call(functools.partial(backward_level, plan, k), out_shape=(seg...  4.47 us
  transfers between devices with their start and end apart: 4, of which 1 were waited for; matrix products, arithmetic and copies ran while one was open for 0% of the time, Pallas kernels for 1%

profile of v2, /device:TPU:1, one launch (start us, length us, event | category | flops | bytes accessed | tf_op | source)
XLA Modules:
  0.0 213.0 jit_solution(10397016003018045528)
XLA Ops:
  7.2 0.9 copy-done.2
  8.1 0.8 copy-done.4
  8.9 1.1 copy-done.6
  10.0 0.7 copy-done.8
  10.7 1.0 forward_first.1
  11.7 3.4 %collective-permute-start.2 = (bf16[1552,128]{1,0:T(8,128)(2,1)S(1)}, bf16[1552,128]{1,0:T(8,128)(2,1)S(1)}, u32[]{:S(2)}, u32[]{:S(2)}) collective-permute-start(bf16[1552,128]{1,0:T(8,128)(2,1)S(1)} %get-tuple-element.23.refs_4_.refs_5_.refs_7_), channel_id=1, source_target_pairs={{0,3},{1,0},{2,1},{3,2},{4,7},{5,4},{6,5},{7,6},{8,11},{9,8},{10,9... | collective-permute-start | bytes 1191944 | tf_op jit(solution)/shard_map/ppermute | solution.py:310
  15.1 0.5 collective-permute-start.1
  15.6 0.6 collective-permute-start
  16.2 24.1 %all_to_all.55.refs_3_.refs_9_ = bf16[64,8,128]{2,1,0:T(8,128)(2,1)S(1)} all-to-all(bf16[64,8,128]{2,1,0:T(8,128)(2,1)S(1)} %get-tuple-element.22), channel_id=1, replica_groups=mesh['chain'=64,'col'=4] {'chain'}, dimensions={0} | all-to-all | bytes 262144 | tf_op jit(solution)/shard_map/all_to_all | solution.py:287
  40.3 0.2 collective-permute-done.refs_5_.refs_6_.refs_8_
  40.5 1.7 forward_second.1
  42.2 24.8 %all_to_all.56.refs_10_.refs_3_.refs_4_ = bf16[64,8,128]{2,1,0:T(8,128)(2,1)S(1)} all-to-all(bf16[64,8,128]{2,1,0:T(8,128)(2,1)S(1)} %get-tuple-element.25), channel_id=1, replica_groups=mesh['chain'=64,'col'=4] {'chain'}, dimensions={0} | all-to-all | bytes 262144 | tf_op jit(solution)/shard_map/all_to_all | solution.py:287
  67.0 1.4 copy-done
  68.4 1.2 forward_level_2.1
  69.6 14.9 %all_to_all.57.refs_11_.refs_3_.refs_5_ = bf16[64,8,128]{2,1,0:T(8,128)(2,1)S(1)} all-to-all(bf16[64,8,128]{2,1,0:T(8,128)(2,1)S(1)} %forward_level_2.1), channel_id=1, replica_groups=mesh['chain'=64,'col'=4] {'chain'}, dimensions={0} | all-to-all | bytes 262144 | tf_op jit(solution)/shard_map/all_to_all | solution.py:287
  84.5 1.2 forward_level_3.1
  85.7 14.9 %all_to_all.58.refs_12_.refs_3_.refs_6_ = bf16[64,8,128]{2,1,0:T(8,128)(2,1)S(1)} all-to-all(bf16[64,8,128]{2,1,0:T(8,128)(2,1)S(1)} %forward_level_3.1), channel_id=1, replica_groups=mesh['chain'=64,'col'=4] {'chain'}, dimensions={0} | all-to-all | bytes 262144 | tf_op jit(solution)/shard_map/all_to_all | solution.py:287
  100.6 1.2 forward_level_4.1
  101.8 14.9 %all_to_all.59.refs_13_.refs_3_.refs_7_ = bf16[64,8,128]{2,1,0:T(8,128)(2,1)S(1)} all-to-all(bf16[64,8,128]{2,1,0:T(8,128)(2,1)S(1)} %forward_level_4.1), channel_id=1, replica_groups=mesh['chain'=64,'col'=4] {'chain'}, dimensions={0} | all-to-all | bytes 262144 | tf_op jit(solution)/shard_map/all_to_all | solution.py:287
  116.8 1.7 turn_level.1
  118.5 14.9 %all_to_all.60.refs_4_ = bf16[64,8,128]{2,1,0:T(8,128)(2,1)S(1)} all-to-all(bf16[64,8,128]{2,1,0:T(8,128)(2,1)S(1)} %get-tuple-element.27), channel_id=1, replica_groups=mesh['chain'=64,'col'=4] {'chain'}, dimensions={0} | all-to-all | bytes 262144 | tf_op jit(solution)/shard_map/all_to_all | solution.py:287
  133.4 1.1 backward_level_4.1
  134.5 14.9 %all_to_all.61.refs_4_ = bf16[64,8,128]{2,1,0:T(8,128)(2,1)S(1)} all-to-all(bf16[64,8,128]{2,1,0:T(8,128)(2,1)S(1)} %get-tuple-element.29), channel_id=1, replica_groups=mesh['chain'=64,'col'=4] {'chain'}, dimensions={0} | all-to-all | bytes 262144 | tf_op jit(solution)/shard_map/all_to_all | solution.py:287
  149.4 1.1 backward_level_3.1
  150.5 15.1 %all_to_all.62.refs_4_ = bf16[64,8,128]{2,1,0:T(8,128)(2,1)S(1)} all-to-all(bf16[64,8,128]{2,1,0:T(8,128)(2,1)S(1)} %get-tuple-element.31), channel_id=1, replica_groups=mesh['chain'=64,'col'=4] {'chain'}, dimensions={0} | all-to-all | bytes 262144 | tf_op jit(solution)/shard_map/all_to_all | solution.py:287
  165.7 1.1 backward_level_2.1
  166.8 15.0 %all_to_all.63.refs_4_ = bf16[64,8,128]{2,1,0:T(8,128)(2,1)S(1)} all-to-all(bf16[64,8,128]{2,1,0:T(8,128)(2,1)S(1)} %get-tuple-element.33), channel_id=1, replica_groups=mesh['chain'=64,'col'=4] {'chain'}, dimensions={0} | all-to-all | bytes 262144 | tf_op jit(solution)/shard_map/all_to_all | solution.py:287
  181.8 1.1 backward_level_1.1
  182.9 14.9 %all_to_all.64.refs_2_ = bf16[64,8,128]{2,1,0:T(8,128)(2,1)S(1)} all-to-all(bf16[64,8,128]{2,1,0:T(8,128)(2,1)S(1)} %get-tuple-element.35), channel_id=1, replica_groups=mesh['chain'=64,'col'=4] {'chain'}, dimensions={0} | all-to-all | bytes 262144 | tf_op jit(solution)/shard_map/all_to_all | solution.py:287
  197.8 0.7 finish.1
  198.5 7.0 %all_to_all.65 = bf16[4,8,8,128]{3,2,1,0:T(8,128)(2,1)S(1)} all-to-all(bf16[4,8,8,128]{3,2,1,0:T(8,128)(2,1)S(1)} %finish.1), channel_id=1, replica_groups=mesh['chain'=64,'col'=4] {'col'}, dimensions={0} | all-to-all | bytes 131072 | tf_op jit(solution)/shard_map/all_to_all | solution.py:387
  205.5 0.6 copy_bitcast_fusion
  (19 shorter events, 0.1 us)
Async XLA Ops:
  7.2 33.3 %copy-start.7 = (s32[6]{0:T(128)S(1)}, s32[6]{0:T(128)}, u32[]{:S(2)}) copy-start(s32[6]{0:T(128)} %refs_0_.21) | copy-start | bytes 76
  7.2 59.9 %all-gather.3.cloned.1.call-start = ((), (), s32[]{:S(2)}) async-start(), calls=%async_computation.11 | async-start | bytes 1966080 | tf_op jit(solution)/shard_map/all_gather | solution.py:313
  7.2 0.9 copy-start.2
  8.1 0.8 copy-start.4
  8.9 1.1 copy-start.6
  10.0 0.7 copy-start.8
  10.7 29.8 %copy-start.3 = (bf16[4,1,128,128]{3,2,1,0:T(8,128)(2,1)S(1)}, bf16[4,1,128,128]{3,2,1,0:T(8,128)(2,1)}, u32[]{:S(2)}) copy-start(bf16[4,1,128,128]{3,2,1,0:T(8,128)(2,1)} %param.8) | copy-start | bytes 393220
  10.7 29.8 %copy-start.5 = (bf16[4,1,32,128]{3,2,1,0:T(8,128)(2,1)S(1)}, bf16[4,1,32,128]{3,2,1,0:T(8,128)(2,1)}, u32[]{:S(2)}) copy-start(bf16[4,1,32,128]{3,2,1,0:T(8,128)(2,1)} %param.5) | copy-start | bytes 98308
  11.7 28.6 %collective-permute-start.2 = (bf16[1552,128]{1,0:T(8,128)(2,1)S(1)}, bf16[1552,128]{1,0:T(8,128)(2,1)S(1)}, u32[]{:S(2)}, u32[]{:S(2)}) collective-permute-start(bf16[1552,128]{1,0:T(8,128)(2,1)S(1)} %get-tuple-element.23.refs_4_.refs_5_.refs_7_), channel_id=1, source_target_pairs={{0,3},{1,0},{2,1},{3,2},{4,7},{5,4},{6,5},{7,6},{8,11},{9,8},{10,9... | collective-permute-start | bytes 1191944 | tf_op jit(solution)/shard_map/ppermute | solution.py:310
  15.1 25.2 %collective-permute-start.1 = (bf16[1552,128]{1,0:T(8,128)(2,1)S(1)}, bf16[1552,128]{1,0:T(8,128)(2,1)S(1)}, u32[]{:S(2)}, u32[]{:S(2)}) collective-permute-start(bf16[1552,128]{1,0:T(8,128)(2,1)S(1)} %get-tuple-element.23.refs_4_.refs_5_.refs_7_), channel_id=1, source_target_pairs={{0,2},{1,3},{2,0},{3,1},{4,6},{5,7},{6,4},{7,5},{8,10},{9,11},{10,... | collective-permute-start | bytes 1191944 | tf_op jit(solution)/shard_map/ppermute | solution.py:310
  15.6 24.9 %collective-permute-start = (bf16[1552,128]{1,0:T(8,128)(2,1)S(1)}, bf16[1552,128]{1,0:T(8,128)(2,1)S(1)}, u32[]{:S(2)}, u32[]{:S(2)}) collective-permute-start(bf16[1552,128]{1,0:T(8,128)(2,1)S(1)} %get-tuple-element.23.refs_4_.refs_5_.refs_7_), channel_id=1, source_target_pairs={{0,1},{1,2},{2,3},{3,0},{4,5},{5,6},{6,7},{7,4},{8,9},{9,10},{10,1... | collective-permute-start | bytes 1191944 | tf_op jit(solution)/shard_map/ppermute | solution.py:310
  67.0 1.4 copy-start
  116.8 16.6 %copy-start.1 = (bf16[6144,128]{1,0:T(8,128)(2,1)S(1)}, bf16[6144,128]{1,0:T(8,128)(2,1)}, u32[]{:S(2)}) copy-start(bf16[6144,128]{1,0:T(8,128)(2,1)} %all-gather.3.cloned.1.call-done) | copy-start | bytes 4718596
Sparse Core Ops, SparseCore 0:
  11.8 37.4 all-gather.2

commit v3 on v2

v3 whole, which is shorter than its diff:
```python
import functools
import jax
import jax.numpy as jnp
from jax import lax
from jax.experimental import pallas as pl
from jax.experimental.pallas import tpu as pltpu
from jax.sharding import PartitionSpec as P

BF16 = jnp.bfloat16
F32 = jnp.float32
NT = (((1,), (1,)), ((), ()))
NN = (((1,), (0,)), ((), ()))
CODE_ROWS = 16
TABLE_ROWS = 8


class Plan:
    def __init__(self, lanes, cols, rows, entries, share, width, levels):
        self.lanes, self.cols, self.rows, self.entries = lanes, cols, rows, entries
        self.share, self.width, self.levels = share, width, levels
        self.deep = entries * width
        self.near = range(1, min(3, levels))
        self.far = range(min(3, levels), levels)

    def slots(self, level):
        return max(0, self.rows - (self.levels - level)), min(level, self.rows - 1)


def locate(plan, level, sizes):
    lane = lax.axis_index("chain")
    start = jnp.int32(0)
    for k in range(level):
        start = start + sizes[k]
    slot = (start - lane + (plan.lanes - 1)) // plan.lanes
    live = (slot < plan.rows) & (slot * plan.lanes + lane < start + sizes[level])
    low, high = plan.slots(level)
    return jnp.clip(slot, low, high), live


def factor_row(plan, factor, level, sizes):
    slot, _ = locate(plan, level, sizes)
    return factor.at[pl.ds(pl.multiple_of(slot * plan.deep, plan.deep), plan.deep)]


def weights_of(plan, level, sources):
    base = (level - (plan.near if level in plan.near else plan.far)[0]) * plan.deep
    return jnp.concatenate(
        [
            source[base + e * plan.width : base + (e + 1) * plan.width, :]
            for source in sources
            for e in range(plan.entries)
        ],
        axis=1,
    )


def places_of(plan, level, table):
    return [
        table[s * TABLE_ROWS + level, e]
        for s in range(plan.cols)
        for e in range(plan.entries)
    ]


def gather_store(plan, level, earlier, store):
    for k in range(level):
        store[pl.ds(k * plan.lanes, plan.lanes)] = earlier[k][...]
    store[level * plan.lanes] = jnp.zeros(store.shape[1:], BF16)


def half_segment(plan, level, table, right, inverse, sources, store):
    chosen = jnp.concatenate([store[at] for at in places_of(plan, level, table)], axis=1)
    weights = weights_of(plan, level, sources)
    summed = lax.dot_general(chosen, weights, NT, preferred_element_type=F32)
    rest = (right[level].astype(F32) - summed).astype(BF16)
    return lax.dot_general(
        rest, inverse[level], NT, preferred_element_type=F32
    ).astype(BF16)


def add_terms(plan, level, live, table, segment, sources, acc):
    segment = jnp.where(live, segment.astype(F32), 0.0).astype(BF16)
    weights = weights_of(plan, level, sources)
    terms = lax.dot_general(segment, weights, NN, preferred_element_type=F32)
    for j, at in enumerate(places_of(plan, level, table)):
        acc[at] = acc[at] + terms[:, j * plan.width : (j + 1) * plan.width]


def forward_first(plan, *refs):
    sizes, pattern, factor, right, inverse = refs[:5]
    out, near, rights, inverses, pats, wide, code, sems = refs[5:]
    col = lax.axis_index("col")
    slots = [locate(plan, k, sizes)[0] for k in range(plan.levels)]
    pick = pltpu.make_async_copy(pattern, pats, sems.at[0])
    pick.start()
    small = []
    for k in range(plan.levels):
        at = 1 + 2 * k
        small.append(
            pltpu.make_async_copy(inverse.at[slots[k]], inverses.at[k], sems.at[at])
        )
        small.append(
            pltpu.make_async_copy(
                right.at[slots[k], col], rights.at[k], sems.at[at + 1]
            )
        )
    for c in small:
        c.start()
    large = [
        pltpu.make_async_copy(
            factor_row(plan, factor, k, sizes),
            near.at[pl.ds(i * plan.deep, plan.deep)],
            sems.at[1 + 2 * plan.levels + i],
        )
        for i, k in enumerate(plan.near)
    ]
    for c in large:
        c.start()
    wide[...] = jnp.zeros(wide.shape, F32)
    pick.wait()
    for k in range(1, plan.levels):
        wide[pl.ds(k, 1), pl.ds(0, plan.entries)] = pats[slots[k]].astype(F32)
    code[...] = wide[...].astype(BF16)
    last = pltpu.make_async_copy(
        code,
        near.at[pl.ds(len(plan.near) * plan.deep, CODE_ROWS)],
        sems.at[1 + 2 * plan.levels + len(plan.near)],
    )
    last.start()
    small[0].wait()
    small[1].wait()
    segment = lax.dot_general(
        rights[0], inverses[0], NT, preferred_element_type=F32
    ).astype(BF16)
    out[...] = jnp.broadcast_to(segment[None], out.shape)
    for c in small[2:] + large:
        c.wait()
    last.wait()


def fill_table(plan, sizes, near, table):
    split = len(plan.near) * plan.deep
    columns = jnp.concatenate(
        [
            near[s][split : split + CODE_ROWS, :].astype(F32)[:TABLE_ROWS]
            for s in range(plan.cols)
        ],
        axis=0,
    ).astype(jnp.int32)
    own_level = lax.rem(lax.broadcasted_iota(jnp.int32, columns.shape, 0), TABLE_ROWS)
    level = jnp.zeros_like(columns)
    end = jnp.int32(0)
    for k in range(plan.levels):
        end = end + sizes[k]
        level = level + (columns >= end).astype(jnp.int32)
    table[...] = jnp.where(
        level < own_level,
        level * plan.lanes + lax.rem(columns, plan.lanes),
        own_level * plan.lanes,
    )


def forward_second(plan, *refs):
    sizes, factor, right, inverse, front = refs[:5]
    near = refs[5 : 5 + plan.cols]
    out, table, far, local, store, sems = refs[5 + plan.cols :]
    copies = [
        pltpu.make_async_copy(
            factor_row(plan, factor, k, sizes),
            far.at[pl.ds(i * plan.deep, plan.deep)],
            sems.at[1 + i],
        )
        for i, k in enumerate(plan.far)
    ]
    for c in copies:
        c.start()
    fill_table(plan, sizes, near, table)
    copy = pltpu.make_async_copy(table, local, sems.at[0])
    copy.start()
    gather_store(plan, 1, [front], store)
    copy.wait()
    segment = half_segment(plan, 1, local, right, inverse, near, store)
    out[...] = jnp.broadcast_to(segment[None], out.shape)
    for c in copies:
        c.wait()


def forward_level(plan, level, *refs):
    table, right, inverse = refs[:3]
    sources = refs[3 : 3 + plan.cols]
    earlier = refs[3 + plan.cols : 3 + plan.cols + level]
    out, store = refs[3 + plan.cols + level :]
    gather_store(plan, level, earlier, store)
    segment = half_segment(plan, level, table, right, inverse, sources, store)
    out[...] = jnp.broadcast_to(segment[None], out.shape)


def turn_level(plan, level, *refs):
    sizes, table, right, inverse = refs[:4]
    sources = refs[4 : 4 + plan.cols]
    earlier = refs[4 + plan.cols : 4 + plan.cols + level]
    half, solved, acc, out, store = refs[4 + plan.cols + level :]
    _, live = locate(plan, level, sizes)
    gather_store(plan, level, earlier, store)
    acc[...] = jnp.zeros(acc.shape, F32)
    segment = half_segment(plan, level, table, right, inverse, sources, store)
    half[...] = segment
    segment = lax.dot_general(
        segment, inverse[level], NN, preferred_element_type=F32
    ).astype(BF16)
    solved[...] = segment
    add_terms(plan, level, live, table, segment, sources, acc)
    out[...] = acc[pl.ds((level - 1) * plan.lanes, plan.lanes)].astype(BF16)


def solve_back(half, inverse, arrived):
    summed = jnp.sum(arrived[...].astype(F32), axis=0)
    rest = (half.astype(F32) - summed).astype(BF16)
    return lax.dot_general(rest, inverse, NN, preferred_element_type=F32).astype(BF16)


def backward_level(plan, level, *refs):
    sizes, table, inverse, front, arrived, _ = refs[:6]
    sources = refs[6 : 6 + plan.cols]
    solved, acc, out = refs[6 + plan.cols :]
    _, live = locate(plan, level, sizes)
    segment = solve_back(front[lax.axis_index("chain")], inverse[level], arrived)
    solved[...] = segment
    add_terms(plan, level, live, table, segment, sources, acc)
    out[...] = acc[pl.ds((level - 1) * plan.lanes, plan.lanes)].astype(BF16)


def finish(plan, *refs):
    levels = plan.levels
    sizes, inverse, arrived = refs[:3]
    fronts = refs[3 : 2 + levels]
    half_last = refs[2 + levels]
    done = refs[3 + levels : 2 + 2 * levels]
    out, hbuf, sbuf = refs[2 + 2 * levels :]
    lane = lax.axis_index("chain")
    for k in range(levels - 1):
        hbuf[k] = fronts[k][lane]
        sbuf[k + 1] = done[k][...]
    hbuf[levels - 1] = half_last[...]
    sbuf[0] = solve_back(hbuf[0], inverse[0], arrived)
    for r in range(plan.rows):
        row = r * plan.lanes + lane
        end = jnp.int32(0)
        level = jnp.int32(0)
        for k in range(levels):
            end = end + sizes[k]
            level = level + (row >= end).astype(jnp.int32)
        h, s = hbuf[level], sbuf[level]
        for q in range(plan.cols):
            out[q, r] = h
            out[q, plan.rows + r] = s


def per_device(rhs, pattern, factor, inverse, level_size):
    lanes = lax.axis_size("chain")
    cols = lax.axis_size("col")
    rows, _, probes, width = rhs.shape
    entries = pattern.shape[2]
    levels = level_size.shape[0]
    share = probes // cols
    plan = Plan(lanes, cols, rows, entries, share, width, levels)

    smem = pl.BlockSpec(memory_space=pltpu.SMEM)
    hbm = pl.BlockSpec(memory_space=pltpu.HBM)
    vmem = pl.BlockSpec(memory_space=pltpu.VMEM)
    segment_shape = pltpu.VMEM((share, width), BF16)
    front_shape = pltpu.VMEM((lanes, share, width), BF16)
    params = pltpu.CompilerParams(vmem_limit_bytes=12 * 1024 * 1024)

    def far_off(x):
        return pltpu.with_memory_space_constraint(x, pltpu.HBM)

    def held(x):
        return pltpu.with_memory_space_constraint(x, pltpu.VMEM)

    def store(level):
        return pltpu.VMEM((level * lanes + 1, share, width), BF16)

    def exchange(x):
        return held(lax.all_to_all(x, "chain", 0, 0, tiled=True))

    def around(x):
        return [held(x)] + [
            held(lax.ppermute(x, "col", [(i, (i + s) % cols) for i in range(cols)]))
            for s in range(1, cols)
        ]

    factor = far_off(factor.reshape(rows * plan.entries * width, width))
    first, own, rights, inverses = pl.pallas_call(
        functools.partial(forward_first, plan),
        out_shape=(
            front_shape,
            pltpu.VMEM((len(plan.near) * plan.deep + CODE_ROWS, width), BF16),
            pltpu.VMEM((levels, share, width), BF16),
            pltpu.VMEM((levels, width, width), BF16),
        ),
        in_specs=[smem, hbm, hbm, hbm, hbm],
        out_specs=(vmem,) * 4,
        scratch_shapes=[
            pltpu.VMEM((rows, 1, entries), jnp.int32),
            pltpu.VMEM((CODE_ROWS, width), F32),
            pltpu.VMEM((CODE_ROWS, width), BF16),
            pltpu.SemaphoreType.DMA((2 + 2 * levels + len(plan.near),)),
        ],
        compiler_params=params,
        name="forward_first",
    )(
        level_size,
        far_off(pattern),
        factor,
        far_off(rhs.reshape(rows, cols, share, width)),
        far_off(inverse.reshape(rows, width, width)),
    )
    rights, inverses = held(rights), held(inverses)
    near = around(own)
    fronts = [exchange(first)]

    mine, table, own = pl.pallas_call(
        functools.partial(forward_second, plan),
        out_shape=(
            front_shape,
            pltpu.VMEM((cols * TABLE_ROWS, width), jnp.int32),
            pltpu.VMEM((len(plan.far) * plan.deep, width), BF16),
        ),
        in_specs=[smem, hbm] + [vmem] * (3 + cols),
        out_specs=(vmem,) * 3,
        scratch_shapes=[
            pltpu.SMEM((cols * TABLE_ROWS, width), jnp.int32),
            store(1),
            pltpu.SemaphoreType.DMA((1 + len(plan.far),)),
        ],
        compiler_params=params,
        name="forward_second",
    )(level_size, factor, rights, inverses, fronts[0], *near)
    far = around(own)
    fronts.append(exchange(mine))

    def sources(level):
        return near if level in plan.near else far

    for k in range(2, levels - 1):
        mine = pl.pallas_call(
            functools.partial(forward_level, plan, k),
            out_shape=front_shape,
            in_specs=[smem] + [vmem] * (2 + cols + k),
            out_specs=vmem,
            scratch_shapes=[store(k)],
            compiler_params=params,
            name=f"forward_level_{k}",
        )(table, rights, inverses, *sources(k), *fronts)
        fronts.append(exchange(mine))

    last = levels - 1
    acc_shape = pltpu.VMEM((last * lanes + 1, share, width), F32)
    half_last, solved, acc, terms = pl.pallas_call(
        functools.partial(turn_level, plan, last),
        out_shape=(segment_shape, segment_shape, acc_shape, front_shape),
        in_specs=[smem, smem] + [vmem] * (2 + cols + last),
        out_specs=(vmem,) * 4,
        scratch_shapes=[store(last)],
        compiler_params=params,
        name="turn_level",
    )(level_size, table, rights, inverses, *sources(last), *fronts)
    done = [held(solved)]
    for k in range(last - 1, 0, -1):
        solved, acc, terms = pl.pallas_call(
            functools.partial(backward_level, plan, k),
            out_shape=(segment_shape, acc_shape, front_shape),
            in_specs=[smem, smem] + [vmem] * (4 + cols),
            out_specs=(vmem,) * 3,
            input_output_aliases={5: 1},
            compiler_params=params,
            name=f"backward_level_{k}",
        )(
            level_size,
            table,
            inverses,
            fronts[k],
            exchange(terms),
            held(acc),
            *sources(k),
        )
        done.insert(0, held(solved))
    shares = pl.pallas_call(
        functools.partial(finish, plan),
        out_shape=pltpu.VMEM((cols, 2 * rows, share, width), BF16),
        in_specs=[smem] + [vmem] * (1 + 2 * levels),
        out_specs=vmem,
        scratch_shapes=[
            pltpu.VMEM((levels, share, width), BF16),
            pltpu.VMEM((levels, share, width), BF16),
        ],
        compiler_params=params,
        name="finish",
    )(level_size, inverses, exchange(terms), *fronts, held(half_last), *done)
    whole = lax.all_to_all(shares, "col", 0, 0, tiled=True)
    whole = whole.transpose(1, 0, 2, 3).reshape(2, rows, 1, probes, width)
    return whole[0], whole[1]


def solution(mesh):
    return jax.shard_map(
        per_device,
        mesh=mesh,
        in_specs=(
            P(None, "chain", None, None),
            P(None, "chain", "col"),
            P(None, "chain", "col", None, None),
            P(None, "chain", None, None),
            P(),
        ),
        out_specs=(P(None, "chain", None, None), P(None, "chain", None, None)),
        check_vma=False,
    )
```

time: 214 us -> 196 us (0.916)
  between operations: 14.1 us -> 0.74 us
  local copies, waits for them, and re-layouts: 5.53 us -> 1.29 us
  blocking collectives: 175 us -> 171 us
  starting transfers between devices: 4.55 us -> 7.9 us
    all_to_all x10, blocking collectives: 168 us -> 161 us  [exchange(): return held(lax.all_to_all(x, 'chain', 0, 0, tiled=True))]
    unnamed x19 -> x3, local copies, waits for them, and re-layouts: 5.53 us -> 1.28 us
    ppermute x3 -> x6, starting transfers between devices: 4.51 us -> 7.9 us  [around(): lax.ppermute(x, 'col', [(i, (i + s) % cols) for i in range(cols)])]
    all_to_all x1, blocking collectives: 6.99 us -> 9.35 us  [per_device(): whole = lax.all_to_all(shares, 'col', 0, 0, tiled=True)]
  transfers between devices with their start and end apart: 4 -> 6, of which waited for: 1 -> 0; matrix products, arithmetic and copies ran while one was open for 0% -> 0% of each run, Pallas kernels for 1% -> 1%
where the time goes in v3:
time: 196 us
  blocking collectives  171 us (87%)
  Pallas kernels  15.2 us (8%)
  starting transfers between devices  7.9 us (4%)
    all_to_all x10, blocking collectives, exchange(): return held(lax.all_to_all(x, 'chain', 0, 0, tiled=True))  161 us
    all_to_all x1, blocking collectives, per_device(): whole = lax.all_to_all(shares, 'col', 0, 0, tiled=True)  9.35 us
    ppermute x6, starting transfers between devices, around(): lax.ppermute(x, 'col', [(i, (i + s) % cols) for i in range(cols)])  7.9 us
    pallas_call x4, Pallas kernels, per_device(): pl.pallas_call(functools.partial(backward_level, plan, k), out_shape=(seg...  4.94 us
  transfers between devices with their start and end apart: 6, of which 0 were waited for; matrix products, arithmetic and copies ran while one was open for 0% of the time, Pallas kernels for 1%

profile of v3, /device:TPU:1, one launch (start us, length us, event | category | flops | bytes accessed | tf_op | source)
XLA Modules:
  0.0 195.9 jit_solution(7274882719258839802)
XLA Ops:
  0.6 0.6 copy-done
  1.3 1.9 forward_first.1
  3.2 3.4 %collective-permute-start.2 = (bf16[1552,128]{1,0:T(8,128)(2,1)S(1)}, bf16[1552,128]{1,0:T(8,128)(2,1)S(1)}, u32[]{:S(2)}, u32[]{:S(2)}) collective-permute-start(bf16[1552,128]{1,0:T(8,128)(2,1)S(1)} %get-tuple-element.27.refs_5_.refs_3_.refs_6_), channel_id=1, source_target_pairs={{0,3},{1,0},{2,1},{3,2},{4,7},{5,4},{6,5},{7,6},{8,11},{9,8},{10,9... | collective-permute-start | bytes 1191944 | tf_op jit(solution)/shard_map/ppermute | solution.py:289
  6.6 0.5 collective-permute-start.1
  7.1 0.6 collective-permute-start
  7.7 24.1 %all_to_all.55.refs_4_.refs_7_.refs_8_.refs_3_ = bf16[64,8,128]{2,1,0:T(8,128)(2,1)S(1)} all-to-all(bf16[64,8,128]{2,1,0:T(8,128)(2,1)S(1)} %get-tuple-element.26), channel_id=1, replica_groups=mesh['chain'=64,'col'=4] {'chain'}, dimensions={0} | all-to-all | bytes 262144 | tf_op jit(solution)/shard_map/all_to_all | solution.py:285
  31.8 0.0 collective-permute-done.2.refs_8_.refs_6_.refs_9_
  31.8 0.0 collective-permute-done.1.refs_7_.refs_5_.refs_8_
  31.8 1.9 forward_second.1
  33.7 2.1 %collective-permute-start.5 = (bf16[2304,128]{1,0:T(8,128)(2,1)S(1)}, bf16[2304,128]{1,0:T(8,128)(2,1)S(1)}, u32[]{:S(2)}, u32[]{:S(2)}) collective-permute-start(bf16[2304,128]{1,0:T(8,128)(2,1)S(1)} %get-tuple-element.30.refs_3_.refs_4_.refs_6_), channel_id=1, source_target_pairs={{0,3},{1,0},{2,1},{3,2},{4,7},{5,4},{6,5},{7,6},{8,11},{9,8},{10,9... | collective-permute-start | bytes 1769480 | tf_op jit(solution)/shard_map/ppermute | solution.py:289
  35.9 1.2 collective-permute-start.4
  37.1 0.0 collective-permute-start.3
  37.1 17.9 %all_to_all.56.refs_8_.refs_9_.refs_3_.refs_4_ = bf16[64,8,128]{2,1,0:T(8,128)(2,1)S(1)} all-to-all(bf16[64,8,128]{2,1,0:T(8,128)(2,1)S(1)} %get-tuple-element.29), channel_id=1, replica_groups=mesh['chain'=64,'col'=4] {'chain'}, dimensions={0} | all-to-all | bytes 262144 | tf_op jit(solution)/shard_map/all_to_all | solution.py:285
  55.0 1.3 forward_level_2.1
  56.3 14.9 %all_to_all.57.refs_9_.refs_10_.refs_3_.refs_5_ = bf16[64,8,128]{2,1,0:T(8,128)(2,1)S(1)} all-to-all(bf16[64,8,128]{2,1,0:T(8,128)(2,1)S(1)} %forward_level_2.1), channel_id=1, replica_groups=mesh['chain'=64,'col'=4] {'chain'}, dimensions={0} | all-to-all | bytes 262144 | tf_op jit(solution)/shard_map/all_to_all | solution.py:285
  71.2 1.3 forward_level_3.1
  72.5 14.9 %all_to_all.58.refs_10_.refs_11_.refs_3_.refs_6_ = bf16[64,8,128]{2,1,0:T(8,128)(2,1)S(1)} all-to-all(bf16[64,8,128]{2,1,0:T(8,128)(2,1)S(1)} %forward_level_3.1), channel_id=1, replica_groups=mesh['chain'=64,'col'=4] {'chain'}, dimensions={0} | all-to-all | bytes 262144 | tf_op jit(solution)/shard_map/all_to_all | solution.py:285
  87.4 1.3 forward_level_4.1
  88.7 14.9 %all_to_all.59.refs_12_.refs_3_.refs_7_ = bf16[64,8,128]{2,1,0:T(8,128)(2,1)S(1)} all-to-all(bf16[64,8,128]{2,1,0:T(8,128)(2,1)S(1)} %forward_level_4.1), channel_id=1, replica_groups=mesh['chain'=64,'col'=4] {'chain'}, dimensions={0} | all-to-all | bytes 262144 | tf_op jit(solution)/shard_map/all_to_all | solution.py:285
  103.6 1.8 turn_level.1
  105.5 14.9 %all_to_all.60.refs_4_ = bf16[64,8,128]{2,1,0:T(8,128)(2,1)S(1)} all-to-all(bf16[64,8,128]{2,1,0:T(8,128)(2,1)S(1)} %get-tuple-element.31), channel_id=1, replica_groups=mesh['chain'=64,'col'=4] {'chain'}, dimensions={0} | all-to-all | bytes 262144 | tf_op jit(solution)/shard_map/all_to_all | solution.py:285
  120.4 1.2 backward_level_4.1
  121.6 15.2 %all_to_all.61.refs_4_ = bf16[64,8,128]{2,1,0:T(8,128)(2,1)S(1)} all-to-all(bf16[64,8,128]{2,1,0:T(8,128)(2,1)S(1)} %get-tuple-element.33), channel_id=1, replica_groups=mesh['chain'=64,'col'=4] {'chain'}, dimensions={0} | all-to-all | bytes 262144 | tf_op jit(solution)/shard_map/all_to_all | solution.py:285
  136.8 1.2 backward_level_3.1
  138.0 14.9 %all_to_all.62.refs_4_ = bf16[64,8,128]{2,1,0:T(8,128)(2,1)S(1)} all-to-all(bf16[64,8,128]{2,1,0:T(8,128)(2,1)S(1)} %get-tuple-element.35), channel_id=1, replica_groups=mesh['chain'=64,'col'=4] {'chain'}, dimensions={0} | all-to-all | bytes 262144 | tf_op jit(solution)/shard_map/all_to_all | solution.py:285
  152.9 1.2 backward_level_2.1
  154.1 14.9 %all_to_all.63.refs_4_ = bf16[64,8,128]{2,1,0:T(8,128)(2,1)S(1)} all-to-all(bf16[64,8,128]{2,1,0:T(8,128)(2,1)S(1)} %get-tuple-element.37), channel_id=1, replica_groups=mesh['chain'=64,'col'=4] {'chain'}, dimensions={0} | all-to-all | bytes 262144 | tf_op jit(solution)/shard_map/all_to_all | solution.py:285
  169.0 1.3 backward_level_1.1
  170.3 14.9 %all_to_all.64.refs_2_ = bf16[64,8,128]{2,1,0:T(8,128)(2,1)S(1)} all-to-all(bf16[64,8,128]{2,1,0:T(8,128)(2,1)S(1)} %get-tuple-element.39), channel_id=1, replica_groups=mesh['chain'=64,'col'=4] {'chain'}, dimensions={0} | all-to-all | bytes 262144 | tf_op jit(solution)/shard_map/all_to_all | solution.py:285
  185.2 0.7 finish.1
  185.9 9.3 %all_to_all.65 = bf16[4,8,8,128]{3,2,1,0:T(8,128)(2,1)S(1)} all-to-all(bf16[4,8,8,128]{3,2,1,0:T(8,128)(2,1)S(1)} %finish.1), channel_id=1, replica_groups=mesh['chain'=64,'col'=4] {'col'}, dimensions={0} | all-to-all | bytes 131072 | tf_op jit(solution)/shard_map/all_to_all | solution.py:401
  195.3 0.6 copy_bitcast_fusion
  (6 shorter events, 0.0 us)
Async XLA Ops:
  0.6 0.7 copy-start
  3.2 28.6 %collective-permute-start.2 = (bf16[1552,128]{1,0:T(8,128)(2,1)S(1)}, bf16[1552,128]{1,0:T(8,128)(2,1)S(1)}, u32[]{:S(2)}, u32[]{:S(2)}) collective-permute-start(bf16[1552,128]{1,0:T(8,128)(2,1)S(1)} %get-tuple-element.27.refs_5_.refs_3_.refs_6_), channel_id=1, source_target_pairs={{0,3},{1,0},{2,1},{3,2},{4,7},{5,4},{6,5},{7,6},{8,11},{9,8},{10,9... | collective-permute-start | bytes 1191944 | tf_op jit(solution)/shard_map/ppermute | solution.py:289
  6.6 25.2 %collective-permute-start.1 = (bf16[1552,128]{1,0:T(8,128)(2,1)S(1)}, bf16[1552,128]{1,0:T(8,128)(2,1)S(1)}, u32[]{:S(2)}, u32[]{:S(2)}) collective-permute-start(bf16[1552,128]{1,0:T(8,128)(2,1)S(1)} %get-tuple-element.27.refs_5_.refs_3_.refs_6_), channel_id=1, source_target_pairs={{0,2},{1,3},{2,0},{3,1},{4,6},{5,7},{6,4},{7,5},{8,10},{9,11},{10,... | collective-permute-start | bytes 1191944 | tf_op jit(solution)/shard_map/ppermute | solution.py:289
  7.1 24.7 %collective-permute-start = (bf16[1552,128]{1,0:T(8,128)(2,1)S(1)}, bf16[1552,128]{1,0:T(8,128)(2,1)S(1)}, u32[]{:S(2)}, u32[]{:S(2)}) collective-permute-start(bf16[1552,128]{1,0:T(8,128)(2,1)S(1)} %get-tuple-element.27.refs_5_.refs_3_.refs_6_), channel_id=1, source_target_pairs={{0,1},{1,2},{2,3},{3,0},{4,5},{5,6},{6,7},{7,4},{8,9},{9,10},{10,1... | collective-permute-start | bytes 1191944 | tf_op jit(solution)/shard_map/ppermute | solution.py:289
  33.7 37.5 %collective-permute-start.5 = (bf16[2304,128]{1,0:T(8,128)(2,1)S(1)}, bf16[2304,128]{1,0:T(8,128)(2,1)S(1)}, u32[]{:S(2)}, u32[]{:S(2)}) collective-permute-start(bf16[2304,128]{1,0:T(8,128)(2,1)S(1)} %get-tuple-element.30.refs_3_.refs_4_.refs_6_), channel_id=1, source_target_pairs={{0,3},{1,0},{2,1},{3,2},{4,7},{5,4},{6,5},{7,6},{8,11},{9,8},{10,9... | collective-permute-start | bytes 1769480 | tf_op jit(solution)/shard_map/ppermute | solution.py:289
  35.9 35.3 %collective-permute-start.4 = (bf16[2304,128]{1,0:T(8,128)(2,1)S(1)}, bf16[2304,128]{1,0:T(8,128)(2,1)S(1)}, u32[]{:S(2)}, u32[]{:S(2)}) collective-permute-start(bf16[2304,128]{1,0:T(8,128)(2,1)S(1)} %get-tuple-element.30.refs_3_.refs_4_.refs_6_), channel_id=1, source_target_pairs={{0,2},{1,3},{2,0},{3,1},{4,6},{5,7},{6,4},{7,5},{8,10},{9,11},{10,... | collective-permute-start | bytes 1769480 | tf_op jit(solution)/shard_map/ppermute | solution.py:289
  37.1 34.1 %collective-permute-start.3 = (bf16[2304,128]{1,0:T(8,128)(2,1)S(1)}, bf16[2304,128]{1,0:T(8,128)(2,1)S(1)}, u32[]{:S(2)}, u32[]{:S(2)}) collective-permute-start(bf16[2304,128]{1,0:T(8,128)(2,1)S(1)} %get-tuple-element.30.refs_3_.refs_4_.refs_6_), channel_id=1, source_target_pairs={{0,1},{1,2},{2,3},{3,0},{4,5},{5,6},{6,7},{7,4},{8,9},{9,10},{10,1... | collective-permute-start | bytes 1769480 | tf_op jit(solution)/shard_map/ppermute | solution.py:289

commit v4 on v3

--- a/solution.py
+++ b/solution.py
@@ -56,7 +56,7 @@
 
 def places_of(plan, level, table):
     return [
-        table[s * TABLE_ROWS + level, e]
+        table[level, s * plan.entries + e]
         for s in range(plan.cols)
         for e in range(plan.entries)
     ]
@@ -78,8 +78,7 @@
     ).astype(BF16)
 
 
-def add_terms(plan, level, live, table, segment, sources, acc):
-    segment = jnp.where(live, segment.astype(F32), 0.0).astype(BF16)
+def add_terms(plan, level, table, segment, sources, acc):
     weights = weights_of(plan, level, sources)
     terms = lax.dot_general(segment, weights, NN, preferred_element_type=F32)
     for j, at in enumerate(places_of(plan, level, table)):
@@ -140,24 +139,30 @@
 
 def fill_table(plan, sizes, near, table):
     split = len(plan.near) * plan.deep
-    columns = jnp.concatenate(
-        [
-            near[s][split : split + CODE_ROWS, :].astype(F32)[:TABLE_ROWS]
-            for s in range(plan.cols)
-        ],
-        axis=0,
-    ).astype(jnp.int32)
-    own_level = lax.rem(lax.broadcasted_iota(jnp.int32, columns.shape, 0), TABLE_ROWS)
-    level = jnp.zeros_like(columns)
-    end = jnp.int32(0)
+    shape = (TABLE_ROWS, plan.width)
+    row_level = lax.broadcasted_iota(jnp.int32, shape, 0)
+    entry = lax.broadcasted_iota(jnp.int32, shape, 1)
+    alive = jnp.zeros(shape, jnp.int32)
+    ends = []
     for k in range(plan.levels):
-        end = end + sizes[k]
-        level = level + (columns >= end).astype(jnp.int32)
-    table[...] = jnp.where(
-        level < own_level,
-        level * plan.lanes + lax.rem(columns, plan.lanes),
-        own_level * plan.lanes,
-    )
+        ends.append((ends[-1] if ends else 0) + sizes[k])
+        live = locate(plan, k, sizes)[1].astype(jnp.int32)
+        alive = alive + jnp.where(row_level == k, live, 0)
+    total = jnp.zeros(shape, jnp.int32)
+    for s in range(plan.cols):
+        columns = near[s][split : split + CODE_ROWS, :].astype(F32)[:TABLE_ROWS]
+        columns = columns.astype(jnp.int32)
+        level = jnp.zeros(shape, jnp.int32)
+        for end in ends:
+            level = level + (columns >= end).astype(jnp.int32)
+        place = jnp.where(
+            (level < row_level) & (alive > 0),
+            level * plan.lanes + lax.rem(columns, plan.lanes),
+            row_level * plan.lanes,
+        )
+        place = jnp.where(entry < plan.entries, place, 0)
+        total = total + (pltpu.roll(place, s * plan.entries, 1) if s else place)
+    table[...] = total
 
 
 def forward_second(plan, *refs):
@@ -196,11 +201,10 @@
 
 
 def turn_level(plan, level, *refs):
-    sizes, table, right, inverse = refs[:4]
-    sources = refs[4 : 4 + plan.cols]
-    earlier = refs[4 + plan.cols : 4 + plan.cols + level]
-    half, solved, acc, out, store = refs[4 + plan.cols + level :]
-    _, live = locate(plan, level, sizes)
+    table, right, inverse = refs[:3]
+    sources = refs[3 : 3 + plan.cols]
+    earlier = refs[3 + plan.cols : 3 + plan.cols + level]
+    half, solved, acc, out, store = refs[3 + plan.cols + level :]
     gather_store(plan, level, earlier, store)
     acc[...] = jnp.zeros(acc.shape, F32)
     segment = half_segment(plan, level, table, right, inverse, sources, store)
@@ -209,7 +213,7 @@
         segment, inverse[level], NN, preferred_element_type=F32
     ).astype(BF16)
     solved[...] = segment
-    add_terms(plan, level, live, table, segment, sources, acc)
+    add_terms(plan, level, table, segment, sources, acc)
     out[...] = acc[pl.ds((level - 1) * plan.lanes, plan.lanes)].astype(BF16)
 
 
@@ -220,13 +224,12 @@
 
 
 def backward_level(plan, level, *refs):
-    sizes, table, inverse, front, arrived, _ = refs[:6]
-    sources = refs[6 : 6 + plan.cols]
-    solved, acc, out = refs[6 + plan.cols :]
-    _, live = locate(plan, level, sizes)
+    table, inverse, front, arrived, _ = refs[:5]
+    sources = refs[5 : 5 + plan.cols]
+    solved, acc, out = refs[5 + plan.cols :]
     segment = solve_back(front[lax.axis_index("chain")], inverse[level], arrived)
     solved[...] = segment
-    add_terms(plan, level, live, table, segment, sources, acc)
+    add_terms(plan, level, table, segment, sources, acc)
     out[...] = acc[pl.ds((level - 1) * plan.lanes, plan.lanes)].astype(BF16)
 
 
@@ -324,13 +327,13 @@
         functools.partial(forward_second, plan),
         out_shape=(
             front_shape,
-            pltpu.VMEM((cols * TABLE_ROWS, width), jnp.int32),
+            pltpu.VMEM((TABLE_ROWS, width), jnp.int32),
             pltpu.VMEM((len(plan.far) * plan.deep, width), BF16),
         ),
         in_specs=[smem, hbm] + [vmem] * (3 + cols),
         out_specs=(vmem,) * 3,
         scratch_shapes=[
-            pltpu.SMEM((cols * TABLE_ROWS, width), jnp.int32),
+            pltpu.SMEM((TABLE_ROWS, width), jnp.int32),
             store(1),
             pltpu.SemaphoreType.DMA((1 + len(plan.far),)),
         ],
@@ -360,24 +363,23 @@
     half_last, solved, acc, terms = pl.pallas_call(
         functools.partial(turn_level, plan, last),
         out_shape=(segment_shape, segment_shape, acc_shape, front_shape),
-        in_specs=[smem, smem] + [vmem] * (2 + cols + last),
+        in_specs=[smem] + [vmem] * (2 + cols + last),
         out_specs=(vmem,) * 4,
         scratch_shapes=[store(last)],
         compiler_params=params,
         name="turn_level",
-    )(level_size, table, rights, inverses, *sources(last), *fronts)
+    )(table, rights, inverses, *sources(last), *fronts)
     done = [held(solved)]
     for k in range(last - 1, 0, -1):
         solved, acc, terms = pl.pallas_call(
             functools.partial(backward_level, plan, k),
             out_shape=(segment_shape, acc_shape, front_shape),
-            in_specs=[smem, smem] + [vmem] * (4 + cols),
+            in_specs=[smem] + [vmem] * (4 + cols),
             out_specs=(vmem,) * 3,
-            input_output_aliases={5: 1},
+            input_output_aliases={4: 1},
             compiler_params=params,
             name=f"backward_level_{k}",
         )(
-            level_size,
             table,
             inverses,
             fronts[k],

time: 196 us -> 195 us (level)
  no operation moved by 1% of the time
where the time goes in v4:
time: 195 us; the launch traced here: 194 us
  blocking collectives  171 us (88%)
  Pallas kernels  13.5 us (7%)
  starting transfers between devices  7.9 us (4%)
    all_to_all x10, blocking collectives, exchange(): return held(lax.all_to_all(x, 'chain', 0, 0, tiled=True))  161 us
    all_to_all x1, blocking collectives, per_device(): whole = lax.all_to_all(shares, 'col', 0, 0, tiled=True)  9.2 us
    ppermute x6, starting transfers between devices, around(): lax.ppermute(x, 'col', [(i, (i + s) % cols) for i in range(cols)])  7.9 us
    pallas_call x4, Pallas kernels, per_device(): pl.pallas_call(functools.partial(backward_level, plan, k), out_shape=(seg...  4.14 us
  transfers between devices with their start and end apart: 6, of which 0 were waited for; matrix products, arithmetic and copies ran while one was open for 0% of the time, Pallas kernels for 1%

profile of v4, /device:TPU:1, one launch (start us, length us, event | category | flops | bytes accessed | tf_op | source)
XLA Modules:
  0.0 194.0 jit_solution(11659347689307559456)
XLA Ops:
  0.6 0.0 copy-start
  0.6 0.6 copy-done
  1.3 1.9 forward_first.1
  3.2 3.4 %collective-permute-start.2 = (bf16[1552,128]{1,0:T(8,128)(2,1)S(1)}, bf16[1552,128]{1,0:T(8,128)(2,1)S(1)}, u32[]{:S(2)}, u32[]{:S(2)}) collective-permute-start(bf16[1552,128]{1,0:T(8,128)(2,1)S(1)} %get-tuple-element.27.refs_5_.refs_3_), channel_id=1, source_target_pairs={{0,3},{1,0},{2,1},{3,2},{4,7},{5,4},{6,5},{7,6},{8,11},{9,8},{10,9... | collective-permute-start | bytes 1191944 | tf_op jit(solution)/shard_map/ppermute | solution.py:292
  6.6 0.5 collective-permute-start.1
  7.1 0.6 collective-permute-start
  7.7 24.1 %all_to_all.55.refs_4_.refs_7_.refs_3_ = bf16[64,8,128]{2,1,0:T(8,128)(2,1)S(1)} all-to-all(bf16[64,8,128]{2,1,0:T(8,128)(2,1)S(1)} %get-tuple-element.26), channel_id=1, replica_groups=mesh['chain'=64,'col'=4] {'chain'}, dimensions={0} | all-to-all | bytes 262144 | tf_op jit(solution)/shard_map/all_to_all | solution.py:288
  31.8 0.0 collective-permute-done.refs_6_.refs_4_
  31.8 1.8 forward_second.1
  33.6 2.1 %collective-permute-start.5 = (bf16[2304,128]{1,0:T(8,128)(2,1)S(1)}, bf16[2304,128]{1,0:T(8,128)(2,1)S(1)}, u32[]{:S(2)}, u32[]{:S(2)}) collective-permute-start(bf16[2304,128]{1,0:T(8,128)(2,1)S(1)} %get-tuple-element.30.refs_3_.refs_5_), channel_id=1, source_target_pairs={{0,3},{1,0},{2,1},{3,2},{4,7},{5,4},{6,5},{7,6},{8,11},{9,8},{10,9... | collective-permute-start | bytes 1769480 | tf_op jit(solution)/shard_map/ppermute | solution.py:292
  35.7 1.2 collective-permute-start.4
  37.0 0.0 collective-permute-start.3
  37.0 17.9 %all_to_all.56.refs_8_.refs_2_.refs_4_ = bf16[64,8,128]{2,1,0:T(8,128)(2,1)S(1)} all-to-all(bf16[64,8,128]{2,1,0:T(8,128)(2,1)S(1)} %get-tuple-element.29), channel_id=1, replica_groups=mesh['chain'=64,'col'=4] {'chain'}, dimensions={0} | all-to-all | bytes 262144 | tf_op jit(solution)/shard_map/all_to_all | solution.py:288
  54.9 1.1 forward_level_2.1
  56.0 14.9 %all_to_all.57.refs_9_.refs_2_.refs_5_ = bf16[64,8,128]{2,1,0:T(8,128)(2,1)S(1)} all-to-all(bf16[64,8,128]{2,1,0:T(8,128)(2,1)S(1)} %forward_level_2.1), channel_id=1, replica_groups=mesh['chain'=64,'col'=4] {'chain'}, dimensions={0} | all-to-all | bytes 262144 | tf_op jit(solution)/shard_map/all_to_all | solution.py:288
  70.9 1.1 forward_level_3.1
  72.0 14.9 %all_to_all.58.refs_10_.refs_2_.refs_6_ = bf16[64,8,128]{2,1,0:T(8,128)(2,1)S(1)} all-to-all(bf16[64,8,128]{2,1,0:T(8,128)(2,1)S(1)} %forward_level_3.1), channel_id=1, replica_groups=mesh['chain'=64,'col'=4] {'chain'}, dimensions={0} | all-to-all | bytes 262144 | tf_op jit(solution)/shard_map/all_to_all | solution.py:288
  86.9 1.1 forward_level_4.1
  88.0 14.9 %all_to_all.59.refs_11_.refs_2_.refs_7_ = bf16[64,8,128]{2,1,0:T(8,128)(2,1)S(1)} all-to-all(bf16[64,8,128]{2,1,0:T(8,128)(2,1)S(1)} %forward_level_4.1), channel_id=1, replica_groups=mesh['chain'=64,'col'=4] {'chain'}, dimensions={0} | all-to-all | bytes 262144 | tf_op jit(solution)/shard_map/all_to_all | solution.py:288
  102.9 1.6 turn_level.1
  104.6 14.9 %all_to_all.60.refs_3_ = bf16[64,8,128]{2,1,0:T(8,128)(2,1)S(1)} all-to-all(bf16[64,8,128]{2,1,0:T(8,128)(2,1)S(1)} %get-tuple-element.31), channel_id=1, replica_groups=mesh['chain'=64,'col'=4] {'chain'}, dimensions={0} | all-to-all | bytes 262144 | tf_op jit(solution)/shard_map/all_to_all | solution.py:288
  119.5 1.0 backward_level_4.1
  120.5 15.1 %all_to_all.61.refs_3_ = bf16[64,8,128]{2,1,0:T(8,128)(2,1)S(1)} all-to-all(bf16[64,8,128]{2,1,0:T(8,128)(2,1)S(1)} %get-tuple-element.33), channel_id=1, replica_groups=mesh['chain'=64,'col'=4] {'chain'}, dimensions={0} | all-to-all | bytes 262144 | tf_op jit(solution)/shard_map/all_to_all | solution.py:288
  135.6 1.1 backward_level_3.1
  136.6 14.9 %all_to_all.62.refs_3_ = bf16[64,8,128]{2,1,0:T(8,128)(2,1)S(1)} all-to-all(bf16[64,8,128]{2,1,0:T(8,128)(2,1)S(1)} %get-tuple-element.35), channel_id=1, replica_groups=mesh['chain'=64,'col'=4] {'chain'}, dimensions={0} | all-to-all | bytes 262144 | tf_op jit(solution)/shard_map/all_to_all | solution.py:288
  151.5 1.0 backward_level_2.1
  152.5 14.9 %all_to_all.63.refs_3_ = bf16[64,8,128]{2,1,0:T(8,128)(2,1)S(1)} all-to-all(bf16[64,8,128]{2,1,0:T(8,128)(2,1)S(1)} %get-tuple-element.37), channel_id=1, replica_groups=mesh['chain'=64,'col'=4] {'chain'}, dimensions={0} | all-to-all | bytes 262144 | tf_op jit(solution)/shard_map/all_to_all | solution.py:288
  167.5 1.0 backward_level_1.1
  168.5 14.9 %all_to_all.64.refs_2_ = bf16[64,8,128]{2,1,0:T(8,128)(2,1)S(1)} all-to-all(bf16[64,8,128]{2,1,0:T(8,128)(2,1)S(1)} %get-tuple-element.39), channel_id=1, replica_groups=mesh['chain'=64,'col'=4] {'chain'}, dimensions={0} | all-to-all | bytes 262144 | tf_op jit(solution)/shard_map/all_to_all | solution.py:288
  183.4 0.7 finish.1
  184.2 9.2 %all_to_all.65 = bf16[4,8,8,128]{3,2,1,0:T(8,128)(2,1)S(1)} all-to-all(bf16[4,8,8,128]{3,2,1,0:T(8,128)(2,1)S(1)} %finish.1), channel_id=1, replica_groups=mesh['chain'=64,'col'=4] {'col'}, dimensions={0} | all-to-all | bytes 131072 | tf_op jit(solution)/shard_map/all_to_all | solution.py:403
  193.4 0.6 copy_bitcast_fusion
  (8 shorter events, 0.0 us)
Async XLA Ops:
  0.6 0.7 copy-start
  3.2 28.6 %collective-permute-start.2 = (bf16[1552,128]{1,0:T(8,128)(2,1)S(1)}, bf16[1552,128]{1,0:T(8,128)(2,1)S(1)}, u32[]{:S(2)}, u32[]{:S(2)}) collective-permute-start(bf16[1552,128]{1,0:T(8,128)(2,1)S(1)} %get-tuple-element.27.refs_5_.refs_3_), channel_id=1, source_target_pairs={{0,3},{1,0},{2,1},{3,2},{4,7},{5,4},{6,5},{7,6},{8,11},{9,8},{10,9... | collective-permute-start | bytes 1191944 | tf_op jit(solution)/shard_map/ppermute | solution.py:292
  6.6 25.2 %collective-permute-start.1 = (bf16[1552,128]{1,0:T(8,128)(2,1)S(1)}, bf16[1552,128]{1,0:T(8,128)(2,1)S(1)}, u32[]{:S(2)}, u32[]{:S(2)}) collective-permute-start(bf16[1552,128]{1,0:T(8,128)(2,1)S(1)} %get-tuple-element.27.refs_5_.refs_3_), channel_id=1, source_target_pairs={{0,2},{1,3},{2,0},{3,1},{4,6},{5,7},{6,4},{7,5},{8,10},{9,11},{10,... | collective-permute-start | bytes 1191944 | tf_op jit(solution)/shard_map/ppermute | solution.py:292
  7.1 24.7 %collective-permute-start = (bf16[1552,128]{1,0:T(8,128)(2,1)S(1)}, bf16[1552,128]{1,0:T(8,128)(2,1)S(1)}, u32[]{:S(2)}, u32[]{:S(2)}) collective-permute-start(bf16[1552,128]{1,0:T(8,128)(2,1)S(1)} %get-tuple-element.27.refs_5_.refs_3_), channel_id=1, source_target_pairs={{0,1},{1,2},{2,3},{3,0},{4,5},{5,6},{6,7},{7,4},{8,9},{9,10},{10,1... | collective-permute-start | bytes 1191944 | tf_op jit(solution)/shard_map/ppermute | solution.py:292
  33.6 37.3 %collective-permute-start.5 = (bf16[2304,128]{1,0:T(8,128)(2,1)S(1)}, bf16[2304,128]{1,0:T(8,128)(2,1)S(1)}, u32[]{:S(2)}, u32[]{:S(2)}) collective-permute-start(bf16[2304,128]{1,0:T(8,128)(2,1)S(1)} %get-tuple-element.30.refs_3_.refs_5_), channel_id=1, source_target_pairs={{0,3},{1,0},{2,1},{3,2},{4,7},{5,4},{6,5},{7,6},{8,11},{9,8},{10,9... | collective-permute-start | bytes 1769480 | tf_op jit(solution)/shard_map/ppermute | solution.py:292
  35.7 35.1 %collective-permute-start.4 = (bf16[2304,128]{1,0:T(8,128)(2,1)S(1)}, bf16[2304,128]{1,0:T(8,128)(2,1)S(1)}, u32[]{:S(2)}, u32[]{:S(2)}) collective-permute-start(bf16[2304,128]{1,0:T(8,128)(2,1)S(1)} %get-tuple-element.30.refs_3_.refs_5_), channel_id=1, source_target_pairs={{0,2},{1,3},{2,0},{3,1},{4,6},{5,7},{6,4},{7,5},{8,10},{9,11},{10,... | collective-permute-start | bytes 1769480 | tf_op jit(solution)/shard_map/ppermute | solution.py:292
  37.0 33.9 %collective-permute-start.3 = (bf16[2304,128]{1,0:T(8,128)(2,1)S(1)}, bf16[2304,128]{1,0:T(8,128)(2,1)S(1)}, u32[]{:S(2)}, u32[]{:S(2)}) collective-permute-start(bf16[2304,128]{1,0:T(8,128)(2,1)S(1)} %get-tuple-element.30.refs_3_.refs_5_), channel_id=1, source_target_pairs={{0,1},{1,2},{2,3},{3,0},{4,5},{5,6},{6,7},{7,4},{8,9},{9,10},{10,1... | collective-permute-start | bytes 1769480 | tf_op jit(solution)/shard_map/ppermute | solution.py:292
  167.5 16.0 %copy-start.1 = (s32[6]{0:T(128)S(1)}, s32[6]{0:T(128)}, u32[]{:S(2)}) copy-start(s32[6]{0:T(128)} %refs_0_.5) | copy-start | bytes 76

commit v5 on v4

--- a/solution.py
+++ b/solution.py
@@ -86,25 +86,31 @@
 
 
 def forward_first(plan, *refs):
-    sizes, pattern, factor, right, inverse = refs[:5]
-    out, near, rights, inverses, pats, wide, code, sems = refs[5:]
+    level_size, pattern, factor, right, inverse = refs[:5]
+    out, near, rights, inverses, sizes, pats, wide, code, sems = refs[5:]
     col = lax.axis_index("col")
-    slots = [locate(plan, k, sizes)[0] for k in range(plan.levels)]
     pick = pltpu.make_async_copy(pattern, pats, sems.at[0])
+    learn = pltpu.make_async_copy(
+        level_size, sizes, sems.at[2 + 2 * plan.levels + len(plan.near)]
+    )
+    learn.start()
     pick.start()
-    small = []
-    for k in range(plan.levels):
-        at = 1 + 2 * k
-        small.append(
-            pltpu.make_async_copy(inverse.at[slots[k]], inverses.at[k], sems.at[at])
-        )
-        small.append(
+
+    def pair(level, slot):
+        at = 1 + 2 * level
+        return [
+            pltpu.make_async_copy(inverse.at[slot], inverses.at[level], sems.at[at]),
             pltpu.make_async_copy(
-                right.at[slots[k], col], rights.at[k], sems.at[at + 1]
-            )
-        )
+                right.at[slot, col], rights.at[level], sems.at[at + 1]
+            ),
+        ]
+
+    small = pair(0, 0)
     for c in small:
         c.start()
+    wide[...] = jnp.zeros(wide.shape, F32)
+    learn.wait()
+    slots = [locate(plan, k, sizes)[0] for k in range(plan.levels)]
     large = [
         pltpu.make_async_copy(
             factor_row(plan, factor, k, sizes),
@@ -115,7 +121,11 @@
     ]
     for c in large:
         c.start()
-    wide[...] = jnp.zeros(wide.shape, F32)
+    for k in range(1, plan.levels):
+        more = pair(k, slots[k])
+        for c in more:
+            c.start()
+        small += more
     pick.wait()
     for k in range(1, plan.levels):
         wide[pl.ds(k, 1), pl.ds(0, plan.entries)] = pats[slots[k]].astype(F32)
@@ -162,13 +172,17 @@
         )
         place = jnp.where(entry < plan.entries, place, 0)
         total = total + (pltpu.roll(place, s * plan.entries, 1) if s else place)
-    table[...] = total
+    own = entry * plan.lanes + lax.axis_index("chain")
+    own_level = jnp.zeros(shape, jnp.int32)
+    for end in ends:
+        own_level = own_level + (own >= end).astype(jnp.int32)
+    table[...] = jnp.where(row_level == TABLE_ROWS - 1, own_level, total)
 
 
 def forward_second(plan, *refs):
     sizes, factor, right, inverse, front = refs[:5]
     near = refs[5 : 5 + plan.cols]
-    out, table, far, local, store, sems = refs[5 + plan.cols :]
+    out, table, far, draft, store, sems = refs[5 + plan.cols :]
     copies = [
         pltpu.make_async_copy(
             factor_row(plan, factor, k, sizes),
@@ -179,12 +193,12 @@
     ]
     for c in copies:
         c.start()
-    fill_table(plan, sizes, near, table)
-    copy = pltpu.make_async_copy(table, local, sems.at[0])
+    fill_table(plan, sizes, near, draft)
+    copy = pltpu.make_async_copy(draft, table, sems.at[0])
     copy.start()
     gather_store(plan, 1, [front], store)
     copy.wait()
-    segment = half_segment(plan, 1, local, right, inverse, near, store)
+    segment = half_segment(plan, 1, table, right, inverse, near, store)
     out[...] = jnp.broadcast_to(segment[None], out.shape)
     for c in copies:
         c.wait()
@@ -235,7 +249,7 @@
 
 def finish(plan, *refs):
     levels = plan.levels
-    sizes, inverse, arrived = refs[:3]
+    table, inverse, arrived = refs[:3]
     fronts = refs[3 : 2 + levels]
     half_last = refs[2 + levels]
     done = refs[3 + levels : 2 + 2 * levels]
@@ -247,12 +261,7 @@
     hbuf[levels - 1] = half_last[...]
     sbuf[0] = solve_back(hbuf[0], inverse[0], arrived)
     for r in range(plan.rows):
-        row = r * plan.lanes + lane
-        end = jnp.int32(0)
-        level = jnp.int32(0)
-        for k in range(levels):
-            end = end + sizes[k]
-            level = level + (row >= end).astype(jnp.int32)
+        level = table[TABLE_ROWS - 1, r]
         h, s = hbuf[level], sbuf[level]
         for q in range(plan.cols):
             out[q, r] = h
@@ -281,6 +290,9 @@
     def held(x):
         return pltpu.with_memory_space_constraint(x, pltpu.VMEM)
 
+    def scalars(x):
+        return pltpu.with_memory_space_constraint(x, pltpu.SMEM)
+
     def store(level):
         return pltpu.VMEM((level * lanes + 1, share, width), BF16)
 
@@ -294,32 +306,33 @@
         ]
 
     factor = far_off(factor.reshape(rows * plan.entries * width, width))
-    first, own, rights, inverses = pl.pallas_call(
+    first, own, rights, inverses, sizes = pl.pallas_call(
         functools.partial(forward_first, plan),
         out_shape=(
             front_shape,
             pltpu.VMEM((len(plan.near) * plan.deep + CODE_ROWS, width), BF16),
             pltpu.VMEM((levels, share, width), BF16),
             pltpu.VMEM((levels, width, width), BF16),
+            pltpu.SMEM((levels,), jnp.int32),
         ),
-        in_specs=[smem, hbm, hbm, hbm, hbm],
-        out_specs=(vmem,) * 4,
+        in_specs=[hbm] * 5,
+        out_specs=(vmem,) * 4 + (smem,),
         scratch_shapes=[
             pltpu.VMEM((rows, 1, entries), jnp.int32),
             pltpu.VMEM((CODE_ROWS, width), F32),
             pltpu.VMEM((CODE_ROWS, width), BF16),
-            pltpu.SemaphoreType.DMA((2 + 2 * levels + len(plan.near),)),
+            pltpu.SemaphoreType.DMA((3 + 2 * levels + len(plan.near),)),
         ],
         compiler_params=params,
         name="forward_first",
     )(
-        level_size,
+        far_off(level_size),
         far_off(pattern),
         factor,
         far_off(rhs.reshape(rows, cols, share, width)),
         far_off(inverse.reshape(rows, width, width)),
     )
-    rights, inverses = held(rights), held(inverses)
+    rights, inverses, sizes = held(rights), held(inverses), scalars(sizes)
     near = around(own)
     fronts = [exchange(first)]
 
@@ -327,19 +340,20 @@
         functools.partial(forward_second, plan),
         out_shape=(
             front_shape,
-            pltpu.VMEM((TABLE_ROWS, width), jnp.int32),
+            pltpu.SMEM((TABLE_ROWS, width), jnp.int32),
             pltpu.VMEM((len(plan.far) * plan.deep, width), BF16),
         ),
         in_specs=[smem, hbm] + [vmem] * (3 + cols),
-        out_specs=(vmem,) * 3,
+        out_specs=(vmem, smem, vmem),
         scratch_shapes=[
-            pltpu.SMEM((TABLE_ROWS, width), jnp.int32),
+            pltpu.VMEM((TABLE_ROWS, width), jnp.int32),
             store(1),
             pltpu.SemaphoreType.DMA((1 + len(plan.far),)),
         ],
         compiler_params=params,
         name="forward_second",
-    )(level_size, factor, rights, inverses, fronts[0], *near)
+    )(sizes, factor, rights, inverses, fronts[0], *near)
+    table = scalars(table)
     far = around(own)
     fronts.append(exchange(mine))
 
@@ -399,7 +413,7 @@
         ],
         compiler_params=params,
         name="finish",
-    )(level_size, inverses, exchange(terms), *fronts, held(half_last), *done)
+    )(table, inverses, exchange(terms), *fronts, held(half_last), *done)
     whole = lax.all_to_all(shares, "col", 0, 0, tiled=True)
     whole = whole.transpose(1, 0, 2, 3).reshape(2, rows, 1, probes, width)
     return whole[0], whole[1]

time: 195 us -> 188 us (0.964)
  Pallas kernels: 13.5 us -> 7.59 us
    pallas_call x4, Pallas kernels: 4.14 us -> 1.75 us  [per_device(): pl.pallas_call(functools.partial(backward_level, plan, k), out_shape=(seg...]
  transfers between devices with their start and end apart: 6 -> 6, of which waited for: 0 -> 0; matrix products, arithmetic and copies ran while one was open for 0% -> 0% of each run, Pallas kernels for 1% -> 0%
where the time goes in v5:
time: 188 us
  blocking collectives  171 us (91%)
  starting transfers between devices  7.9 us (4%)
  Pallas kernels  7.59 us (4%)
    all_to_all x10, blocking collectives, exchange(): return held(lax.all_to_all(x, 'chain', 0, 0, tiled=True))  161 us
    all_to_all x1, blocking collectives, per_device(): whole = lax.all_to_all(shares, 'col', 0, 0, tiled=True)  9.19 us
    ppermute x6, starting transfers between devices, around(): lax.ppermute(x, 'col', [(i, (i + s) % cols) for i in range(cols)])  7.9 us
  transfers between devices with their start and end apart: 6, of which 0 were waited for; matrix products, arithmetic and copies ran while one was open for 0% of the time, Pallas kernels for 0%

profile of v5, /device:TPU:1, one launch (start us, length us, event | category | flops | bytes accessed | tf_op | source)
XLA Modules:
  0.0 187.6 jit_solution(15154392201909102389)
XLA Ops:
  0.6 1.9 %forward_first.1 = (bf16[64,8,128]{2,1,0:T(8,128)(2,1)S(1)}, bf16[1552,128]{1,0:T(8,128)(2,1)S(1)}, bf16[6,8,128]{2,1,0:T(8,128)(2,1)S(1)}, bf16[6,128,128]{2,1,0:T(8,128)(2,1)S(1)}, s32[6]{0:T(128)S(4)}) custom-call(s32[6]{0:T(128)} %refs_0_.1, s32[4,1,6]{2,1,0:T(1,128)} %refs_1_.1, bf16[3072,128]{1,0:T(8,128)(2,1)} %bitcast.12, ...), custom_call_target="tpu_custom_call" | custom-call | tf_op jit(solution)/shard_map/forward_first/pallas_call | solution.py:309
  2.5 3.4 %collective-permute-start.2 = (bf16[1552,128]{1,0:T(8,128)(2,1)S(1)}, bf16[1552,128]{1,0:T(8,128)(2,1)S(1)}, u32[]{:S(2)}, u32[]{:S(2)}) collective-permute-start(bf16[1552,128]{1,0:T(8,128)(2,1)S(1)} %get-tuple-element.29.refs_5_.refs_3_), channel_id=1, source_target_pairs={{0,3},{1,0},{2,1},{3,2},{4,7},{5,4},{6,5},{7,6},{8,11},{9,8},{10,9... | collective-permute-start | bytes 1191944 | tf_op jit(solution)/shard_map/ppermute | solution.py:304
  5.9 0.5 collective-permute-start.1
  6.4 0.6 collective-permute-start
  7.0 24.1 %all_to_all.55.refs_4_.refs_7_.refs_3_ = bf16[64,8,128]{2,1,0:T(8,128)(2,1)S(1)} all-to-all(bf16[64,8,128]{2,1,0:T(8,128)(2,1)S(1)} %get-tuple-element.28), channel_id=1, replica_groups=mesh['chain'=64,'col'=4] {'chain'}, dimensions={0} | all-to-all | bytes 262144 | tf_op jit(solution)/shard_map/all_to_all | solution.py:300
  31.1 0.0 collective-permute-done.2.refs_8_.refs_6_
  31.1 0.0 collective-permute-done.1.refs_7_.refs_5_
  31.1 0.0 collective-permute-done.refs_6_.refs_4_
  31.1 1.3 forward_second.1
  32.4 2.1 %collective-permute-start.5 = (bf16[2304,128]{1,0:T(8,128)(2,1)S(1)}, bf16[2304,128]{1,0:T(8,128)(2,1)S(1)}, u32[]{:S(2)}, u32[]{:S(2)}) collective-permute-start(bf16[2304,128]{1,0:T(8,128)(2,1)S(1)} %get-tuple-element.32.refs_3_.refs_5_), channel_id=1, source_target_pairs={{0,3},{1,0},{2,1},{3,2},{4,7},{5,4},{6,5},{7,6},{8,11},{9,8},{10,9... | collective-permute-start | bytes 1769480 | tf_op jit(solution)/shard_map/ppermute | solution.py:304
  34.5 1.2 collective-permute-start.4
  35.8 0.0 collective-permute-start.3
  35.8 17.9 %all_to_all.56.refs_8_.refs_2_.refs_4_ = bf16[64,8,128]{2,1,0:T(8,128)(2,1)S(1)} all-to-all(bf16[64,8,128]{2,1,0:T(8,128)(2,1)S(1)} %get-tuple-element.31), channel_id=1, replica_groups=mesh['chain'=64,'col'=4] {'chain'}, dimensions={0} | all-to-all | bytes 262144 | tf_op jit(solution)/shard_map/all_to_all | solution.py:300
  53.7 0.5 forward_level_2.1
  54.1 14.9 %all_to_all.57.refs_9_.refs_2_.refs_5_ = bf16[64,8,128]{2,1,0:T(8,128)(2,1)S(1)} all-to-all(bf16[64,8,128]{2,1,0:T(8,128)(2,1)S(1)} %forward_level_2.1), channel_id=1, replica_groups=mesh['chain'=64,'col'=4] {'chain'}, dimensions={0} | all-to-all | bytes 262144 | tf_op jit(solution)/shard_map/all_to_all | solution.py:300
  69.1 0.5 forward_level_3.1
  69.6 14.9 %all_to_all.58.refs_10_.refs_2_.refs_6_ = bf16[64,8,128]{2,1,0:T(8,128)(2,1)S(1)} all-to-all(bf16[64,8,128]{2,1,0:T(8,128)(2,1)S(1)} %forward_level_3.1), channel_id=1, replica_groups=mesh['chain'=64,'col'=4] {'chain'}, dimensions={0} | all-to-all | bytes 262144 | tf_op jit(solution)/shard_map/all_to_all | solution.py:300
  84.5 0.5 forward_level_4.1
  85.0 14.9 %all_to_all.59.refs_11_.refs_2_.refs_7_ = bf16[64,8,128]{2,1,0:T(8,128)(2,1)S(1)} all-to-all(bf16[64,8,128]{2,1,0:T(8,128)(2,1)S(1)} %forward_level_4.1), channel_id=1, replica_groups=mesh['chain'=64,'col'=4] {'chain'}, dimensions={0} | all-to-all | bytes 262144 | tf_op jit(solution)/shard_map/all_to_all | solution.py:300
  99.9 1.0 turn_level.1
  101.0 14.9 %all_to_all.60.refs_3_ = bf16[64,8,128]{2,1,0:T(8,128)(2,1)S(1)} all-to-all(bf16[64,8,128]{2,1,0:T(8,128)(2,1)S(1)} %get-tuple-element.33), channel_id=1, replica_groups=mesh['chain'=64,'col'=4] {'chain'}, dimensions={0} | all-to-all | bytes 262144 | tf_op jit(solution)/shard_map/all_to_all | solution.py:300
  115.9 0.5 backward_level_4.1
  116.4 15.2 %all_to_all.61.refs_3_ = bf16[64,8,128]{2,1,0:T(8,128)(2,1)S(1)} all-to-all(bf16[64,8,128]{2,1,0:T(8,128)(2,1)S(1)} %get-tuple-element.35), channel_id=1, replica_groups=mesh['chain'=64,'col'=4] {'chain'}, dimensions={0} | all-to-all | bytes 262144 | tf_op jit(solution)/shard_map/all_to_all | solution.py:300
  131.5 0.4 backward_level_3.1
  131.9 14.9 %all_to_all.62.refs_3_ = bf16[64,8,128]{2,1,0:T(8,128)(2,1)S(1)} all-to-all(bf16[64,8,128]{2,1,0:T(8,128)(2,1)S(1)} %get-tuple-element.37), channel_id=1, replica_groups=mesh['chain'=64,'col'=4] {'chain'}, dimensions={0} | all-to-all | bytes 262144 | tf_op jit(solution)/shard_map/all_to_all | solution.py:300
  146.8 0.4 backward_level_2.1
  147.3 14.9 %all_to_all.63.refs_3_ = bf16[64,8,128]{2,1,0:T(8,128)(2,1)S(1)} all-to-all(bf16[64,8,128]{2,1,0:T(8,128)(2,1)S(1)} %get-tuple-element.39), channel_id=1, replica_groups=mesh['chain'=64,'col'=4] {'chain'}, dimensions={0} | all-to-all | bytes 262144 | tf_op jit(solution)/shard_map/all_to_all | solution.py:300
  162.1 0.4 backward_level_1.1
  162.6 14.9 %all_to_all.64.refs_2_ = bf16[64,8,128]{2,1,0:T(8,128)(2,1)S(1)} all-to-all(bf16[64,8,128]{2,1,0:T(8,128)(2,1)S(1)} %get-tuple-element.41), channel_id=1, replica_groups=mesh['chain'=64,'col'=4] {'chain'}, dimensions={0} | all-to-all | bytes 262144 | tf_op jit(solution)/shard_map/all_to_all | solution.py:300
  177.5 0.2 finish.1
  177.7 9.2 %all_to_all.65 = bf16[4,8,8,128]{3,2,1,0:T(8,128)(2,1)S(1)} all-to-all(bf16[4,8,8,128]{3,2,1,0:T(8,128)(2,1)S(1)} %finish.1), channel_id=1, replica_groups=mesh['chain'=64,'col'=4] {'col'}, dimensions={0} | all-to-all | bytes 131072 | tf_op jit(solution)/shard_map/all_to_all | solution.py:417
  186.9 0.6 copy_bitcast_fusion
  (4 shorter events, 0.0 us)
Async XLA Ops:
  2.5 28.6 %collective-permute-start.2 = (bf16[1552,128]{1,0:T(8,128)(2,1)S(1)}, bf16[1552,128]{1,0:T(8,128)(2,1)S(1)}, u32[]{:S(2)}, u32[]{:S(2)}) collective-permute-start(bf16[1552,128]{1,0:T(8,128)(2,1)S(1)} %get-tuple-element.29.refs_5_.refs_3_), channel_id=1, source_target_pairs={{0,3},{1,0},{2,1},{3,2},{4,7},{5,4},{6,5},{7,6},{8,11},{9,8},{10,9... | collective-permute-start | bytes 1191944 | tf_op jit(solution)/shard_map/ppermute | solution.py:304
  5.9 25.2 %collective-permute-start.1 = (bf16[1552,128]{1,0:T(8,128)(2,1)S(1)}, bf16[1552,128]{1,0:T(8,128)(2,1)S(1)}, u32[]{:S(2)}, u32[]{:S(2)}) collective-permute-start(bf16[1552,128]{1,0:T(8,128)(2,1)S(1)} %get-tuple-element.29.refs_5_.refs_3_), channel_id=1, source_target_pairs={{0,2},{1,3},{2,0},{3,1},{4,6},{5,7},{6,4},{7,5},{8,10},{9,11},{10,... | collective-permute-start | bytes 1191944 | tf_op jit(solution)/shard_map/ppermute | solution.py:304
  6.4 24.7 %collective-permute-start = (bf16[1552,128]{1,0:T(8,128)(2,1)S(1)}, bf16[1552,128]{1,0:T(8,128)(2,1)S(1)}, u32[]{:S(2)}, u32[]{:S(2)}) collective-permute-start(bf16[1552,128]{1,0:T(8,128)(2,1)S(1)} %get-tuple-element.29.refs_5_.refs_3_), channel_id=1, source_target_pairs={{0,1},{1,2},{2,3},{3,0},{4,5},{5,6},{6,7},{7,4},{8,9},{9,10},{10,1... | collective-permute-start | bytes 1191944 | tf_op jit(solution)/shard_map/ppermute | solution.py:304
  32.4 36.7 %collective-permute-start.5 = (bf16[2304,128]{1,0:T(8,128)(2,1)S(1)}, bf16[2304,128]{1,0:T(8,128)(2,1)S(1)}, u32[]{:S(2)}, u32[]{:S(2)}) collective-permute-start(bf16[2304,128]{1,0:T(8,128)(2,1)S(1)} %get-tuple-element.32.refs_3_.refs_5_), channel_id=1, source_target_pairs={{0,3},{1,0},{2,1},{3,2},{4,7},{5,4},{6,5},{7,6},{8,11},{9,8},{10,9... | collective-permute-start | bytes 1769480 | tf_op jit(solution)/shard_map/ppermute | solution.py:304
  34.5 34.5 %collective-permute-start.4 = (bf16[2304,128]{1,0:T(8,128)(2,1)S(1)}, bf16[2304,128]{1,0:T(8,128)(2,1)S(1)}, u32[]{:S(2)}, u32[]{:S(2)}) collective-permute-start(bf16[2304,128]{1,0:T(8,128)(2,1)S(1)} %get-tuple-element.32.refs_3_.refs_5_), channel_id=1, source_target_pairs={{0,2},{1,3},{2,0},{3,1},{4,6},{5,7},{6,4},{7,5},{8,10},{9,11},{10,... | collective-permute-start | bytes 1769480 | tf_op jit(solution)/shard_map/ppermute | solution.py:304
  35.8 33.3 %collective-permute-start.3 = (bf16[2304,128]{1,0:T(8,128)(2,1)S(1)}, bf16[2304,128]{1,0:T(8,128)(2,1)S(1)}, u32[]{:S(2)}, u32[]{:S(2)}) collective-permute-start(bf16[2304,128]{1,0:T(8,128)(2,1)S(1)} %get-tuple-element.32.refs_3_.refs_5_), channel_id=1, source_target_pairs={{0,1},{1,2},{2,3},{3,0},{4,5},{5,6},{6,7},{7,4},{8,9},{9,10},{10,1... | collective-permute-start | bytes 1769480 | tf_op jit(solution)/shard_map/ppermute | solution.py:304

commit v6 on v5

--- a/solution.py
+++ b/solution.py
@@ -301,8 +301,8 @@
 
     def around(x):
         return [held(x)] + [
-            held(lax.ppermute(x, "col", [(i, (i + s) % cols) for i in range(cols)]))
-            for s in range(1, cols)
+            held(lax.ppermute(x, "col", [(i, i ^ s) for i in range(cols)]))
+            for s in (1, 3, 2)
         ]
 
     factor = far_off(factor.reshape(rows * plan.entries * width, width))

time: 188 us -> 187 us (level)
  blocking collectives: 171 us -> 168 us
where the time goes in v6:
time: 187 us; the launch traced here: 186 us
  blocking collectives  168 us (90%)
  starting transfers between devices  8.75 us (5%)
  Pallas kernels  7.6 us (4%)
    all_to_all x10, blocking collectives, exchange(): return held(lax.all_to_all(x, 'chain', 0, 0, tiled=True))  160 us
    ppermute x6, starting transfers between devices, around(): lax.ppermute(x, 'col', [(i, i ^ s) for i in range(cols)])  8.75 us
    all_to_all x1, blocking collectives, per_device(): whole = lax.all_to_all(shares, 'col', 0, 0, tiled=True)  7.87 us
  transfers between devices with their start and end apart: 6, of which 0 were waited for; matrix products, arithmetic and copies ran while one was open for 0% of the time, Pallas kernels for 0%

profile of v6, /device:TPU:1, one launch (start us, length us, event | category | flops | bytes accessed | tf_op | source)
XLA Modules:
  0.0 185.8 jit_solution(12497239391102089269)
XLA Ops:
  0.6 1.9 %forward_first.1 = (bf16[64,8,128]{2,1,0:T(8,128)(2,1)S(1)}, bf16[1552,128]{1,0:T(8,128)(2,1)S(1)}, bf16[6,8,128]{2,1,0:T(8,128)(2,1)S(1)}, bf16[6,128,128]{2,1,0:T(8,128)(2,1)S(1)}, s32[6]{0:T(128)S(4)}) custom-call(s32[6]{0:T(128)} %refs_0_.1, s32[4,1,6]{2,1,0:T(1,128)} %refs_1_.1, bf16[3072,128]{1,0:T(8,128)(2,1)} %bitcast.12, ...), custom_call_target="tpu_custom_call" | custom-call | tf_op jit(solution)/shard_map/forward_first/pallas_call | solution.py:309
  2.5 3.7 %collective-permute-start.2 = (bf16[1552,128]{1,0:T(8,128)(2,1)S(1)}, bf16[1552,128]{1,0:T(8,128)(2,1)S(1)}, u32[]{:S(2)}, u32[]{:S(2)}) collective-permute-start(bf16[1552,128]{1,0:T(8,128)(2,1)S(1)} %get-tuple-element.29.refs_5_.refs_3_), channel_id=1, source_target_pairs={{0,2},{1,3},{2,0},{3,1},{4,6},{5,7},{6,4},{7,5},{8,10},{9,11},{10,... | collective-permute-start | bytes 1191944 | tf_op jit(solution)/shard_map/ppermute | solution.py:304
  6.2 0.9 collective-permute-start.1
  7.1 0.0 collective-permute-start
  7.1 23.8 %all_to_all.55.refs_4_.refs_7_.refs_3_ = bf16[64,8,128]{2,1,0:T(8,128)(2,1)S(1)} all-to-all(bf16[64,8,128]{2,1,0:T(8,128)(2,1)S(1)} %get-tuple-element.28), channel_id=1, replica_groups=mesh['chain'=64,'col'=4] {'chain'}, dimensions={0} | all-to-all | bytes 262144 | tf_op jit(solution)/shard_map/all_to_all | solution.py:300
  30.8 0.0 collective-permute-done.2.refs_8_.refs_6_
  30.9 0.0 collective-permute-done.1.refs_7_.refs_5_
  30.9 0.0 collective-permute-done.refs_6_.refs_4_
  30.9 1.3 forward_second.1
  32.1 3.4 %collective-permute-start.5 = (bf16[2304,128]{1,0:T(8,128)(2,1)S(1)}, bf16[2304,128]{1,0:T(8,128)(2,1)S(1)}, u32[]{:S(2)}, u32[]{:S(2)}) collective-permute-start(bf16[2304,128]{1,0:T(8,128)(2,1)S(1)} %get-tuple-element.32.refs_3_.refs_5_), channel_id=1, source_target_pairs={{0,2},{1,3},{2,0},{3,1},{4,6},{5,7},{6,4},{7,5},{8,10},{9,11},{10,... | collective-permute-start | bytes 1769480 | tf_op jit(solution)/shard_map/ppermute | solution.py:304
  35.5 0.9 collective-permute-start.4
  36.3 0.0 collective-permute-start.3
  36.3 16.9 %all_to_all.56.refs_8_.refs_2_.refs_4_ = bf16[64,8,128]{2,1,0:T(8,128)(2,1)S(1)} all-to-all(bf16[64,8,128]{2,1,0:T(8,128)(2,1)S(1)} %get-tuple-element.31), channel_id=1, replica_groups=mesh['chain'=64,'col'=4] {'chain'}, dimensions={0} | all-to-all | bytes 262144 | tf_op jit(solution)/shard_map/all_to_all | solution.py:300
  53.2 0.5 forward_level_2.1
  53.7 14.9 %all_to_all.57.refs_9_.refs_2_.refs_5_ = bf16[64,8,128]{2,1,0:T(8,128)(2,1)S(1)} all-to-all(bf16[64,8,128]{2,1,0:T(8,128)(2,1)S(1)} %forward_level_2.1), channel_id=1, replica_groups=mesh['chain'=64,'col'=4] {'chain'}, dimensions={0} | all-to-all | bytes 262144 | tf_op jit(solution)/shard_map/all_to_all | solution.py:300
  68.6 0.5 forward_level_3.1
  69.1 14.9 %all_to_all.58.refs_10_.refs_2_.refs_6_ = bf16[64,8,128]{2,1,0:T(8,128)(2,1)S(1)} all-to-all(bf16[64,8,128]{2,1,0:T(8,128)(2,1)S(1)} %forward_level_3.1), channel_id=1, replica_groups=mesh['chain'=64,'col'=4] {'chain'}, dimensions={0} | all-to-all | bytes 262144 | tf_op jit(solution)/shard_map/all_to_all | solution.py:300
  84.1 0.5 forward_level_4.1
  84.6 14.9 %all_to_all.59.refs_11_.refs_2_.refs_7_ = bf16[64,8,128]{2,1,0:T(8,128)(2,1)S(1)} all-to-all(bf16[64,8,128]{2,1,0:T(8,128)(2,1)S(1)} %forward_level_4.1), channel_id=1, replica_groups=mesh['chain'=64,'col'=4] {'chain'}, dimensions={0} | all-to-all | bytes 262144 | tf_op jit(solution)/shard_map/all_to_all | solution.py:300
  99.5 1.0 turn_level.1
  100.5 14.9 %all_to_all.60.refs_3_ = bf16[64,8,128]{2,1,0:T(8,128)(2,1)S(1)} all-to-all(bf16[64,8,128]{2,1,0:T(8,128)(2,1)S(1)} %get-tuple-element.33), channel_id=1, replica_groups=mesh['chain'=64,'col'=4] {'chain'}, dimensions={0} | all-to-all | bytes 262144 | tf_op jit(solution)/shard_map/all_to_all | solution.py:300
  115.5 0.4 backward_level_4.1
  115.9 14.9 %all_to_all.61.refs_3_ = bf16[64,8,128]{2,1,0:T(8,128)(2,1)S(1)} all-to-all(bf16[64,8,128]{2,1,0:T(8,128)(2,1)S(1)} %get-tuple-element.35), channel_id=1, replica_groups=mesh['chain'=64,'col'=4] {'chain'}, dimensions={0} | all-to-all | bytes 262144 | tf_op jit(solution)/shard_map/all_to_all | solution.py:300
  130.8 0.4 backward_level_3.1
  131.2 15.1 %all_to_all.62.refs_3_ = bf16[64,8,128]{2,1,0:T(8,128)(2,1)S(1)} all-to-all(bf16[64,8,128]{2,1,0:T(8,128)(2,1)S(1)} %get-tuple-element.37), channel_id=1, replica_groups=mesh['chain'=64,'col'=4] {'chain'}, dimensions={0} | all-to-all | bytes 262144 | tf_op jit(solution)/shard_map/all_to_all | solution.py:300
  146.3 0.5 backward_level_2.1
  146.8 14.9 %all_to_all.63.refs_3_ = bf16[64,8,128]{2,1,0:T(8,128)(2,1)S(1)} all-to-all(bf16[64,8,128]{2,1,0:T(8,128)(2,1)S(1)} %get-tuple-element.39), channel_id=1, replica_groups=mesh['chain'=64,'col'=4] {'chain'}, dimensions={0} | all-to-all | bytes 262144 | tf_op jit(solution)/shard_map/all_to_all | solution.py:300
  161.7 0.4 backward_level_1.1
  162.2 14.9 %all_to_all.64.refs_2_ = bf16[64,8,128]{2,1,0:T(8,128)(2,1)S(1)} all-to-all(bf16[64,8,128]{2,1,0:T(8,128)(2,1)S(1)} %get-tuple-element.41), channel_id=1, replica_groups=mesh['chain'=64,'col'=4] {'chain'}, dimensions={0} | all-to-all | bytes 262144 | tf_op jit(solution)/shard_map/all_to_all | solution.py:300
  177.1 0.2 finish.1
  177.3 7.9 %all_to_all.65 = bf16[4,8,8,128]{3,2,1,0:T(8,128)(2,1)S(1)} all-to-all(bf16[4,8,8,128]{3,2,1,0:T(8,128)(2,1)S(1)} %finish.1), channel_id=1, replica_groups=mesh['chain'=64,'col'=4] {'col'}, dimensions={0} | all-to-all | bytes 131072 | tf_op jit(solution)/shard_map/all_to_all | solution.py:417
  185.2 0.6 copy_bitcast_fusion
  (4 shorter events, 0.0 us)
Async XLA Ops:
  2.5 28.3 %collective-permute-start.2 = (bf16[1552,128]{1,0:T(8,128)(2,1)S(1)}, bf16[1552,128]{1,0:T(8,128)(2,1)S(1)}, u32[]{:S(2)}, u32[]{:S(2)}) collective-permute-start(bf16[1552,128]{1,0:T(8,128)(2,1)S(1)} %get-tuple-element.29.refs_5_.refs_3_), channel_id=1, source_target_pairs={{0,2},{1,3},{2,0},{3,1},{4,6},{5,7},{6,4},{7,5},{8,10},{9,11},{10,... | collective-permute-start | bytes 1191944 | tf_op jit(solution)/shard_map/ppermute | solution.py:304
  6.2 24.7 %collective-permute-start.1 = (bf16[1552,128]{1,0:T(8,128)(2,1)S(1)}, bf16[1552,128]{1,0:T(8,128)(2,1)S(1)}, u32[]{:S(2)}, u32[]{:S(2)}) collective-permute-start(bf16[1552,128]{1,0:T(8,128)(2,1)S(1)} %get-tuple-element.29.refs_5_.refs_3_), channel_id=1, source_target_pairs={{0,3},{1,2},{2,1},{3,0},{4,7},{5,6},{6,5},{7,4},{8,11},{9,10},{10,... | collective-permute-start | bytes 1191944 | tf_op jit(solution)/shard_map/ppermute | solution.py:304
  7.1 23.8 %collective-permute-start = (bf16[1552,128]{1,0:T(8,128)(2,1)S(1)}, bf16[1552,128]{1,0:T(8,128)(2,1)S(1)}, u32[]{:S(2)}, u32[]{:S(2)}) collective-permute-start(bf16[1552,128]{1,0:T(8,128)(2,1)S(1)} %get-tuple-element.29.refs_5_.refs_3_), channel_id=1, source_target_pairs={{0,1},{1,0},{2,3},{3,2},{4,5},{5,4},{6,7},{7,6},{8,9},{9,8},{10,11... | collective-permute-start | bytes 1191944 | tf_op jit(solution)/shard_map/ppermute | solution.py:304
  32.1 36.5 %collective-permute-start.5 = (bf16[2304,128]{1,0:T(8,128)(2,1)S(1)}, bf16[2304,128]{1,0:T(8,128)(2,1)S(1)}, u32[]{:S(2)}, u32[]{:S(2)}) collective-permute-start(bf16[2304,128]{1,0:T(8,128)(2,1)S(1)} %get-tuple-element.32.refs_3_.refs_5_), channel_id=1, source_target_pairs={{0,2},{1,3},{2,0},{3,1},{4,6},{5,7},{6,4},{7,5},{8,10},{9,11},{10,... | collective-permute-start | bytes 1769480 | tf_op jit(solution)/shard_map/ppermute | solution.py:304
  35.5 33.2 %collective-permute-start.4 = (bf16[2304,128]{1,0:T(8,128)(2,1)S(1)}, bf16[2304,128]{1,0:T(8,128)(2,1)S(1)}, u32[]{:S(2)}, u32[]{:S(2)}) collective-permute-start(bf16[2304,128]{1,0:T(8,128)(2,1)S(1)} %get-tuple-element.32.refs_3_.refs_5_), channel_id=1, source_target_pairs={{0,3},{1,2},{2,1},{3,0},{4,7},{5,6},{6,5},{7,4},{8,11},{9,10},{10,... | collective-permute-start | bytes 1769480 | tf_op jit(solution)/shard_map/ppermute | solution.py:304
  36.3 32.3 %collective-permute-start.3 = (bf16[2304,128]{1,0:T(8,128)(2,1)S(1)}, bf16[2304,128]{1,0:T(8,128)(2,1)S(1)}, u32[]{:S(2)}, u32[]{:S(2)}) collective-permute-start(bf16[2304,128]{1,0:T(8,128)(2,1)S(1)} %get-tuple-element.32.refs_3_.refs_5_), channel_id=1, source_target_pairs={{0,1},{1,0},{2,3},{3,2},{4,5},{5,4},{6,7},{7,6},{8,9},{9,8},{10,11... | collective-permute-start | bytes 1769480 | tf_op jit(solution)/shard_map/ppermute | solution.py:304

commit v7 on v6

--- a/solution.py
+++ b/solution.py
@@ -35,11 +35,6 @@
     live = (slot < plan.rows) & (slot * plan.lanes + lane < start + sizes[level])
     low, high = plan.slots(level)
     return jnp.clip(slot, low, high), live
-
-
-def factor_row(plan, factor, level, sizes):
-    slot, _ = locate(plan, level, sizes)
-    return factor.at[pl.ds(pl.multiple_of(slot * plan.deep, plan.deep), plan.deep)]
 
 
 def weights_of(plan, level, sources):
@@ -87,64 +82,45 @@
 
 def forward_first(plan, *refs):
     level_size, pattern, factor, right, inverse = refs[:5]
-    out, near, rights, inverses, sizes, pats, wide, code, sems = refs[5:]
+    out, near, far, rights, inverses, sizes = refs[5:11]
+    pats, blocks, sides, diagonal, wide, sems = refs[11:]
     col = lax.axis_index("col")
-    pick = pltpu.make_async_copy(pattern, pats, sems.at[0])
-    learn = pltpu.make_async_copy(
-        level_size, sizes, sems.at[2 + 2 * plan.levels + len(plan.near)]
-    )
-    learn.start()
-    pick.start()
-
-    def pair(level, slot):
-        at = 1 + 2 * level
-        return [
-            pltpu.make_async_copy(inverse.at[slot], inverses.at[level], sems.at[at]),
-            pltpu.make_async_copy(
-                right.at[slot, col], rights.at[level], sems.at[at + 1]
-            ),
-        ]
-
-    small = pair(0, 0)
-    for c in small:
+    loads = [
+        (level_size, sizes),
+        (inverse, diagonal),
+        (right.at[:, col], sides),
+        (factor, blocks),
+        (pattern, pats),
+    ]
+    copies = [
+        pltpu.make_async_copy(source, target, sems.at[i])
+        for i, (source, target) in enumerate(loads)
+    ]
+    for c in copies:
         c.start()
     wide[...] = jnp.zeros(wide.shape, F32)
-    learn.wait()
+    copies[0].wait()
     slots = [locate(plan, k, sizes)[0] for k in range(plan.levels)]
-    large = [
-        pltpu.make_async_copy(
-            factor_row(plan, factor, k, sizes),
-            near.at[pl.ds(i * plan.deep, plan.deep)],
-            sems.at[1 + 2 * plan.levels + i],
-        )
-        for i, k in enumerate(plan.near)
-    ]
-    for c in large:
-        c.start()
-    for k in range(1, plan.levels):
-        more = pair(k, slots[k])
-        for c in more:
-            c.start()
-        small += more
-    pick.wait()
+    copies[1].wait()
+    copies[2].wait()
+    segment = lax.dot_general(
+        sides[0], diagonal[0], NT, preferred_element_type=F32
+    ).astype(BF16)
+    out[...] = jnp.broadcast_to(segment[None], out.shape)
+    for k in range(plan.levels):
+        rights[k] = sides[slots[k]]
+        inverses[k] = diagonal[slots[k]]
+    copies[3].wait()
+    copies[4].wait()
+    for target, levels in ((near, plan.near), (far, plan.far)):
+        for i, k in enumerate(levels):
+            at = pl.multiple_of(slots[k] * plan.deep, plan.deep)
+            target[pl.ds(i * plan.deep, plan.deep), :] = blocks[
+                pl.ds(at, plan.deep), :
+            ]
     for k in range(1, plan.levels):
         wide[pl.ds(k, 1), pl.ds(0, plan.entries)] = pats[slots[k]].astype(F32)
-    code[...] = wide[...].astype(BF16)
-    last = pltpu.make_async_copy(
-        code,
-        near.at[pl.ds(len(plan.near) * plan.deep, CODE_ROWS)],
-        sems.at[1 + 2 * plan.levels + len(plan.near)],
-    )
-    last.start()
-    small[0].wait()
-    small[1].wait()
-    segment = lax.dot_general(
-        rights[0], inverses[0], NT, preferred_element_type=F32
-    ).astype(BF16)
-    out[...] = jnp.broadcast_to(segment[None], out.shape)
-    for c in small[2:] + large:
-        c.wait()
-    last.wait()
+    near[pl.ds(len(plan.near) * plan.deep, CODE_ROWS), :] = wide[...].astype(BF16)
 
 
 def fill_table(plan, sizes, near, table):
@@ -179,29 +155,21 @@
     table[...] = jnp.where(row_level == TABLE_ROWS - 1, own_level, total)
 
 
+def after(far, segment, same):
+    pass
+
+
 def forward_second(plan, *refs):
-    sizes, factor, right, inverse, front = refs[:5]
-    near = refs[5 : 5 + plan.cols]
-    out, table, far, draft, store, sems = refs[5 + plan.cols :]
-    copies = [
-        pltpu.make_async_copy(
-            factor_row(plan, factor, k, sizes),
-            far.at[pl.ds(i * plan.deep, plan.deep)],
-            sems.at[1 + i],
-        )
-        for i, k in enumerate(plan.far)
-    ]
-    for c in copies:
-        c.start()
+    sizes, right, inverse, front = refs[:4]
+    near = refs[4 : 4 + plan.cols]
+    out, table, draft, store, sem = refs[4 + plan.cols :]
     fill_table(plan, sizes, near, draft)
-    copy = pltpu.make_async_copy(draft, table, sems.at[0])
+    copy = pltpu.make_async_copy(draft, table, sem)
     copy.start()
     gather_store(plan, 1, [front], store)
     copy.wait()
     segment = half_segment(plan, 1, table, right, inverse, near, store)
     out[...] = jnp.broadcast_to(segment[None], out.shape)
-    for c in copies:
-        c.wait()
 
 
 def forward_level(plan, level, *refs):
@@ -306,22 +274,26 @@
         ]
 
     factor = far_off(factor.reshape(rows * plan.entries * width, width))
-    first, own, rights, inverses, sizes = pl.pallas_call(
+    far_shape = pltpu.VMEM((len(plan.far) * plan.deep, width), BF16)
+    first, own, later, rights, inverses, sizes = pl.pallas_call(
         functools.partial(forward_first, plan),
         out_shape=(
             front_shape,
             pltpu.VMEM((len(plan.near) * plan.deep + CODE_ROWS, width), BF16),
+            far_shape,
             pltpu.VMEM((levels, share, width), BF16),
             pltpu.VMEM((levels, width, width), BF16),
             pltpu.SMEM((levels,), jnp.int32),
         ),
         in_specs=[hbm] * 5,
-        out_specs=(vmem,) * 4 + (smem,),
+        out_specs=(vmem,) * 5 + (smem,),
         scratch_shapes=[
             pltpu.VMEM((rows, 1, entries), jnp.int32),
+            pltpu.VMEM((rows * plan.deep, width), BF16),
+            pltpu.VMEM((rows, share, width), BF16),
+            pltpu.VMEM((rows, width, width), BF16),
             pltpu.VMEM((CODE_ROWS, width), F32),
-            pltpu.VMEM((CODE_ROWS, width), BF16),
-            pltpu.SemaphoreType.DMA((3 + 2 * levels + len(plan.near),)),
+            pltpu.SemaphoreType.DMA((5,)),
         ],
         compiler_params=params,
         name="forward_first",
@@ -335,26 +307,33 @@
     rights, inverses, sizes = held(rights), held(inverses), scalars(sizes)
     near = around(own)
     fronts = [exchange(first)]
-
-    mine, table, own = pl.pallas_call(
+    mine, table = pl.pallas_call(
         functools.partial(forward_second, plan),
         out_shape=(
             front_shape,
             pltpu.SMEM((TABLE_ROWS, width), jnp.int32),
-            pltpu.VMEM((len(plan.far) * plan.deep, width), BF16),
         ),
-        in_specs=[smem, hbm] + [vmem] * (3 + cols),
-        out_specs=(vmem, smem, vmem),
+        in_specs=[smem] + [vmem] * (3 + cols),
+        out_specs=(vmem, smem),
         scratch_shapes=[
             pltpu.VMEM((TABLE_ROWS, width), jnp.int32),
             store(1),
-            pltpu.SemaphoreType.DMA((1 + len(plan.far),)),
+            pltpu.SemaphoreType.DMA,
         ],
         compiler_params=params,
         name="forward_second",
-    )(sizes, factor, rights, inverses, fronts[0], *near)
+    )(sizes, rights, inverses, fronts[0], *near)
     table = scalars(table)
-    far = around(own)
+    later = pl.pallas_call(
+        after,
+        out_shape=far_shape,
+        in_specs=[vmem, vmem],
+        out_specs=vmem,
+        input_output_aliases={0: 0},
+        compiler_params=params,
+        name="after",
+    )(held(later), held(mine))
+    far = around(later)
     fronts.append(exchange(mine))
 
     def sources(level):

time: 187 us -> 186 us (level)
  no operation moved by 1% of the time
where the time goes in v7:
time: 186 us; the launch traced here: 185 us
  blocking collectives  168 us (90%)
  starting transfers between devices  8.75 us (5%)
  Pallas kernels  7.02 us (4%)
    all_to_all x10, blocking collectives, exchange(): return held(lax.all_to_all(x, 'chain', 0, 0, tiled=True))  160 us
    ppermute x6, starting transfers between devices, around(): lax.ppermute(x, 'col', [(i, i ^ s) for i in range(cols)])  8.75 us
    all_to_all x1, blocking collectives, per_device(): whole = lax.all_to_all(shares, 'col', 0, 0, tiled=True)  7.85 us
  transfers between devices with their start and end apart: 6, of which 0 were waited for; matrix products, arithmetic and copies ran while one was open for 0% of the time, Pallas kernels for 0%

profile of v7, /device:TPU:1, one launch (start us, length us, event | category | flops | bytes accessed | tf_op | source)
XLA Modules:
  0.0 185.2 jit_solution(17800466418452219945)
XLA Ops:
  0.6 1.3 forward_first.1
  2.0 3.7 %collective-permute-start.2 = (bf16[1552,128]{1,0:T(8,128)(2,1)S(1)}, bf16[1552,128]{1,0:T(8,128)(2,1)S(1)}, u32[]{:S(2)}, u32[]{:S(2)}) collective-permute-start(bf16[1552,128]{1,0:T(8,128)(2,1)S(1)} %get-tuple-element.29.refs_4_.refs_3_.refs_5_), channel_id=1, source_target_pairs={{0,2},{1,3},{2,0},{3,1},{4,6},{5,7},{6,4},{7,5},{8,10},{9,11},{10,... | collective-permute-start | bytes 1191944 | tf_op jit(solution)/shard_map/ppermute | solution.py:272
  5.6 0.9 collective-permute-start.1
  6.5 0.0 collective-permute-start
  6.5 23.8 %all_to_all.55.refs_3_.refs_7_ = bf16[64,8,128]{2,1,0:T(8,128)(2,1)S(1)} all-to-all(bf16[64,8,128]{2,1,0:T(8,128)(2,1)S(1)} %get-tuple-element.28), channel_id=1, replica_groups=mesh['chain'=64,'col'=4] {'chain'}, dimensions={0} | all-to-all | bytes 262144 | tf_op jit(solution)/shard_map/all_to_all | solution.py:268
  30.3 0.0 collective-permute-done.2.refs_7_.refs_6_.refs_8_
  30.3 0.0 collective-permute-done.1.refs_6_.refs_5_.refs_7_
  30.3 0.0 collective-permute-done.refs_5_.refs_4_.refs_6_
  30.3 1.2 forward_second.1
  31.6 3.4 %collective-permute-start.5 = (bf16[2304,128]{1,0:T(8,128)(2,1)S(1)}, bf16[2304,128]{1,0:T(8,128)(2,1)S(1)}, u32[]{:S(2)}, u32[]{:S(2)}) collective-permute-start(bf16[2304,128]{1,0:T(8,128)(2,1)S(1)} %after.1.refs_3_.refs_5_), channel_id=1, source_target_pairs={{0,2},{1,3},{2,0},{3,1},{4,6},{5,7},{6,4},{7,5},{8,10},{9,11},{10,... | collective-permute-start | bytes 1769480 | tf_op jit(solution)/shard_map/ppermute | solution.py:272
  34.9 0.9 collective-permute-start.4
  35.8 16.9 %all_to_all.56.refs_8_.refs_2_.refs_4_ = bf16[64,8,128]{2,1,0:T(8,128)(2,1)S(1)} all-to-all(bf16[64,8,128]{2,1,0:T(8,128)(2,1)S(1)} %get-tuple-element.31.segment), channel_id=1, replica_groups=mesh['chain'=64,'col'=4] {'chain'}, dimensions={0} | all-to-all | bytes 262144 | tf_op jit(solution)/shard_map/all_to_all | solution.py:268
  52.7 0.5 forward_level_2.1
  53.1 14.9 %all_to_all.57.refs_9_.refs_2_.refs_5_ = bf16[64,8,128]{2,1,0:T(8,128)(2,1)S(1)} all-to-all(bf16[64,8,128]{2,1,0:T(8,128)(2,1)S(1)} %forward_level_2.1), channel_id=1, replica_groups=mesh['chain'=64,'col'=4] {'chain'}, dimensions={0} | all-to-all | bytes 262144 | tf_op jit(solution)/shard_map/all_to_all | solution.py:268
  68.1 0.0 collective-permute-done.3.refs_4_.refs_6_
  68.1 0.5 forward_level_3.1
  68.6 14.9 %all_to_all.58.refs_10_.refs_2_.refs_6_ = bf16[64,8,128]{2,1,0:T(8,128)(2,1)S(1)} all-to-all(bf16[64,8,128]{2,1,0:T(8,128)(2,1)S(1)} %forward_level_3.1), channel_id=1, replica_groups=mesh['chain'=64,'col'=4] {'chain'}, dimensions={0} | all-to-all | bytes 262144 | tf_op jit(solution)/shard_map/all_to_all | solution.py:268
  83.5 0.5 forward_level_4.1
  84.0 14.9 %all_to_all.59.refs_11_.refs_2_.refs_7_ = bf16[64,8,128]{2,1,0:T(8,128)(2,1)S(1)} all-to-all(bf16[64,8,128]{2,1,0:T(8,128)(2,1)S(1)} %forward_level_4.1), channel_id=1, replica_groups=mesh['chain'=64,'col'=4] {'chain'}, dimensions={0} | all-to-all | bytes 262144 | tf_op jit(solution)/shard_map/all_to_all | solution.py:268
  98.9 1.0 turn_level.1
  100.0 14.9 %all_to_all.60.refs_3_ = bf16[64,8,128]{2,1,0:T(8,128)(2,1)S(1)} all-to-all(bf16[64,8,128]{2,1,0:T(8,128)(2,1)S(1)} %get-tuple-element.33), channel_id=1, replica_groups=mesh['chain'=64,'col'=4] {'chain'}, dimensions={0} | all-to-all | bytes 262144 | tf_op jit(solution)/shard_map/all_to_all | solution.py:268
  114.9 0.4 backward_level_4.1
  115.3 14.9 %all_to_all.61.refs_3_ = bf16[64,8,128]{2,1,0:T(8,128)(2,1)S(1)} all-to-all(bf16[64,8,128]{2,1,0:T(8,128)(2,1)S(1)} %get-tuple-element.35), channel_id=1, replica_groups=mesh['chain'=64,'col'=4] {'chain'}, dimensions={0} | all-to-all | bytes 262144 | tf_op jit(solution)/shard_map/all_to_all | solution.py:268
  130.2 0.5 backward_level_3.1
  130.7 15.1 %all_to_all.62.refs_3_ = bf16[64,8,128]{2,1,0:T(8,128)(2,1)S(1)} all-to-all(bf16[64,8,128]{2,1,0:T(8,128)(2,1)S(1)} %get-tuple-element.37), channel_id=1, replica_groups=mesh['chain'=64,'col'=4] {'chain'}, dimensions={0} | all-to-all | bytes 262144 | tf_op jit(solution)/shard_map/all_to_all | solution.py:268
  145.8 0.4 backward_level_2.1
  146.2 14.9 %all_to_all.63.refs_3_ = bf16[64,8,128]{2,1,0:T(8,128)(2,1)S(1)} all-to-all(bf16[64,8,128]{2,1,0:T(8,128)(2,1)S(1)} %get-tuple-element.39), channel_id=1, replica_groups=mesh['chain'=64,'col'=4] {'chain'}, dimensions={0} | all-to-all | bytes 262144 | tf_op jit(solution)/shard_map/all_to_all | solution.py:268
  161.1 0.4 backward_level_1.1
  161.6 15.0 %all_to_all.64.refs_2_ = bf16[64,8,128]{2,1,0:T(8,128)(2,1)S(1)} all-to-all(bf16[64,8,128]{2,1,0:T(8,128)(2,1)S(1)} %get-tuple-element.41), channel_id=1, replica_groups=mesh['chain'=64,'col'=4] {'chain'}, dimensions={0} | all-to-all | bytes 262144 | tf_op jit(solution)/shard_map/all_to_all | solution.py:268
  176.5 0.2 finish.1
  176.7 7.8 %all_to_all.65 = bf16[4,8,8,128]{3,2,1,0:T(8,128)(2,1)S(1)} all-to-all(bf16[4,8,8,128]{3,2,1,0:T(8,128)(2,1)S(1)} %finish.1), channel_id=1, replica_groups=mesh['chain'=64,'col'=4] {'col'}, dimensions={0} | all-to-all | bytes 131072 | tf_op jit(solution)/shard_map/all_to_all | solution.py:396
  184.6 0.6 copy_bitcast_fusion
  (5 shorter events, 0.0 us)
Async XLA Ops:
  2.0 28.3 %collective-permute-start.2 = (bf16[1552,128]{1,0:T(8,128)(2,1)S(1)}, bf16[1552,128]{1,0:T(8,128)(2,1)S(1)}, u32[]{:S(2)}, u32[]{:S(2)}) collective-permute-start(bf16[1552,128]{1,0:T(8,128)(2,1)S(1)} %get-tuple-element.29.refs_4_.refs_3_.refs_5_), channel_id=1, source_target_pairs={{0,2},{1,3},{2,0},{3,1},{4,6},{5,7},{6,4},{7,5},{8,10},{9,11},{10,... | collective-permute-start | bytes 1191944 | tf_op jit(solution)/shard_map/ppermute | solution.py:272
  5.6 24.7 %collective-permute-start.1 = (bf16[1552,128]{1,0:T(8,128)(2,1)S(1)}, bf16[1552,128]{1,0:T(8,128)(2,1)S(1)}, u32[]{:S(2)}, u32[]{:S(2)}) collective-permute-start(bf16[1552,128]{1,0:T(8,128)(2,1)S(1)} %get-tuple-element.29.refs_4_.refs_3_.refs_5_), channel_id=1, source_target_pairs={{0,3},{1,2},{2,1},{3,0},{4,7},{5,6},{6,5},{7,4},{8,11},{9,10},{10,... | collective-permute-start | bytes 1191944 | tf_op jit(solution)/shard_map/ppermute | solution.py:272
  6.5 23.8 %collective-permute-start = (bf16[1552,128]{1,0:T(8,128)(2,1)S(1)}, bf16[1552,128]{1,0:T(8,128)(2,1)S(1)}, u32[]{:S(2)}, u32[]{:S(2)}) collective-permute-start(bf16[1552,128]{1,0:T(8,128)(2,1)S(1)} %get-tuple-element.29.refs_4_.refs_3_.refs_5_), channel_id=1, source_target_pairs={{0,1},{1,0},{2,3},{3,2},{4,5},{5,4},{6,7},{7,6},{8,9},{9,8},{10,11... | collective-permute-start | bytes 1191944 | tf_op jit(solution)/shard_map/ppermute | solution.py:272
  31.6 36.5 %collective-permute-start.5 = (bf16[2304,128]{1,0:T(8,128)(2,1)S(1)}, bf16[2304,128]{1,0:T(8,128)(2,1)S(1)}, u32[]{:S(2)}, u32[]{:S(2)}) collective-permute-start(bf16[2304,128]{1,0:T(8,128)(2,1)S(1)} %after.1.refs_3_.refs_5_), channel_id=1, source_target_pairs={{0,2},{1,3},{2,0},{3,1},{4,6},{5,7},{6,4},{7,5},{8,10},{9,11},{10,... | collective-permute-start | bytes 1769480 | tf_op jit(solution)/shard_map/ppermute | solution.py:272
  34.9 33.2 %collective-permute-start.4 = (bf16[2304,128]{1,0:T(8,128)(2,1)S(1)}, bf16[2304,128]{1,0:T(8,128)(2,1)S(1)}, u32[]{:S(2)}, u32[]{:S(2)}) collective-permute-start(bf16[2304,128]{1,0:T(8,128)(2,1)S(1)} %after.1.refs_3_.refs_5_), channel_id=1, source_target_pairs={{0,3},{1,2},{2,1},{3,0},{4,7},{5,6},{6,5},{7,4},{8,11},{9,10},{10,... | collective-permute-start | bytes 1769480 | tf_op jit(solution)/shard_map/ppermute | solution.py:272
  35.8 32.3 %collective-permute-start.3 = (bf16[2304,128]{1,0:T(8,128)(2,1)S(1)}, bf16[2304,128]{1,0:T(8,128)(2,1)S(1)}, u32[]{:S(2)}, u32[]{:S(2)}) collective-permute-start(bf16[2304,128]{1,0:T(8,128)(2,1)S(1)} %after.1.refs_3_.refs_5_), channel_id=1, source_target_pairs={{0,1},{1,0},{2,3},{3,2},{4,5},{5,4},{6,7},{7,6},{8,9},{9,8},{10,11... | collective-permute-start | bytes 1769480 | tf_op jit(solution)/shard_map/ppermute | solution.py:272

commit v8 on v7

--- a/solution.py
+++ b/solution.py
@@ -12,6 +12,7 @@
 NN = (((1,), (0,)), ((), ()))
 CODE_ROWS = 16
 TABLE_ROWS = 8
+PAIR = 2
 
 
 class Plan:
@@ -58,8 +59,9 @@
 
 
 def gather_store(plan, level, earlier, store):
-    for k in range(level):
-        store[pl.ds(k * plan.lanes, plan.lanes)] = earlier[k][...]
+    part = plan.lanes // PAIR
+    for k in range(PAIR * level):
+        store[pl.ds(k * part, part)] = earlier[k][...]
     store[level * plan.lanes] = jnp.zeros(store.shape[1:], BF16)
 
 
@@ -78,6 +80,14 @@
     terms = lax.dot_general(segment, weights, NN, preferred_element_type=F32)
     for j, at in enumerate(places_of(plan, level, table)):
         acc[at] = acc[at] + terms[:, j * plan.width : (j + 1) * plan.width]
+
+
+def give_terms(plan, level, acc, out):
+    core = lax.rem(lax.axis_index("chain"), PAIR)
+    part = plan.lanes // PAIR
+    for i in range(PAIR):
+        at = level * plan.lanes + i * part
+        out[:, core ^ i] = acc[pl.ds(at, part)].astype(BF16)
 
 
 def forward_first(plan, *refs):
@@ -124,6 +134,7 @@
 
 
 def fill_table(plan, sizes, near, table):
+    core = lax.rem(lax.axis_index("chain"), PAIR)
     split = len(plan.near) * plan.deep
     shape = (TABLE_ROWS, plan.width)
     row_level = lax.broadcasted_iota(jnp.int32, shape, 0)
@@ -141,9 +152,12 @@
         level = jnp.zeros(shape, jnp.int32)
         for end in ends:
             level = level + (columns >= end).astype(jnp.int32)
+        there = lax.rem(columns, plan.lanes)
+        apart = lax.rem(there, PAIR) ^ core
+        there = apart * (plan.lanes // PAIR) + there // PAIR
         place = jnp.where(
             (level < row_level) & (alive > 0),
-            level * plan.lanes + lax.rem(columns, plan.lanes),
+            level * plan.lanes + there,
             row_level * plan.lanes,
         )
         place = jnp.where(entry < plan.entries, place, 0)
@@ -160,13 +174,14 @@
 
 
 def forward_second(plan, *refs):
-    sizes, right, inverse, front = refs[:4]
-    near = refs[4 : 4 + plan.cols]
-    out, table, draft, store, sem = refs[4 + plan.cols :]
+    sizes, right, inverse = refs[:3]
+    fronts = refs[3 : 3 + PAIR]
+    near = refs[3 + PAIR : 3 + PAIR + plan.cols]
+    out, table, draft, store, sem = refs[3 + PAIR + plan.cols :]
     fill_table(plan, sizes, near, draft)
     copy = pltpu.make_async_copy(draft, table, sem)
     copy.start()
-    gather_store(plan, 1, [front], store)
+    gather_store(plan, 1, fronts, store)
     copy.wait()
     segment = half_segment(plan, 1, table, right, inverse, near, store)
     out[...] = jnp.broadcast_to(segment[None], out.shape)
@@ -175,8 +190,8 @@
 def forward_level(plan, level, *refs):
     table, right, inverse = refs[:3]
     sources = refs[3 : 3 + plan.cols]
-    earlier = refs[3 + plan.cols : 3 + plan.cols + level]
-    out, store = refs[3 + plan.cols + level :]
+    earlier = refs[3 + plan.cols : 3 + plan.cols + PAIR * level]
+    out, store = refs[3 + plan.cols + PAIR * level :]
     gather_store(plan, level, earlier, store)
     segment = half_segment(plan, level, table, right, inverse, sources, store)
     out[...] = jnp.broadcast_to(segment[None], out.shape)
@@ -185,8 +200,8 @@
 def turn_level(plan, level, *refs):
     table, right, inverse = refs[:3]
     sources = refs[3 : 3 + plan.cols]
-    earlier = refs[3 + plan.cols : 3 + plan.cols + level]
-    half, solved, acc, out, store = refs[3 + plan.cols + level :]
+    earlier = refs[3 + plan.cols : 3 + plan.cols + PAIR * level]
+    half, solved, acc, out, store = refs[3 + plan.cols + PAIR * level :]
     gather_store(plan, level, earlier, store)
     acc[...] = jnp.zeros(acc.shape, F32)
     segment = half_segment(plan, level, table, right, inverse, sources, store)
@@ -196,7 +211,7 @@
     ).astype(BF16)
     solved[...] = segment
     add_terms(plan, level, table, segment, sources, acc)
-    out[...] = acc[pl.ds((level - 1) * plan.lanes, plan.lanes)].astype(BF16)
+    give_terms(plan, level - 1, acc, out)
 
 
 def solve_back(half, inverse, arrived):
@@ -209,10 +224,10 @@
     table, inverse, front, arrived, _ = refs[:5]
     sources = refs[5 : 5 + plan.cols]
     solved, acc, out = refs[5 + plan.cols :]
-    segment = solve_back(front[lax.axis_index("chain")], inverse[level], arrived)
+    segment = solve_back(front[lax.axis_index("chain") // PAIR], inverse[level], arrived)
     solved[...] = segment
     add_terms(plan, level, table, segment, sources, acc)
-    out[...] = acc[pl.ds((level - 1) * plan.lanes, plan.lanes)].astype(BF16)
+    give_terms(plan, level - 1, acc, out)
 
 
 def finish(plan, *refs):
@@ -224,7 +239,7 @@
     out, hbuf, sbuf = refs[2 + 2 * levels :]
     lane = lax.axis_index("chain")
     for k in range(levels - 1):
-        hbuf[k] = fronts[k][lane]
+        hbuf[k] = fronts[k][lane // PAIR]
         sbuf[k + 1] = done[k][...]
     hbuf[levels - 1] = half_last[...]
     sbuf[0] = solve_back(hbuf[0], inverse[0], arrived)
@@ -249,7 +264,8 @@
     hbm = pl.BlockSpec(memory_space=pltpu.HBM)
     vmem = pl.BlockSpec(memory_space=pltpu.VMEM)
     segment_shape = pltpu.VMEM((share, width), BF16)
-    front_shape = pltpu.VMEM((lanes, share, width), BF16)
+    front_shape = pltpu.VMEM((lanes // PAIR, share, width), BF16)
+    terms_shape = pltpu.VMEM((lanes // PAIR, PAIR, share, width), BF16)
     params = pltpu.CompilerParams(vmem_limit_bytes=12 * 1024 * 1024)
 
     def far_off(x):
@@ -265,6 +281,13 @@
         return pltpu.VMEM((level * lanes + 1, share, width), BF16)
 
     def exchange(x):
+        groups = [list(range(i, lanes, PAIR)) for i in range(PAIR)]
+        own = lax.all_to_all(x, "chain", 0, 0, tiled=True, axis_index_groups=groups)
+        other = lax.ppermute(own, "chain", [(i, i ^ 1) for i in range(lanes)])
+        return [held(own), held(other)]
+
+    def exchange_back(x):
+        x = x.reshape(lanes, share, width)
         return held(lax.all_to_all(x, "chain", 0, 0, tiled=True))
 
     def around(x):
@@ -306,14 +329,14 @@
     )
     rights, inverses, sizes = held(rights), held(inverses), scalars(sizes)
     near = around(own)
-    fronts = [exchange(first)]
+    fronts = exchange(first)
     mine, table = pl.pallas_call(
         functools.partial(forward_second, plan),
         out_shape=(
             front_shape,
             pltpu.SMEM((TABLE_ROWS, width), jnp.int32),
         ),
-        in_specs=[smem] + [vmem] * (3 + cols),
+        in_specs=[smem] + [vmem] * (2 + PAIR + cols),
         out_specs=(vmem, smem),
         scratch_shapes=[
             pltpu.VMEM((TABLE_ROWS, width), jnp.int32),
@@ -322,7 +345,7 @@
         ],
         compiler_params=params,
         name="forward_second",
-    )(sizes, rights, inverses, fronts[0], *near)
+    )(sizes, rights, inverses, *fronts, *near)
     table = scalars(table)
     later = pl.pallas_call(
         after,
@@ -334,7 +357,7 @@
         name="after",
     )(held(later), held(mine))
     far = around(later)
-    fronts.append(exchange(mine))
+    fronts += exchange(mine)
 
     def sources(level):
         return near if level in plan.near else far
@@ -343,20 +366,20 @@
         mine = pl.pallas_call(
             functools.partial(forward_level, plan, k),
             out_shape=front_shape,
-            in_specs=[smem] + [vmem] * (2 + cols + k),
+            in_specs=[smem] + [vmem] * (2 + cols + PAIR * k),
             out_specs=vmem,
             scratch_shapes=[store(k)],
             compiler_params=params,
             name=f"forward_level_{k}",
         )(table, rights, inverses, *sources(k), *fronts)
-        fronts.append(exchange(mine))
+        fronts += exchange(mine)
 
     last = levels - 1
     acc_shape = pltpu.VMEM((last * lanes + 1, share, width), F32)
     half_last, solved, acc, terms = pl.pallas_call(
         functools.partial(turn_level, plan, last),
-        out_shape=(segment_shape, segment_shape, acc_shape, front_shape),
-        in_specs=[smem] + [vmem] * (2 + cols + last),
+        out_shape=(segment_shape, segment_shape, acc_shape, terms_shape),
+        in_specs=[smem] + [vmem] * (2 + cols + PAIR * last),
         out_specs=(vmem,) * 4,
         scratch_shapes=[store(last)],
         compiler_params=params,
@@ -366,7 +389,7 @@
     for k in range(last - 1, 0, -1):
         solved, acc, terms = pl.pallas_call(
             functools.partial(backward_level, plan, k),
-            out_shape=(segment_shape, acc_shape, front_shape),
+            out_shape=(segment_shape, acc_shape, terms_shape),
             in_specs=[smem] + [vmem] * (4 + cols),
             out_specs=(vmem,) * 3,
             input_output_aliases={4: 1},
@@ -375,8 +398,8 @@
         )(
             table,
             inverses,
-            fronts[k],
-            exchange(terms),
+            fronts[PAIR * k],
+            exchange_back(terms),
             held(acc),
             *sources(k),
         )
@@ -392,7 +415,7 @@
         ],
         compiler_params=params,
         name="finish",
-    )(table, inverses, exchange(terms), *fronts, held(half_last), *done)
+    )(table, inverses, exchange_back(terms), *fronts[::PAIR], held(half_last), *done)
     whole = lax.all_to_all(shares, "col", 0, 0, tiled=True)
     whole = whole.transpose(1, 0, 2, 3).reshape(2, rows, 1, probes, width)
     return whole[0], whole[1]

time: 186 us -> 184 us (0.989)
  blocking collectives: 168 us -> 152 us
  starting transfers between devices: 8.75 us -> 18.7 us
  waiting for transfers between devices: 0.02 us -> 4.53 us
    all_to_all x10, blocking collectives: 160 us -> 144 us  [the longest x5 74.8 us: exchange_back(): return held(lax.all_to_all(x, 'chain', 0, 0, tiled=True))]
    ppermute x0 -> x5, starting transfers between devices: none -> 9.98 us  [exchange(): other = lax.ppermute(own, 'chain', [(i, i ^ 1) for i in range(lanes)])]
    ppermute x0 -> x5, waiting for transfers between devices: none -> 4.51 us  [exchange(): other = lax.ppermute(own, 'chain', [(i, i ^ 1) for i in range(lanes)])]
  transfers between devices with their start and end apart: 6 -> 11, of which waited for: 0 -> 5; matrix products, arithmetic and copies ran while one was open for 0% -> 0% of each run, Pallas kernels for 0% -> 0%
where the time goes in v8:
time: 184 us; the launch traced here: 183 us
  blocking collectives  152 us (83%)
  starting transfers between devices  18.7 us (10%)
  Pallas kernels  6.83 us (4%)
  waiting for transfers between devices  4.53 us (2%)
    all_to_all x5, blocking collectives, exchange_back(): return held(lax.all_to_all(x, 'chain', 0, 0, tiled=True))  74.8 us
    all_to_all x5, blocking collectives, exchange(): own = lax.all_to_all(x, 'chain', 0, 0, tiled=True, axis_index_groups=groups)  69 us
    ppermute x5, starting transfers between devices, exchange(): other = lax.ppermute(own, 'chain', [(i, i ^ 1) for i in range(lanes)])  9.98 us
    ppermute x6, starting transfers between devices, around(): lax.ppermute(x, 'col', [(i, i ^ s) for i in range(cols)])  8.73 us
    all_to_all x1, blocking collectives, per_device(): whole = lax.all_to_all(shares, 'col', 0, 0, tiled=True)  7.81 us
    ppermute x5, waiting for transfers between devices, exchange(): other = lax.ppermute(own, 'chain', [(i, i ^ 1) for i in range(lanes)])  4.51 us
  transfers between devices with their start and end apart: 11, of which 5 were waited for; matrix products, arithmetic and copies ran while one was open for 0% of the time, Pallas kernels for 0%

profile of v8, /device:TPU:1, one launch (start us, length us, event | category | flops | bytes accessed | tf_op | source)
XLA Modules:
  0.0 183.0 jit_solution(16773532954094896094)
XLA Ops:
  0.6 1.3 forward_first.1
  2.0 3.7 %collective-permute-start.3 = (bf16[1552,128]{1,0:T(8,128)(2,1)S(1)}, bf16[1552,128]{1,0:T(8,128)(2,1)S(1)}, u32[]{:S(2)}, u32[]{:S(2)}) collective-permute-start(bf16[1552,128]{1,0:T(8,128)(2,1)S(1)} %get-tuple-element.29.refs_5_.refs_3_), channel_id=1, source_target_pairs={{0,2},{1,3},{2,0},{3,1},{4,6},{5,7},{6,4},{7,5},{8,10},{9,11},{10,... | collective-permute-start | bytes 1191944 | tf_op jit(solution)/shard_map/ppermute | solution.py:295
  5.6 0.9 collective-permute-start.2
  6.5 19.8 %all_to_all.55.refs_3_.refs_7_ = bf16[32,8,128]{2,1,0:T(8,128)(2,1)S(1)} all-to-all(bf16[32,8,128]{2,1,0:T(8,128)(2,1)S(1)} %get-tuple-element.28), channel_id=1, replica_groups={{0,8,16,24,32,40,48,56,64,72,80,88,96,104,112,120,128,136,144,152,160,1..., dimensions={0} | all-to-all | bytes 131072 | tf_op jit(solution)/shard_map/all_to_all | solution.py:285
  26.3 2.7 %collective-permute-start = (bf16[32,8,128]{2,1,0:T(8,128)(2,1)S(1)}, bf16[32,8,128]{2,1,0:T(8,128)(2,1)S(1)}, u32[]{:S(2)}, u32[]{:S(2)}) collective-permute-start(bf16[32,8,128]{2,1,0:T(8,128)(2,1)S(1)} %all_to_all.55.refs_3_.refs_7_), channel_id=1, source_target_pairs={{0,4},{4,0},{8,12},{12,8},{16,20},{20,16},{24,28},{28,24},{32,36},... | collective-permute-start | bytes 196616 | tf_op jit(solution)/shard_map/ppermute | solution.py:286
  29.0 0.9 collective-permute-done.refs_4_.refs_8_
  29.9 1.2 forward_second.1
  31.2 3.3 %collective-permute-start.7 = (bf16[2304,128]{1,0:T(8,128)(2,1)S(1)}, bf16[2304,128]{1,0:T(8,128)(2,1)S(1)}, u32[]{:S(2)}, u32[]{:S(2)}) collective-permute-start(bf16[2304,128]{1,0:T(8,128)(2,1)S(1)} %after.1.refs_3_.refs_5_), channel_id=1, source_target_pairs={{0,2},{1,3},{2,0},{3,1},{4,6},{5,7},{6,4},{7,5},{8,10},{9,11},{10,... | collective-permute-start | bytes 1769480 | tf_op jit(solution)/shard_map/ppermute | solution.py:295
  34.5 0.9 collective-permute-start.6
  35.4 13.5 %all_to_all.56.refs_9_.refs_2_.refs_4_ = bf16[32,8,128]{2,1,0:T(8,128)(2,1)S(1)} all-to-all(bf16[32,8,128]{2,1,0:T(8,128)(2,1)S(1)} %get-tuple-element.31.segment), channel_id=1, replica_groups={{0,8,16,24,32,40,48,56,64,72,80,88,96,104,112,120,128,136,144,152,160,1..., dimensions={0} | all-to-all | bytes 131072 | tf_op jit(solution)/shard_map/all_to_all | solution.py:285
  48.8 2.5 %collective-permute-start.4 = (bf16[32,8,128]{2,1,0:T(8,128)(2,1)S(1)}, bf16[32,8,128]{2,1,0:T(8,128)(2,1)S(1)}, u32[]{:S(2)}, u32[]{:S(2)}) collective-permute-start(bf16[32,8,128]{2,1,0:T(8,128)(2,1)S(1)} %all_to_all.56.refs_9_.refs_2_.refs_4_), channel_id=1, source_target_pairs={{0,4},{4,0},{8,12},{12,8},{16,20},{20,16},{24,28},{28,24},{32,36},... | collective-permute-start | bytes 196616 | tf_op jit(solution)/shard_map/ppermute | solution.py:286
  51.4 0.9 collective-permute-done.4.refs_10_
  52.7 11.9 %all_to_all.57.refs_11_.refs_2_.refs_5_ = bf16[32,8,128]{2,1,0:T(8,128)(2,1)S(1)} all-to-all(bf16[32,8,128]{2,1,0:T(8,128)(2,1)S(1)} %forward_level_2.1), channel_id=1, replica_groups={{0,8,16,24,32,40,48,56,64,72,80,88,96,104,112,120,128,136,144,152,160,1..., dimensions={0} | all-to-all | bytes 131072 | tf_op jit(solution)/shard_map/all_to_all | solution.py:285
  64.6 1.6 collective-permute-start.8
  66.1 0.9 collective-permute-done.8.refs_12_
  67.5 11.9 %all_to_all.58.refs_13_.refs_2_.refs_6_ = bf16[32,8,128]{2,1,0:T(8,128)(2,1)S(1)} all-to-all(bf16[32,8,128]{2,1,0:T(8,128)(2,1)S(1)} %forward_level_3.1), channel_id=1, replica_groups={{0,8,16,24,32,40,48,56,64,72,80,88,96,104,112,120,128,136,144,152,160,1..., dimensions={0} | all-to-all | bytes 131072 | tf_op jit(solution)/shard_map/all_to_all | solution.py:285
  79.4 1.6 collective-permute-start.9
  81.0 0.9 collective-permute-done.9.refs_14_
  82.3 11.9 %all_to_all.59.refs_15_.refs_2_.refs_7_ = bf16[32,8,128]{2,1,0:T(8,128)(2,1)S(1)} all-to-all(bf16[32,8,128]{2,1,0:T(8,128)(2,1)S(1)} %forward_level_4.1), channel_id=1, replica_groups={{0,8,16,24,32,40,48,56,64,72,80,88,96,104,112,120,128,136,144,152,160,1..., dimensions={0} | all-to-all | bytes 131072 | tf_op jit(solution)/shard_map/all_to_all | solution.py:285
  94.2 1.6 collective-permute-start.10
  95.8 0.9 collective-permute-done.10.refs_16_
  96.7 1.0 turn_level.1
  97.8 14.9 %all_to_all.60.refs_3_ = bf16[64,8,128]{2,1,0:T(8,128)(2,1)S(1)} all-to-all(bf16[64,8,128]{2,1,0:T(8,128)(2,1)S(1)} %bitcast.17), channel_id=1, replica_groups=mesh['chain'=64,'col'=4] {'chain'}, dimensions={0} | all-to-all | bytes 262144 | tf_op jit(solution)/shard_map/all_to_all | solution.py:291
  113.1 14.9 %all_to_all.61.refs_3_ = bf16[64,8,128]{2,1,0:T(8,128)(2,1)S(1)} all-to-all(bf16[64,8,128]{2,1,0:T(8,128)(2,1)S(1)} %bitcast.20), channel_id=1, replica_groups=mesh['chain'=64,'col'=4] {'chain'}, dimensions={0} | all-to-all | bytes 262144 | tf_op jit(solution)/shard_map/all_to_all | solution.py:291
  128.1 0.5 backward_level_3.1
  128.5 15.1 %all_to_all.62.refs_3_ = bf16[64,8,128]{2,1,0:T(8,128)(2,1)S(1)} all-to-all(bf16[64,8,128]{2,1,0:T(8,128)(2,1)S(1)} %bitcast.18), channel_id=1, replica_groups=mesh['chain'=64,'col'=4] {'chain'}, dimensions={0} | all-to-all | bytes 262144 | tf_op jit(solution)/shard_map/all_to_all | solution.py:291
  143.6 0.4 backward_level_2.1
  144.0 14.9 %all_to_all.63.refs_3_ = bf16[64,8,128]{2,1,0:T(8,128)(2,1)S(1)} all-to-all(bf16[64,8,128]{2,1,0:T(8,128)(2,1)S(1)} %bitcast.21), channel_id=1, replica_groups=mesh['chain'=64,'col'=4] {'chain'}, dimensions={0} | all-to-all | bytes 262144 | tf_op jit(solution)/shard_map/all_to_all | solution.py:291
  159.0 0.5 backward_level_1.1
  159.4 14.9 %all_to_all.64.refs_2_ = bf16[64,8,128]{2,1,0:T(8,128)(2,1)S(1)} all-to-all(bf16[64,8,128]{2,1,0:T(8,128)(2,1)S(1)} %bitcast.19), channel_id=1, replica_groups=mesh['chain'=64,'col'=4] {'chain'}, dimensions={0} | all-to-all | bytes 262144 | tf_op jit(solution)/shard_map/all_to_all | solution.py:291
  174.5 7.8 %all_to_all.65 = bf16[4,8,8,128]{3,2,1,0:T(8,128)(2,1)S(1)} all-to-all(bf16[4,8,8,128]{3,2,1,0:T(8,128)(2,1)S(1)} %finish.1), channel_id=1, replica_groups=mesh['chain'=64,'col'=4] {'col'}, dimensions={0} | all-to-all | bytes 131072 | tf_op jit(solution)/shard_map/all_to_all | solution.py:419
  182.4 0.6 copy_bitcast_fusion
  (15 shorter events, 1.9 us)
Async XLA Ops:
  2.0 27.9 %collective-permute-start.3 = (bf16[1552,128]{1,0:T(8,128)(2,1)S(1)}, bf16[1552,128]{1,0:T(8,128)(2,1)S(1)}, u32[]{:S(2)}, u32[]{:S(2)}) collective-permute-start(bf16[1552,128]{1,0:T(8,128)(2,1)S(1)} %get-tuple-element.29.refs_5_.refs_3_), channel_id=1, source_target_pairs={{0,2},{1,3},{2,0},{3,1},{4,6},{5,7},{6,4},{7,5},{8,10},{9,11},{10,... | collective-permute-start | bytes 1191944 | tf_op jit(solution)/shard_map/ppermute | solution.py:295
  5.6 24.3 %collective-permute-start.2 = (bf16[1552,128]{1,0:T(8,128)(2,1)S(1)}, bf16[1552,128]{1,0:T(8,128)(2,1)S(1)}, u32[]{:S(2)}, u32[]{:S(2)}) collective-permute-start(bf16[1552,128]{1,0:T(8,128)(2,1)S(1)} %get-tuple-element.29.refs_5_.refs_3_), channel_id=1, source_target_pairs={{0,3},{1,2},{2,1},{3,0},{4,7},{5,6},{6,5},{7,4},{8,11},{9,10},{10,... | collective-permute-start | bytes 1191944 | tf_op jit(solution)/shard_map/ppermute | solution.py:295
  6.5 23.4 %collective-permute-start.1 = (bf16[1552,128]{1,0:T(8,128)(2,1)S(1)}, bf16[1552,128]{1,0:T(8,128)(2,1)S(1)}, u32[]{:S(2)}, u32[]{:S(2)}) collective-permute-start(bf16[1552,128]{1,0:T(8,128)(2,1)S(1)} %get-tuple-element.29.refs_5_.refs_3_), channel_id=1, source_target_pairs={{0,1},{1,0},{2,3},{3,2},{4,5},{5,4},{6,7},{7,6},{8,9},{9,8},{10,11... | collective-permute-start | bytes 1191944 | tf_op jit(solution)/shard_map/ppermute | solution.py:295
  26.3 3.6 %collective-permute-start = (bf16[32,8,128]{2,1,0:T(8,128)(2,1)S(1)}, bf16[32,8,128]{2,1,0:T(8,128)(2,1)S(1)}, u32[]{:S(2)}, u32[]{:S(2)}) collective-permute-start(bf16[32,8,128]{2,1,0:T(8,128)(2,1)S(1)} %all_to_all.55.refs_3_.refs_7_), channel_id=1, source_target_pairs={{0,4},{4,0},{8,12},{12,8},{16,20},{20,16},{24,28},{28,24},{32,36},... | collective-permute-start | bytes 196616 | tf_op jit(solution)/shard_map/ppermute | solution.py:286
  31.2 35.9 %collective-permute-start.7 = (bf16[2304,128]{1,0:T(8,128)(2,1)S(1)}, bf16[2304,128]{1,0:T(8,128)(2,1)S(1)}, u32[]{:S(2)}, u32[]{:S(2)}) collective-permute-start(bf16[2304,128]{1,0:T(8,128)(2,1)S(1)} %after.1.refs_3_.refs_5_), channel_id=1, source_target_pairs={{0,2},{1,3},{2,0},{3,1},{4,6},{5,7},{6,4},{7,5},{8,10},{9,11},{10,... | collective-permute-start | bytes 1769480 | tf_op jit(solution)/shard_map/ppermute | solution.py:295
  34.5 32.5 %collective-permute-start.6 = (bf16[2304,128]{1,0:T(8,128)(2,1)S(1)}, bf16[2304,128]{1,0:T(8,128)(2,1)S(1)}, u32[]{:S(2)}, u32[]{:S(2)}) collective-permute-start(bf16[2304,128]{1,0:T(8,128)(2,1)S(1)} %after.1.refs_3_.refs_5_), channel_id=1, source_target_pairs={{0,3},{1,2},{2,1},{3,0},{4,7},{5,6},{6,5},{7,4},{8,11},{9,10},{10,... | collective-permute-start | bytes 1769480 | tf_op jit(solution)/shard_map/ppermute | solution.py:295
  35.4 31.7 %collective-permute-start.5 = (bf16[2304,128]{1,0:T(8,128)(2,1)S(1)}, bf16[2304,128]{1,0:T(8,128)(2,1)S(1)}, u32[]{:S(2)}, u32[]{:S(2)}) collective-permute-start(bf16[2304,128]{1,0:T(8,128)(2,1)S(1)} %after.1.refs_3_.refs_5_), channel_id=1, source_target_pairs={{0,1},{1,0},{2,3},{3,2},{4,5},{5,4},{6,7},{7,6},{8,9},{9,8},{10,11... | collective-permute-start | bytes 1769480 | tf_op jit(solution)/shard_map/ppermute | solution.py:295
  48.8 3.4 %collective-permute-start.4 = (bf16[32,8,128]{2,1,0:T(8,128)(2,1)S(1)}, bf16[32,8,128]{2,1,0:T(8,128)(2,1)S(1)}, u32[]{:S(2)}, u32[]{:S(2)}) collective-permute-start(bf16[32,8,128]{2,1,0:T(8,128)(2,1)S(1)} %all_to_all.56.refs_9_.refs_2_.refs_4_), channel_id=1, source_target_pairs={{0,4},{4,0},{8,12},{12,8},{16,20},{20,16},{24,28},{28,24},{32,36},... | collective-permute-start | bytes 196616 | tf_op jit(solution)/shard_map/ppermute | solution.py:286
  64.6 2.5 %collective-permute-start.8 = (bf16[32,8,128]{2,1,0:T(8,128)(2,1)S(1)}, bf16[32,8,128]{2,1,0:T(8,128)(2,1)S(1)}, u32[]{:S(2)}, u32[]{:S(2)}) collective-permute-start(bf16[32,8,128]{2,1,0:T(8,128)(2,1)S(1)} %all_to_all.57.refs_11_.refs_2_.refs_5_), channel_id=1, source_target_pairs={{0,4},{4,0},{8,12},{12,8},{16,20},{20,16},{24,28},{28,24},{32,36},... | collective-permute-start | bytes 196616 | tf_op jit(solution)/shard_map/ppermute | solution.py:286
  79.4 2.5 %collective-permute-start.9 = (bf16[32,8,128]{2,1,0:T(8,128)(2,1)S(1)}, bf16[32,8,128]{2,1,0:T(8,128)(2,1)S(1)}, u32[]{:S(2)}, u32[]{:S(2)}) collective-permute-start(bf16[32,8,128]{2,1,0:T(8,128)(2,1)S(1)} %all_to_all.58.refs_13_.refs_2_.refs_6_), channel_id=1, source_target_pairs={{0,4},{4,0},{8,12},{12,8},{16,20},{20,16},{24,28},{28,24},{32,36},... | collective-permute-start | bytes 196616 | tf_op jit(solution)/shard_map/ppermute | solution.py:286
  94.2 2.5 %collective-permute-start.10 = (bf16[32,8,128]{2,1,0:T(8,128)(2,1)S(1)}, bf16[32,8,128]{2,1,0:T(8,128)(2,1)S(1)}, u32[]{:S(2)}, u32[]{:S(2)}) collective-permute-start(bf16[32,8,128]{2,1,0:T(8,128)(2,1)S(1)} %all_to_all.59.refs_15_.refs_2_.refs_7_), channel_id=1, source_target_pairs={{0,4},{4,0},{8,12},{12,8},{16,20},{20,16},{24,28},{28,24},{32,36},... | collective-permute-start | bytes 196616 | tf_op jit(solution)/shard_map/ppermute | solution.py:286

commit v9 on v8

--- a/solution.py
+++ b/solution.py
@@ -82,12 +82,14 @@
         acc[at] = acc[at] + terms[:, j * plan.width : (j + 1) * plan.width]
 
 
-def give_terms(plan, level, acc, out):
-    core = lax.rem(lax.axis_index("chain"), PAIR)
+def give_terms(plan, level, acc, own, other):
     part = plan.lanes // PAIR
-    for i in range(PAIR):
-        at = level * plan.lanes + i * part
-        out[:, core ^ i] = acc[pl.ds(at, part)].astype(BF16)
+    own[...] = acc[pl.ds(level * plan.lanes, part)]
+    other[...] = acc[pl.ds(level * plan.lanes + part, part)].astype(BF16)
+
+
+def add_other(own, other, out):
+    out[...] = (own[...] + other[...].astype(F32)).astype(BF16)
 
 
 def forward_first(plan, *refs):
@@ -201,7 +203,7 @@
     table, right, inverse = refs[:3]
     sources = refs[3 : 3 + plan.cols]
     earlier = refs[3 + plan.cols : 3 + plan.cols + PAIR * level]
-    half, solved, acc, out, store = refs[3 + plan.cols + PAIR * level :]
+    half, solved, acc, own, other, store = refs[3 + plan.cols + PAIR * level :]
     gather_store(plan, level, earlier, store)
     acc[...] = jnp.zeros(acc.shape, F32)
     segment = half_segment(plan, level, table, right, inverse, sources, store)
@@ -211,7 +213,7 @@
     ).astype(BF16)
     solved[...] = segment
     add_terms(plan, level, table, segment, sources, acc)
-    give_terms(plan, level - 1, acc, out)
+    give_terms(plan, level - 1, acc, own, other)
 
 
 def solve_back(half, inverse, arrived):
@@ -223,11 +225,11 @@
 def backward_level(plan, level, *refs):
     table, inverse, front, arrived, _ = refs[:5]
     sources = refs[5 : 5 + plan.cols]
-    solved, acc, out = refs[5 + plan.cols :]
+    solved, acc, own, other = refs[5 + plan.cols :]
     segment = solve_back(front[lax.axis_index("chain") // PAIR], inverse[level], arrived)
     solved[...] = segment
     add_terms(plan, level, table, segment, sources, acc)
-    give_terms(plan, level - 1, acc, out)
+    give_terms(plan, level - 1, acc, own, other)
 
 
 def finish(plan, *refs):
@@ -265,7 +267,7 @@
     vmem = pl.BlockSpec(memory_space=pltpu.VMEM)
     segment_shape = pltpu.VMEM((share, width), BF16)
     front_shape = pltpu.VMEM((lanes // PAIR, share, width), BF16)
-    terms_shape = pltpu.VMEM((lanes // PAIR, PAIR, share, width), BF16)
+    own_shape = pltpu.VMEM((lanes // PAIR, share, width), F32)
     params = pltpu.CompilerParams(vmem_limit_bytes=12 * 1024 * 1024)
 
     def far_off(x):
@@ -280,15 +282,29 @@
     def store(level):
         return pltpu.VMEM((level * lanes + 1, share, width), BF16)
 
+    def across(x):
+        return held(lax.ppermute(x, "chain", [(i, i ^ 1) for i in range(lanes)]))
+
+    def among(x):
+        groups = [list(range(i, lanes, PAIR)) for i in range(PAIR)]
+        return held(
+            lax.all_to_all(x, "chain", 0, 0, tiled=True, axis_index_groups=groups)
+        )
+
     def exchange(x):
-        groups = [list(range(i, lanes, PAIR)) for i in range(PAIR)]
-        own = lax.all_to_all(x, "chain", 0, 0, tiled=True, axis_index_groups=groups)
-        other = lax.ppermute(own, "chain", [(i, i ^ 1) for i in range(lanes)])
-        return [held(own), held(other)]
-
-    def exchange_back(x):
-        x = x.reshape(lanes, share, width)
-        return held(lax.all_to_all(x, "chain", 0, 0, tiled=True))
+        own = among(x)
+        return [own, across(own)]
+
+    def exchange_back(own, other):
+        whole = pl.pallas_call(
+            add_other,
+            out_shape=front_shape,
+            in_specs=[vmem, vmem],
+            out_specs=vmem,
+            compiler_params=params,
+            name="add_other",
+        )(held(own), across(other))
+        return among(whole)
 
     def around(x):
         return [held(x)] + [
@@ -376,22 +392,22 @@
 
     last = levels - 1
     acc_shape = pltpu.VMEM((last * lanes + 1, share, width), F32)
-    half_last, solved, acc, terms = pl.pallas_call(
+    half_last, solved, acc, *terms = pl.pallas_call(
         functools.partial(turn_level, plan, last),
-        out_shape=(segment_shape, segment_shape, acc_shape, terms_shape),
+        out_shape=(segment_shape, segment_shape, acc_shape, own_shape, front_shape),
         in_specs=[smem] + [vmem] * (2 + cols + PAIR * last),
-        out_specs=(vmem,) * 4,
+        out_specs=(vmem,) * 5,
         scratch_shapes=[store(last)],
         compiler_params=params,
         name="turn_level",
     )(table, rights, inverses, *sources(last), *fronts)
     done = [held(solved)]
     for k in range(last - 1, 0, -1):
-        solved, acc, terms = pl.pallas_call(
+        solved, acc, *terms = pl.pallas_call(
             functools.partial(backward_level, plan, k),
-            out_shape=(segment_shape, acc_shape, terms_shape),
+            out_shape=(segment_shape, acc_shape, own_shape, front_shape),
             in_specs=[smem] + [vmem] * (4 + cols),
-            out_specs=(vmem,) * 3,
+            out_specs=(vmem,) * 4,
             input_output_aliases={4: 1},
             compiler_params=params,
             name=f"backward_level_{k}",
@@ -399,7 +415,7 @@
             table,
             inverses,
             fronts[PAIR * k],
-            exchange_back(terms),
+            exchange_back(*terms),
             held(acc),
             *sources(k),
         )
@@ -415,7 +431,7 @@
         ],
         compiler_params=params,
         name="finish",
-    )(table, inverses, exchange_back(terms), *fronts[::PAIR], held(half_last), *done)
+    )(table, inverses, exchange_back(*terms), *fronts[::PAIR], held(half_last), *done)
     whole = lax.all_to_all(shares, "col", 0, 0, tiled=True)
     whole = whole.transpose(1, 0, 2, 3).reshape(2, rows, 1, probes, width)
     return whole[0], whole[1]

time: 184 us -> 180 us (0.978)
  blocking collectives: 152 us -> 136 us
  starting transfers between devices: 18.7 us -> 26.1 us
  waiting for transfers between devices: 4.53 us -> 9.04 us
    all_to_all x10, blocking collectives: 144 us -> 128 us  [among(): lax.all_to_all(x, 'chain', 0, 0, tiled=True, axis_index_groups=groups)]
    ppermute x5 -> x10, starting transfers between devices: 9.98 us -> 17.3 us  [across(): return held(lax.ppermute(x, 'chain', [(i, i ^ 1) for i in range(lanes)]))]
    ppermute x5 -> x10, waiting for transfers between devices: 4.51 us -> 9.02 us  [across(): return held(lax.ppermute(x, 'chain', [(i, i ^ 1) for i in range(lanes)]))]
  transfers between devices with their start and end apart: 11 -> 16, of which waited for: 5 -> 10; matrix products, arithmetic and copies ran while one was open for 0% -> 0% of each run, Pallas kernels for 0% -> 0%
where the time goes in v9:
time: 180 us; the launch traced here: 179 us
  blocking collectives  136 us (76%)
  starting transfers between devices  26.1 us (14%)
  waiting for transfers between devices  9.04 us (5%)
  Pallas kernels  6.71 us (4%)
    all_to_all x10, blocking collectives, among(): lax.all_to_all(x, 'chain', 0, 0, tiled=True, axis_index_groups=groups)  128 us
    ppermute x10, starting transfers between devices, across(): return held(lax.ppermute(x, 'chain', [(i, i ^ 1) for i in range(lanes)]))  17.3 us
    ppermute x10, waiting for transfers between devices, across(): return held(lax.ppermute(x, 'chain', [(i, i ^ 1) for i in range(lanes)]))  9.02 us
    ppermute x6, starting transfers between devices, around(): lax.ppermute(x, 'col', [(i, i ^ s) for i in range(cols)])  8.73 us
    all_to_all x1, blocking collectives, per_device(): whole = lax.all_to_all(shares, 'col', 0, 0, tiled=True)  7.86 us
  transfers between devices with their start and end apart: 16, of which 10 were waited for; matrix products, arithmetic and copies ran while one was open for 0% of the time, Pallas kernels for 0%

profile of v9, /device:TPU:1, one launch (start us, length us, event | category | flops | bytes accessed | tf_op | source)
XLA Modules:
  0.0 179.3 jit_solution(7322293447620045999)
XLA Ops:
  0.6 1.3 forward_first.1
  2.0 3.7 %collective-permute-start.3 = (bf16[1552,128]{1,0:T(8,128)(2,1)S(1)}, bf16[1552,128]{1,0:T(8,128)(2,1)S(1)}, u32[]{:S(2)}, u32[]{:S(2)}) collective-permute-start(bf16[1552,128]{1,0:T(8,128)(2,1)S(1)} %get-tuple-element.34.refs_5_.refs_3_), channel_id=1, source_target_pairs={{0,2},{1,3},{2,0},{3,1},{4,6},{5,7},{6,4},{7,5},{8,10},{9,11},{10,... | collective-permute-start | bytes 1191944 | tf_op jit(solution)/shard_map/ppermute | solution.py:311
  6.5 19.8 %all_to_all.55.refs_3_.refs_7_ = bf16[32,8,128]{2,1,0:T(8,128)(2,1)S(1)} all-to-all(bf16[32,8,128]{2,1,0:T(8,128)(2,1)S(1)} %get-tuple-element.33), channel_id=1, replica_groups={{0,8,16,24,32,40,48,56,64,72,80,88,96,104,112,120,128,136,144,152,160,1..., dimensions={0} | all-to-all | bytes 131072 | tf_op jit(solution)/shard_map/all_to_all | solution.py:291
  26.3 2.7 %collective-permute-start = (bf16[32,8,128]{2,1,0:T(8,128)(2,1)S(1)}, bf16[32,8,128]{2,1,0:T(8,128)(2,1)S(1)}, u32[]{:S(2)}, u32[]{:S(2)}) collective-permute-start(bf16[32,8,128]{2,1,0:T(8,128)(2,1)S(1)} %all_to_all.55.refs_3_.refs_7_), channel_id=1, source_target_pairs={{0,4},{4,0},{8,12},{12,8},{16,20},{20,16},{24,28},{28,24},{32,36},... | collective-permute-start | bytes 196616 | tf_op jit(solution)/shard_map/ppermute | solution.py:286
  29.0 0.9 collective-permute-done.refs_4_.refs_8_
  29.9 1.2 forward_second.1
  31.2 3.3 %collective-permute-start.7 = (bf16[2304,128]{1,0:T(8,128)(2,1)S(1)}, bf16[2304,128]{1,0:T(8,128)(2,1)S(1)}, u32[]{:S(2)}, u32[]{:S(2)}) collective-permute-start(bf16[2304,128]{1,0:T(8,128)(2,1)S(1)} %after.1.refs_3_.refs_5_), channel_id=1, source_target_pairs={{0,2},{1,3},{2,0},{3,1},{4,6},{5,7},{6,4},{7,5},{8,10},{9,11},{10,... | collective-permute-start | bytes 1769480 | tf_op jit(solution)/shard_map/ppermute | solution.py:311
  35.4 13.5 %all_to_all.56.refs_9_.refs_2_.refs_4_ = bf16[32,8,128]{2,1,0:T(8,128)(2,1)S(1)} all-to-all(bf16[32,8,128]{2,1,0:T(8,128)(2,1)S(1)} %get-tuple-element.36.segment), channel_id=1, replica_groups={{0,8,16,24,32,40,48,56,64,72,80,88,96,104,112,120,128,136,144,152,160,1..., dimensions={0} | all-to-all | bytes 131072 | tf_op jit(solution)/shard_map/all_to_all | solution.py:291
  48.8 2.5 %collective-permute-start.4 = (bf16[32,8,128]{2,1,0:T(8,128)(2,1)S(1)}, bf16[32,8,128]{2,1,0:T(8,128)(2,1)S(1)}, u32[]{:S(2)}, u32[]{:S(2)}) collective-permute-start(bf16[32,8,128]{2,1,0:T(8,128)(2,1)S(1)} %all_to_all.56.refs_9_.refs_2_.refs_4_), channel_id=1, source_target_pairs={{0,4},{4,0},{8,12},{12,8},{16,20},{20,16},{24,28},{28,24},{32,36},... | collective-permute-start | bytes 196616 | tf_op jit(solution)/shard_map/ppermute | solution.py:286
  51.4 0.9 collective-permute-done.4.refs_10_
  52.7 11.9 %all_to_all.57.refs_11_.refs_2_.refs_5_ = bf16[32,8,128]{2,1,0:T(8,128)(2,1)S(1)} all-to-all(bf16[32,8,128]{2,1,0:T(8,128)(2,1)S(1)} %forward_level_2.1), channel_id=1, replica_groups={{0,8,16,24,32,40,48,56,64,72,80,88,96,104,112,120,128,136,144,152,160,1..., dimensions={0} | all-to-all | bytes 131072 | tf_op jit(solution)/shard_map/all_to_all | solution.py:291
  64.6 1.6 collective-permute-start.8
  66.1 0.9 collective-permute-done.8.refs_12_
  67.5 11.9 %all_to_all.58.refs_13_.refs_2_.refs_6_ = bf16[32,8,128]{2,1,0:T(8,128)(2,1)S(1)} all-to-all(bf16[32,8,128]{2,1,0:T(8,128)(2,1)S(1)} %forward_level_3.1), channel_id=1, replica_groups={{0,8,16,24,32,40,48,56,64,72,80,88,96,104,112,120,128,136,144,152,160,1..., dimensions={0} | all-to-all | bytes 131072 | tf_op jit(solution)/shard_map/all_to_all | solution.py:291
  79.4 1.6 collective-permute-start.9
  81.0 0.9 collective-permute-done.9.refs_14_
  82.3 11.9 %all_to_all.59.refs_15_.refs_2_.refs_7_ = bf16[32,8,128]{2,1,0:T(8,128)(2,1)S(1)} all-to-all(bf16[32,8,128]{2,1,0:T(8,128)(2,1)S(1)} %forward_level_4.1), channel_id=1, replica_groups={{0,8,16,24,32,40,48,56,64,72,80,88,96,104,112,120,128,136,144,152,160,1..., dimensions={0} | all-to-all | bytes 131072 | tf_op jit(solution)/shard_map/all_to_all | solution.py:291
  94.2 1.6 collective-permute-start.10
  95.8 0.9 collective-permute-done.10.refs_16_
  96.7 1.0 turn_level.1
  98.2 0.9 collective-permute-done.11.other
  99.1 11.8 %all_to_all.60.refs_3_ = bf16[32,8,128]{2,1,0:T(8,128)(2,1)S(1)} all-to-all(bf16[32,8,128]{2,1,0:T(8,128)(2,1)S(1)} %add_other.5), channel_id=1, replica_groups={{0,8,16,24,32,40,48,56,64,72,80,88,96,104,112,120,128,136,144,152,160,1..., dimensions={0} | all-to-all | bytes 131072 | tf_op jit(solution)/shard_map/all_to_all | solution.py:291
  111.4 1.7 collective-permute-start.12
  113.0 0.9 collective-permute-done.12.other
  113.9 11.8 %all_to_all.61.refs_3_ = bf16[32,8,128]{2,1,0:T(8,128)(2,1)S(1)} all-to-all(bf16[32,8,128]{2,1,0:T(8,128)(2,1)S(1)} %add_other.6), channel_id=1, replica_groups={{0,8,16,24,32,40,48,56,64,72,80,88,96,104,112,120,128,136,144,152,160,1..., dimensions={0} | all-to-all | bytes 131072 | tf_op jit(solution)/shard_map/all_to_all | solution.py:291
  126.2 1.9 %collective-permute-start.13 = (bf16[32,8,128]{2,1,0:T(8,128)(2,1)S(1)}, bf16[32,8,128]{2,1,0:T(8,128)(2,1)S(1)}, u32[]{:S(2)}, u32[]{:S(2)}) collective-permute-start(bf16[32,8,128]{2,1,0:T(8,128)(2,1)S(1)} %get-tuple-element.45), channel_id=1, source_target_pairs={{0,4},{4,0},{8,12},{12,8},{16,20},{20,16},{24,28},{28,24},{32,36},... | collective-permute-start | bytes 196616 | tf_op jit(solution)/shard_map/ppermute | solution.py:286
  129.0 11.8 %all_to_all.62.refs_3_ = bf16[32,8,128]{2,1,0:T(8,128)(2,1)S(1)} all-to-all(bf16[32,8,128]{2,1,0:T(8,128)(2,1)S(1)} %add_other.7), channel_id=1, replica_groups={{0,8,16,24,32,40,48,56,64,72,80,88,96,104,112,120,128,136,144,152,160,1..., dimensions={0} | all-to-all | bytes 131072 | tf_op jit(solution)/shard_map/all_to_all | solution.py:291
  141.3 1.7 collective-permute-start.14
  143.9 11.8 %all_to_all.63.refs_3_ = bf16[32,8,128]{2,1,0:T(8,128)(2,1)S(1)} all-to-all(bf16[32,8,128]{2,1,0:T(8,128)(2,1)S(1)} %add_other.8), channel_id=1, replica_groups={{0,8,16,24,32,40,48,56,64,72,80,88,96,104,112,120,128,136,144,152,160,1..., dimensions={0} | all-to-all | bytes 131072 | tf_op jit(solution)/shard_map/all_to_all | solution.py:291
  156.2 1.7 collective-permute-start.15
  158.7 11.8 %all_to_all.64.refs_2_ = bf16[32,8,128]{2,1,0:T(8,128)(2,1)S(1)} all-to-all(bf16[32,8,128]{2,1,0:T(8,128)(2,1)S(1)} %add_other.9), channel_id=1, replica_groups={{0,8,16,24,32,40,48,56,64,72,80,88,96,104,112,120,128,136,144,152,160,1..., dimensions={0} | all-to-all | bytes 131072 | tf_op jit(solution)/shard_map/all_to_all | solution.py:291
  170.8 7.9 %all_to_all.65 = bf16[4,8,8,128]{3,2,1,0:T(8,128)(2,1)S(1)} all-to-all(bf16[4,8,8,128]{3,2,1,0:T(8,128)(2,1)S(1)} %finish.1), channel_id=1, replica_groups=mesh['chain'=64,'col'=4] {'col'}, dimensions={0} | all-to-all | bytes 131072 | tf_op jit(solution)/shard_map/all_to_all | solution.py:435
  (30 shorter events, 8.6 us)
Async XLA Ops:
  2.0 27.9 %collective-permute-start.3 = (bf16[1552,128]{1,0:T(8,128)(2,1)S(1)}, bf16[1552,128]{1,0:T(8,128)(2,1)S(1)}, u32[]{:S(2)}, u32[]{:S(2)}) collective-permute-start(bf16[1552,128]{1,0:T(8,128)(2,1)S(1)} %get-tuple-element.34.refs_5_.refs_3_), channel_id=1, source_target_pairs={{0,2},{1,3},{2,0},{3,1},{4,6},{5,7},{6,4},{7,5},{8,10},{9,11},{10,... | collective-permute-start | bytes 1191944 | tf_op jit(solution)/shard_map/ppermute | solution.py:311
  5.6 24.3 %collective-permute-start.2 = (bf16[1552,128]{1,0:T(8,128)(2,1)S(1)}, bf16[1552,128]{1,0:T(8,128)(2,1)S(1)}, u32[]{:S(2)}, u32[]{:S(2)}) collective-permute-start(bf16[1552,128]{1,0:T(8,128)(2,1)S(1)} %get-tuple-element.34.refs_5_.refs_3_), channel_id=1, source_target_pairs={{0,3},{1,2},{2,1},{3,0},{4,7},{5,6},{6,5},{7,4},{8,11},{9,10},{10,... | collective-permute-start | bytes 1191944 | tf_op jit(solution)/shard_map/ppermute | solution.py:311
  6.5 23.4 %collective-permute-start.1 = (bf16[1552,128]{1,0:T(8,128)(2,1)S(1)}, bf16[1552,128]{1,0:T(8,128)(2,1)S(1)}, u32[]{:S(2)}, u32[]{:S(2)}) collective-permute-start(bf16[1552,128]{1,0:T(8,128)(2,1)S(1)} %get-tuple-element.34.refs_5_.refs_3_), channel_id=1, source_target_pairs={{0,1},{1,0},{2,3},{3,2},{4,5},{5,4},{6,7},{7,6},{8,9},{9,8},{10,11... | collective-permute-start | bytes 1191944 | tf_op jit(solution)/shard_map/ppermute | solution.py:311
  26.3 3.6 %collective-permute-start = (bf16[32,8,128]{2,1,0:T(8,128)(2,1)S(1)}, bf16[32,8,128]{2,1,0:T(8,128)(2,1)S(1)}, u32[]{:S(2)}, u32[]{:S(2)}) collective-permute-start(bf16[32,8,128]{2,1,0:T(8,128)(2,1)S(1)} %all_to_all.55.refs_3_.refs_7_), channel_id=1, source_target_pairs={{0,4},{4,0},{8,12},{12,8},{16,20},{20,16},{24,28},{28,24},{32,36},... | collective-permute-start | bytes 196616 | tf_op jit(solution)/shard_map/ppermute | solution.py:286
  31.2 35.9 %collective-permute-start.7 = (bf16[2304,128]{1,0:T(8,128)(2,1)S(1)}, bf16[2304,128]{1,0:T(8,128)(2,1)S(1)}, u32[]{:S(2)}, u32[]{:S(2)}) collective-permute-start(bf16[2304,128]{1,0:T(8,128)(2,1)S(1)} %after.1.refs_3_.refs_5_), channel_id=1, source_target_pairs={{0,2},{1,3},{2,0},{3,1},{4,6},{5,7},{6,4},{7,5},{8,10},{9,11},{10,... | collective-permute-start | bytes 1769480 | tf_op jit(solution)/shard_map/ppermute | solution.py:311
  34.5 32.6 %collective-permute-start.6 = (bf16[2304,128]{1,0:T(8,128)(2,1)S(1)}, bf16[2304,128]{1,0:T(8,128)(2,1)S(1)}, u32[]{:S(2)}, u32[]{:S(2)}) collective-permute-start(bf16[2304,128]{1,0:T(8,128)(2,1)S(1)} %after.1.refs_3_.refs_5_), channel_id=1, source_target_pairs={{0,3},{1,2},{2,1},{3,0},{4,7},{5,6},{6,5},{7,4},{8,11},{9,10},{10,... | collective-permute-start | bytes 1769480 | tf_op jit(solution)/shard_map/ppermute | solution.py:311
  35.4 31.7 %collective-permute-start.5 = (bf16[2304,128]{1,0:T(8,128)(2,1)S(1)}, bf16[2304,128]{1,0:T(8,128)(2,1)S(1)}, u32[]{:S(2)}, u32[]{:S(2)}) collective-permute-start(bf16[2304,128]{1,0:T(8,128)(2,1)S(1)} %after.1.refs_3_.refs_5_), channel_id=1, source_target_pairs={{0,1},{1,0},{2,3},{3,2},{4,5},{5,4},{6,7},{7,6},{8,9},{9,8},{10,11... | collective-permute-start | bytes 1769480 | tf_op jit(solution)/shard_map/ppermute | solution.py:311
  48.8 3.4 %collective-permute-start.4 = (bf16[32,8,128]{2,1,0:T(8,128)(2,1)S(1)}, bf16[32,8,128]{2,1,0:T(8,128)(2,1)S(1)}, u32[]{:S(2)}, u32[]{:S(2)}) collective-permute-start(bf16[32,8,128]{2,1,0:T(8,128)(2,1)S(1)} %all_to_all.56.refs_9_.refs_2_.refs_4_), channel_id=1, source_target_pairs={{0,4},{4,0},{8,12},{12,8},{16,20},{20,16},{24,28},{28,24},{32,36},... | collective-permute-start | bytes 196616 | tf_op jit(solution)/shard_map/ppermute | solution.py:286
  64.6 2.5 %collective-permute-start.8 = (bf16[32,8,128]{2,1,0:T(8,128)(2,1)S(1)}, bf16[32,8,128]{2,1,0:T(8,128)(2,1)S(1)}, u32[]{:S(2)}, u32[]{:S(2)}) collective-permute-start(bf16[32,8,128]{2,1,0:T(8,128)(2,1)S(1)} %all_to_all.57.refs_11_.refs_2_.refs_5_), channel_id=1, source_target_pairs={{0,4},{4,0},{8,12},{12,8},{16,20},{20,16},{24,28},{28,24},{32,36},... | collective-permute-start | bytes 196616 | tf_op jit(solution)/shard_map/ppermute | solution.py:286
  79.4 2.5 %collective-permute-start.9 = (bf16[32,8,128]{2,1,0:T(8,128)(2,1)S(1)}, bf16[32,8,128]{2,1,0:T(8,128)(2,1)S(1)}, u32[]{:S(2)}, u32[]{:S(2)}) collective-permute-start(bf16[32,8,128]{2,1,0:T(8,128)(2,1)S(1)} %all_to_all.58.refs_13_.refs_2_.refs_6_), channel_id=1, source_target_pairs={{0,4},{4,0},{8,12},{12,8},{16,20},{20,16},{24,28},{28,24},{32,36},... | collective-permute-start | bytes 196616 | tf_op jit(solution)/shard_map/ppermute | solution.py:286
  94.2 2.5 %collective-permute-start.10 = (bf16[32,8,128]{2,1,0:T(8,128)(2,1)S(1)}, bf16[32,8,128]{2,1,0:T(8,128)(2,1)S(1)}, u32[]{:S(2)}, u32[]{:S(2)}) collective-permute-start(bf16[32,8,128]{2,1,0:T(8,128)(2,1)S(1)} %all_to_all.59.refs_15_.refs_2_.refs_7_), channel_id=1, source_target_pairs={{0,4},{4,0},{8,12},{12,8},{16,20},{20,16},{24,28},{28,24},{32,36},... | collective-permute-start | bytes 196616 | tf_op jit(solution)/shard_map/ppermute | solution.py:286
  97.8 1.3 collective-permute-start.11
  111.4 2.6 %collective-permute-start.12 = (bf16[32,8,128]{2,1,0:T(8,128)(2,1)S(1)}, bf16[32,8,128]{2,1,0:T(8,128)(2,1)S(1)}, u32[]{:S(2)}, u32[]{:S(2)}) collective-permute-start(bf16[32,8,128]{2,1,0:T(8,128)(2,1)S(1)} %get-tuple-element.42), channel_id=1, source_target_pairs={{0,4},{4,0},{8,12},{12,8},{16,20},{20,16},{24,28},{28,24},{32,36},... | collective-permute-start | bytes 196616 | tf_op jit(solution)/shard_map/ppermute | solution.py:286
  126.2 2.8 %collective-permute-start.13 = (bf16[32,8,128]{2,1,0:T(8,128)(2,1)S(1)}, bf16[32,8,128]{2,1,0:T(8,128)(2,1)S(1)}, u32[]{:S(2)}, u32[]{:S(2)}) collective-permute-start(bf16[32,8,128]{2,1,0:T(8,128)(2,1)S(1)} %get-tuple-element.45), channel_id=1, source_target_pairs={{0,4},{4,0},{8,12},{12,8},{16,20},{20,16},{24,28},{28,24},{32,36},... | collective-permute-start | bytes 196616 | tf_op jit(solution)/shard_map/ppermute | solution.py:286
  141.3 2.6 %collective-permute-start.14 = (bf16[32,8,128]{2,1,0:T(8,128)(2,1)S(1)}, bf16[32,8,128]{2,1,0:T(8,128)(2,1)S(1)}, u32[]{:S(2)}, u32[]{:S(2)}) collective-permute-start(bf16[32,8,128]{2,1,0:T(8,128)(2,1)S(1)} %get-tuple-element.48), channel_id=1, source_target_pairs={{0,4},{4,0},{8,12},{12,8},{16,20},{20,16},{24,28},{28,24},{32,36},... | collective-permute-start | bytes 196616 | tf_op jit(solution)/shard_map/ppermute | solution.py:286
  156.2 2.6 %collective-permute-start.15 = (bf16[32,8,128]{2,1,0:T(8,128)(2,1)S(1)}, bf16[32,8,128]{2,1,0:T(8,128)(2,1)S(1)}, u32[]{:S(2)}, u32[]{:S(2)}) collective-permute-start(bf16[32,8,128]{2,1,0:T(8,128)(2,1)S(1)} %get-tuple-element.51), channel_id=1, source_target_pairs={{0,4},{4,0},{8,12},{12,8},{16,20},{20,16},{24,28},{28,24},{32,36},... | collective-permute-start | bytes 196616 | tf_op jit(solution)/shard_map/ppermute | solution.py:286

commit v10 on v9

--- a/solution.py
+++ b/solution.py
@@ -346,6 +346,17 @@
     rights, inverses, sizes = held(rights), held(inverses), scalars(sizes)
     near = around(own)
     fronts = exchange(first)
+    later = pl.pallas_call(
+        after,
+        out_shape=far_shape,
+        in_specs=[vmem, vmem],
+        out_specs=vmem,
+        input_output_aliases={0: 0},
+        compiler_params=params,
+        name="after",
+    )(held(later), fronts[0])
+    far = around(later)
+
     mine, table = pl.pallas_call(
         functools.partial(forward_second, plan),
         out_shape=(
@@ -363,16 +374,6 @@
         name="forward_second",
     )(sizes, rights, inverses, *fronts, *near)
     table = scalars(table)
-    later = pl.pallas_call(
-        after,
-        out_shape=far_shape,
-        in_specs=[vmem, vmem],
-        out_specs=vmem,
-        input_output_aliases={0: 0},
-        compiler_params=params,
-        name="after",
-    )(held(later), held(mine))
-    far = around(later)
     fronts += exchange(mine)
 
     def sources(level):

time: 180 us -> 178 us (0.989)
  transfers between devices with their start and end apart: 16 -> 16, of which waited for: 10 -> 9; matrix products, arithmetic and copies ran while one was open for 0% -> 0% of each run, Pallas kernels for 0% -> 1%
where the time goes in v10:
time: 178 us; the launch traced here: 177 us
  blocking collectives  135 us (76%)
  starting transfers between devices  25.3 us (14%)
  waiting for transfers between devices  8.13 us (5%)
  Pallas kernels  6.72 us (4%)
    all_to_all x10, blocking collectives, among(): lax.all_to_all(x, 'chain', 0, 0, tiled=True, axis_index_groups=groups)  127 us
    ppermute x10, starting transfers between devices, across(): return held(lax.ppermute(x, 'chain', [(i, i ^ 1) for i in range(lanes)]))  16.7 us
    all_to_all x1, blocking collectives, per_device(): whole = lax.all_to_all(shares, 'col', 0, 0, tiled=True)  8.78 us
    ppermute x6, starting transfers between devices, around(): lax.ppermute(x, 'col', [(i, i ^ s) for i in range(cols)])  8.64 us
    ppermute x10, waiting for transfers between devices, across(): return held(lax.ppermute(x, 'chain', [(i, i ^ 1) for i in range(lanes)]))  8.11 us
  transfers between devices with their start and end apart: 16, of which 9 were waited for; matrix products, arithmetic and copies ran while one was open for 0% of the time, Pallas kernels for 1%

profile of v10, /device:TPU:1, one launch (start us, length us, event | category | flops | bytes accessed | tf_op | source)
XLA Modules:
  0.0 176.9 jit_solution(16401585533366104819)
XLA Ops:
  0.6 1.3 forward_first.1
  2.0 3.7 %collective-permute-start.3 = (bf16[1552,128]{1,0:T(8,128)(2,1)S(1)}, bf16[1552,128]{1,0:T(8,128)(2,1)S(1)}, u32[]{:S(2)}, u32[]{:S(2)}) collective-permute-start(bf16[1552,128]{1,0:T(8,128)(2,1)S(1)} %get-tuple-element.34.refs_5_.refs_3_), channel_id=1, source_target_pairs={{0,2},{1,3},{2,0},{3,1},{4,6},{5,7},{6,4},{7,5},{8,10},{9,11},{10,... | collective-permute-start | bytes 1191944 | tf_op jit(solution)/shard_map/ppermute | solution.py:311
  6.5 19.8 %all_to_all.55.refs_3_.refs_7_.segment = bf16[32,8,128]{2,1,0:T(8,128)(2,1)S(1)} all-to-all(bf16[32,8,128]{2,1,0:T(8,128)(2,1)S(1)} %get-tuple-element.33), channel_id=1, replica_groups={{0,8,16,24,32,40,48,56,64,72,80,88,96,104,112,120,128,136,144,152,160,1..., dimensions={0} | all-to-all | bytes 131072 | tf_op jit(solution)/shard_map/all_to_all | solution.py:291
  26.3 2.7 %collective-permute-start = (bf16[32,8,128]{2,1,0:T(8,128)(2,1)S(1)}, bf16[32,8,128]{2,1,0:T(8,128)(2,1)S(1)}, u32[]{:S(2)}, u32[]{:S(2)}) collective-permute-start(bf16[32,8,128]{2,1,0:T(8,128)(2,1)S(1)} %all_to_all.55.refs_3_.refs_7_.segment), channel_id=1, source_target_pairs={{0,4},{4,0},{8,12},{12,8},{16,20},{20,16},{24,28},{28,24},{32,36},... | collective-permute-start | bytes 196616 | tf_op jit(solution)/shard_map/ppermute | solution.py:286
  29.0 3.3 %collective-permute-start.7 = (bf16[2304,128]{1,0:T(8,128)(2,1)S(1)}, bf16[2304,128]{1,0:T(8,128)(2,1)S(1)}, u32[]{:S(2)}, u32[]{:S(2)}) collective-permute-start(bf16[2304,128]{1,0:T(8,128)(2,1)S(1)} %after.1.refs_3_.refs_5_), channel_id=1, source_target_pairs={{0,2},{1,3},{2,0},{3,1},{4,6},{5,7},{6,4},{7,5},{8,10},{9,11},{10,... | collective-permute-start | bytes 1769480 | tf_op jit(solution)/shard_map/ppermute | solution.py:311
  33.2 1.2 forward_second.1
  34.4 11.9 %all_to_all.56.refs_9_.refs_2_.refs_4_ = bf16[32,8,128]{2,1,0:T(8,128)(2,1)S(1)} all-to-all(bf16[32,8,128]{2,1,0:T(8,128)(2,1)S(1)} %get-tuple-element.36), channel_id=1, replica_groups={{0,8,16,24,32,40,48,56,64,72,80,88,96,104,112,120,128,136,144,152,160,1..., dimensions={0} | all-to-all | bytes 131072 | tf_op jit(solution)/shard_map/all_to_all | solution.py:291
  46.3 1.8 %collective-permute-start.4 = (bf16[32,8,128]{2,1,0:T(8,128)(2,1)S(1)}, bf16[32,8,128]{2,1,0:T(8,128)(2,1)S(1)}, u32[]{:S(2)}, u32[]{:S(2)}) collective-permute-start(bf16[32,8,128]{2,1,0:T(8,128)(2,1)S(1)} %all_to_all.56.refs_9_.refs_2_.refs_4_), channel_id=1, source_target_pairs={{0,4},{4,0},{8,12},{12,8},{16,20},{20,16},{24,28},{28,24},{32,36},... | collective-permute-start | bytes 196616 | tf_op jit(solution)/shard_map/ppermute | solution.py:286
  48.1 0.9 collective-permute-done.4.refs_10_
  49.4 11.9 %all_to_all.57.refs_11_.refs_2_.refs_5_ = bf16[32,8,128]{2,1,0:T(8,128)(2,1)S(1)} all-to-all(bf16[32,8,128]{2,1,0:T(8,128)(2,1)S(1)} %forward_level_2.1), channel_id=1, replica_groups={{0,8,16,24,32,40,48,56,64,72,80,88,96,104,112,120,128,136,144,152,160,1..., dimensions={0} | all-to-all | bytes 131072 | tf_op jit(solution)/shard_map/all_to_all | solution.py:291
  61.3 1.6 collective-permute-start.8
  64.2 11.9 %all_to_all.58.refs_13_.refs_2_.refs_6_ = bf16[32,8,128]{2,1,0:T(8,128)(2,1)S(1)} all-to-all(bf16[32,8,128]{2,1,0:T(8,128)(2,1)S(1)} %forward_level_3.1), channel_id=1, replica_groups={{0,8,16,24,32,40,48,56,64,72,80,88,96,104,112,120,128,136,144,152,160,1..., dimensions={0} | all-to-all | bytes 131072 | tf_op jit(solution)/shard_map/all_to_all | solution.py:291
  76.1 1.6 collective-permute-start.9
  77.7 0.9 collective-permute-done.9.refs_14_
  79.0 11.9 %all_to_all.59.refs_15_.refs_2_.refs_7_ = bf16[32,8,128]{2,1,0:T(8,128)(2,1)S(1)} all-to-all(bf16[32,8,128]{2,1,0:T(8,128)(2,1)S(1)} %forward_level_4.1), channel_id=1, replica_groups={{0,8,16,24,32,40,48,56,64,72,80,88,96,104,112,120,128,136,144,152,160,1..., dimensions={0} | all-to-all | bytes 131072 | tf_op jit(solution)/shard_map/all_to_all | solution.py:291
  90.9 1.6 collective-permute-start.10
  92.5 0.9 collective-permute-done.10.refs_16_
  93.4 1.0 turn_level.1
  94.9 0.9 collective-permute-done.11.other
  95.8 11.8 %all_to_all.60.refs_3_ = bf16[32,8,128]{2,1,0:T(8,128)(2,1)S(1)} all-to-all(bf16[32,8,128]{2,1,0:T(8,128)(2,1)S(1)} %add_other.5), channel_id=1, replica_groups={{0,8,16,24,32,40,48,56,64,72,80,88,96,104,112,120,128,136,144,152,160,1..., dimensions={0} | all-to-all | bytes 131072 | tf_op jit(solution)/shard_map/all_to_all | solution.py:291
  108.1 1.7 collective-permute-start.12
  109.7 0.9 collective-permute-done.12.other
  110.7 11.8 %all_to_all.61.refs_3_ = bf16[32,8,128]{2,1,0:T(8,128)(2,1)S(1)} all-to-all(bf16[32,8,128]{2,1,0:T(8,128)(2,1)S(1)} %add_other.6), channel_id=1, replica_groups={{0,8,16,24,32,40,48,56,64,72,80,88,96,104,112,120,128,136,144,152,160,1..., dimensions={0} | all-to-all | bytes 131072 | tf_op jit(solution)/shard_map/all_to_all | solution.py:291
  122.9 1.9 %collective-permute-start.13 = (bf16[32,8,128]{2,1,0:T(8,128)(2,1)S(1)}, bf16[32,8,128]{2,1,0:T(8,128)(2,1)S(1)}, u32[]{:S(2)}, u32[]{:S(2)}) collective-permute-start(bf16[32,8,128]{2,1,0:T(8,128)(2,1)S(1)} %get-tuple-element.45), channel_id=1, source_target_pairs={{0,4},{4,0},{8,12},{12,8},{16,20},{20,16},{24,28},{28,24},{32,36},... | collective-permute-start | bytes 196616 | tf_op jit(solution)/shard_map/ppermute | solution.py:286
  124.9 0.9 collective-permute-done.13.other
  125.8 11.8 %all_to_all.62.refs_3_ = bf16[32,8,128]{2,1,0:T(8,128)(2,1)S(1)} all-to-all(bf16[32,8,128]{2,1,0:T(8,128)(2,1)S(1)} %add_other.7), channel_id=1, replica_groups={{0,8,16,24,32,40,48,56,64,72,80,88,96,104,112,120,128,136,144,152,160,1..., dimensions={0} | all-to-all | bytes 131072 | tf_op jit(solution)/shard_map/all_to_all | solution.py:291
  138.0 1.6 collective-permute-start.14
  140.6 11.8 %all_to_all.63.refs_3_ = bf16[32,8,128]{2,1,0:T(8,128)(2,1)S(1)} all-to-all(bf16[32,8,128]{2,1,0:T(8,128)(2,1)S(1)} %add_other.8), channel_id=1, replica_groups={{0,8,16,24,32,40,48,56,64,72,80,88,96,104,112,120,128,136,144,152,160,1..., dimensions={0} | all-to-all | bytes 131072 | tf_op jit(solution)/shard_map/all_to_all | solution.py:291
  152.9 1.7 collective-permute-start.15
  154.5 0.9 collective-permute-done.15.other
  155.5 11.8 %all_to_all.64.refs_2_ = bf16[32,8,128]{2,1,0:T(8,128)(2,1)S(1)} all-to-all(bf16[32,8,128]{2,1,0:T(8,128)(2,1)S(1)} %add_other.9), channel_id=1, replica_groups={{0,8,16,24,32,40,48,56,64,72,80,88,96,104,112,120,128,136,144,152,160,1..., dimensions={0} | all-to-all | bytes 131072 | tf_op jit(solution)/shard_map/all_to_all | solution.py:291
  167.5 8.8 %all_to_all.65 = bf16[4,8,8,128]{3,2,1,0:T(8,128)(2,1)S(1)} all-to-all(bf16[4,8,8,128]{3,2,1,0:T(8,128)(2,1)S(1)} %finish.1), channel_id=1, replica_groups=mesh['chain'=64,'col'=4] {'col'}, dimensions={0} | all-to-all | bytes 131072 | tf_op jit(solution)/shard_map/all_to_all | solution.py:436
  (30 shorter events, 7.7 us)
Async XLA Ops:
  2.0 31.1 %collective-permute-start.3 = (bf16[1552,128]{1,0:T(8,128)(2,1)S(1)}, bf16[1552,128]{1,0:T(8,128)(2,1)S(1)}, u32[]{:S(2)}, u32[]{:S(2)}) collective-permute-start(bf16[1552,128]{1,0:T(8,128)(2,1)S(1)} %get-tuple-element.34.refs_5_.refs_3_), channel_id=1, source_target_pairs={{0,2},{1,3},{2,0},{3,1},{4,6},{5,7},{6,4},{7,5},{8,10},{9,11},{10,... | collective-permute-start | bytes 1191944 | tf_op jit(solution)/shard_map/ppermute | solution.py:311
  5.6 27.5 %collective-permute-start.2 = (bf16[1552,128]{1,0:T(8,128)(2,1)S(1)}, bf16[1552,128]{1,0:T(8,128)(2,1)S(1)}, u32[]{:S(2)}, u32[]{:S(2)}) collective-permute-start(bf16[1552,128]{1,0:T(8,128)(2,1)S(1)} %get-tuple-element.34.refs_5_.refs_3_), channel_id=1, source_target_pairs={{0,3},{1,2},{2,1},{3,0},{4,7},{5,6},{6,5},{7,4},{8,11},{9,10},{10,... | collective-permute-start | bytes 1191944 | tf_op jit(solution)/shard_map/ppermute | solution.py:311
  6.5 26.6 %collective-permute-start.1 = (bf16[1552,128]{1,0:T(8,128)(2,1)S(1)}, bf16[1552,128]{1,0:T(8,128)(2,1)S(1)}, u32[]{:S(2)}, u32[]{:S(2)}) collective-permute-start(bf16[1552,128]{1,0:T(8,128)(2,1)S(1)} %get-tuple-element.34.refs_5_.refs_3_), channel_id=1, source_target_pairs={{0,1},{1,0},{2,3},{3,2},{4,5},{5,4},{6,7},{7,6},{8,9},{9,8},{10,11... | collective-permute-start | bytes 1191944 | tf_op jit(solution)/shard_map/ppermute | solution.py:311
  26.3 5.9 %collective-permute-start = (bf16[32,8,128]{2,1,0:T(8,128)(2,1)S(1)}, bf16[32,8,128]{2,1,0:T(8,128)(2,1)S(1)}, u32[]{:S(2)}, u32[]{:S(2)}) collective-permute-start(bf16[32,8,128]{2,1,0:T(8,128)(2,1)S(1)} %all_to_all.55.refs_3_.refs_7_.segment), channel_id=1, source_target_pairs={{0,4},{4,0},{8,12},{12,8},{16,20},{20,16},{24,28},{28,24},{32,36},... | collective-permute-start | bytes 196616 | tf_op jit(solution)/shard_map/ppermute | solution.py:286
  29.0 33.9 %collective-permute-start.7 = (bf16[2304,128]{1,0:T(8,128)(2,1)S(1)}, bf16[2304,128]{1,0:T(8,128)(2,1)S(1)}, u32[]{:S(2)}, u32[]{:S(2)}) collective-permute-start(bf16[2304,128]{1,0:T(8,128)(2,1)S(1)} %after.1.refs_3_.refs_5_), channel_id=1, source_target_pairs={{0,2},{1,3},{2,0},{3,1},{4,6},{5,7},{6,4},{7,5},{8,10},{9,11},{10,... | collective-permute-start | bytes 1769480 | tf_op jit(solution)/shard_map/ppermute | solution.py:311
  32.3 30.6 %collective-permute-start.6 = (bf16[2304,128]{1,0:T(8,128)(2,1)S(1)}, bf16[2304,128]{1,0:T(8,128)(2,1)S(1)}, u32[]{:S(2)}, u32[]{:S(2)}) collective-permute-start(bf16[2304,128]{1,0:T(8,128)(2,1)S(1)} %after.1.refs_3_.refs_5_), channel_id=1, source_target_pairs={{0,3},{1,2},{2,1},{3,0},{4,7},{5,6},{6,5},{7,4},{8,11},{9,10},{10,... | collective-permute-start | bytes 1769480 | tf_op jit(solution)/shard_map/ppermute | solution.py:311
  33.1 29.7 %collective-permute-start.5 = (bf16[2304,128]{1,0:T(8,128)(2,1)S(1)}, bf16[2304,128]{1,0:T(8,128)(2,1)S(1)}, u32[]{:S(2)}, u32[]{:S(2)}) collective-permute-start(bf16[2304,128]{1,0:T(8,128)(2,1)S(1)} %after.1.refs_3_.refs_5_), channel_id=1, source_target_pairs={{0,1},{1,0},{2,3},{3,2},{4,5},{5,4},{6,7},{7,6},{8,9},{9,8},{10,11... | collective-permute-start | bytes 1769480 | tf_op jit(solution)/shard_map/ppermute | solution.py:311
  46.3 2.7 %collective-permute-start.4 = (bf16[32,8,128]{2,1,0:T(8,128)(2,1)S(1)}, bf16[32,8,128]{2,1,0:T(8,128)(2,1)S(1)}, u32[]{:S(2)}, u32[]{:S(2)}) collective-permute-start(bf16[32,8,128]{2,1,0:T(8,128)(2,1)S(1)} %all_to_all.56.refs_9_.refs_2_.refs_4_), channel_id=1, source_target_pairs={{0,4},{4,0},{8,12},{12,8},{16,20},{20,16},{24,28},{28,24},{32,36},... | collective-permute-start | bytes 196616 | tf_op jit(solution)/shard_map/ppermute | solution.py:286
  61.3 2.5 %collective-permute-start.8 = (bf16[32,8,128]{2,1,0:T(8,128)(2,1)S(1)}, bf16[32,8,128]{2,1,0:T(8,128)(2,1)S(1)}, u32[]{:S(2)}, u32[]{:S(2)}) collective-permute-start(bf16[32,8,128]{2,1,0:T(8,128)(2,1)S(1)} %all_to_all.57.refs_11_.refs_2_.refs_5_), channel_id=1, source_target_pairs={{0,4},{4,0},{8,12},{12,8},{16,20},{20,16},{24,28},{28,24},{32,36},... | collective-permute-start | bytes 196616 | tf_op jit(solution)/shard_map/ppermute | solution.py:286
  76.1 2.5 %collective-permute-start.9 = (bf16[32,8,128]{2,1,0:T(8,128)(2,1)S(1)}, bf16[32,8,128]{2,1,0:T(8,128)(2,1)S(1)}, u32[]{:S(2)}, u32[]{:S(2)}) collective-permute-start(bf16[32,8,128]{2,1,0:T(8,128)(2,1)S(1)} %all_to_all.58.refs_13_.refs_2_.refs_6_), channel_id=1, source_target_pairs={{0,4},{4,0},{8,12},{12,8},{16,20},{20,16},{24,28},{28,24},{32,36},... | collective-permute-start | bytes 196616 | tf_op jit(solution)/shard_map/ppermute | solution.py:286
  90.9 2.5 %collective-permute-start.10 = (bf16[32,8,128]{2,1,0:T(8,128)(2,1)S(1)}, bf16[32,8,128]{2,1,0:T(8,128)(2,1)S(1)}, u32[]{:S(2)}, u32[]{:S(2)}) collective-permute-start(bf16[32,8,128]{2,1,0:T(8,128)(2,1)S(1)} %all_to_all.59.refs_15_.refs_2_.refs_7_), channel_id=1, source_target_pairs={{0,4},{4,0},{8,12},{12,8},{16,20},{20,16},{24,28},{28,24},{32,36},... | collective-permute-start | bytes 196616 | tf_op jit(solution)/shard_map/ppermute | solution.py:286
  94.5 1.3 collective-permute-start.11
  108.1 2.6 %collective-permute-start.12 = (bf16[32,8,128]{2,1,0:T(8,128)(2,1)S(1)}, bf16[32,8,128]{2,1,0:T(8,128)(2,1)S(1)}, u32[]{:S(2)}, u32[]{:S(2)}) collective-permute-start(bf16[32,8,128]{2,1,0:T(8,128)(2,1)S(1)} %get-tuple-element.42), channel_id=1, source_target_pairs={{0,4},{4,0},{8,12},{12,8},{16,20},{20,16},{24,28},{28,24},{32,36},... | collective-permute-start | bytes 196616 | tf_op jit(solution)/shard_map/ppermute | solution.py:286
  122.9 2.8 %collective-permute-start.13 = (bf16[32,8,128]{2,1,0:T(8,128)(2,1)S(1)}, bf16[32,8,128]{2,1,0:T(8,128)(2,1)S(1)}, u32[]{:S(2)}, u32[]{:S(2)}) collective-permute-start(bf16[32,8,128]{2,1,0:T(8,128)(2,1)S(1)} %get-tuple-element.45), channel_id=1, source_target_pairs={{0,4},{4,0},{8,12},{12,8},{16,20},{20,16},{24,28},{28,24},{32,36},... | collective-permute-start | bytes 196616 | tf_op jit(solution)/shard_map/ppermute | solution.py:286
  138.0 2.5 %collective-permute-start.14 = (bf16[32,8,128]{2,1,0:T(8,128)(2,1)S(1)}, bf16[32,8,128]{2,1,0:T(8,128)(2,1)S(1)}, u32[]{:S(2)}, u32[]{:S(2)}) collective-permute-start(bf16[32,8,128]{2,1,0:T(8,128)(2,1)S(1)} %get-tuple-element.48), channel_id=1, source_target_pairs={{0,4},{4,0},{8,12},{12,8},{16,20},{20,16},{24,28},{28,24},{32,36},... | collective-permute-start | bytes 196616 | tf_op jit(solution)/shard_map/ppermute | solution.py:286
  152.9 2.6 %collective-permute-start.15 = (bf16[32,8,128]{2,1,0:T(8,128)(2,1)S(1)}, bf16[32,8,128]{2,1,0:T(8,128)(2,1)S(1)}, u32[]{:S(2)}, u32[]{:S(2)}) collective-permute-start(bf16[32,8,128]{2,1,0:T(8,128)(2,1)S(1)} %get-tuple-element.51), channel_id=1, source_target_pairs={{0,4},{4,0},{8,12},{12,8},{16,20},{20,16},{24,28},{28,24},{32,36},... | collective-permute-start | bytes 196616 | tf_op jit(solution)/shard_map/ppermute | solution.py:286

commit v11 on v10

--- a/solution.py
+++ b/solution.py
@@ -309,7 +309,7 @@
     def around(x):
         return [held(x)] + [
             held(lax.ppermute(x, "col", [(i, i ^ s) for i in range(cols)]))
-            for s in (1, 3, 2)
+            for s in (2, 3, 1)
         ]
 
     factor = far_off(factor.reshape(rows * plan.entries * width, width))

time: 178 us -> 177 us (level)
  no operation moved by 1% of the time
where the time goes in v11:
time: 177 us; the launch traced here: 176 us
  blocking collectives  135 us (76%)
  starting transfers between devices  25.3 us (14%)
  waiting for transfers between devices  8.13 us (5%)
  Pallas kernels  6.73 us (4%)
    all_to_all x10, blocking collectives, among(): lax.all_to_all(x, 'chain', 0, 0, tiled=True, axis_index_groups=groups)  127 us
    ppermute x10, starting transfers between devices, across(): return held(lax.ppermute(x, 'chain', [(i, i ^ 1) for i in range(lanes)]))  17 us
    ppermute x6, starting transfers between devices, around(): lax.ppermute(x, 'col', [(i, i ^ s) for i in range(cols)])  8.33 us
    ppermute x10, waiting for transfers between devices, across(): return held(lax.ppermute(x, 'chain', [(i, i ^ 1) for i in range(lanes)]))  8.11 us
    all_to_all x1, blocking collectives, per_device(): whole = lax.all_to_all(shares, 'col', 0, 0, tiled=True)  7.98 us
  transfers between devices with their start and end apart: 16, of which 9 were waited for; matrix products, arithmetic and copies ran while one was open for 0% of the time, Pallas kernels for 1%

profile of v11, /device:TPU:1, one launch (start us, length us, event | category | flops | bytes accessed | tf_op | source)
XLA Modules:
  0.0 176.1 jit_solution(1925337253818426472)
XLA Ops:
  0.6 1.3 forward_first.1
  2.0 2.1 %collective-permute-start.3 = (bf16[1552,128]{1,0:T(8,128)(2,1)S(1)}, bf16[1552,128]{1,0:T(8,128)(2,1)S(1)}, u32[]{:S(2)}, u32[]{:S(2)}) collective-permute-start(bf16[1552,128]{1,0:T(8,128)(2,1)S(1)} %get-tuple-element.34.refs_5_.refs_3_), channel_id=1, source_target_pairs={{0,1},{1,0},{2,3},{3,2},{4,5},{5,4},{6,7},{7,6},{8,9},{9,8},{10,11... | collective-permute-start | bytes 1191944 | tf_op jit(solution)/shard_map/ppermute | solution.py:311
  4.1 1.8 %collective-permute-start.2 = (bf16[1552,128]{1,0:T(8,128)(2,1)S(1)}, bf16[1552,128]{1,0:T(8,128)(2,1)S(1)}, u32[]{:S(2)}, u32[]{:S(2)}) collective-permute-start(bf16[1552,128]{1,0:T(8,128)(2,1)S(1)} %get-tuple-element.34.refs_5_.refs_3_), channel_id=1, source_target_pairs={{0,3},{1,2},{2,1},{3,0},{4,7},{5,6},{6,5},{7,4},{8,11},{9,10},{10,... | collective-permute-start | bytes 1191944 | tf_op jit(solution)/shard_map/ppermute | solution.py:311
  6.6 19.8 %all_to_all.55.refs_3_.refs_7_.segment = bf16[32,8,128]{2,1,0:T(8,128)(2,1)S(1)} all-to-all(bf16[32,8,128]{2,1,0:T(8,128)(2,1)S(1)} %get-tuple-element.33), channel_id=1, replica_groups={{0,8,16,24,32,40,48,56,64,72,80,88,96,104,112,120,128,136,144,152,160,1..., dimensions={0} | all-to-all | bytes 131072 | tf_op jit(solution)/shard_map/all_to_all | solution.py:291
  26.4 2.7 %collective-permute-start = (bf16[32,8,128]{2,1,0:T(8,128)(2,1)S(1)}, bf16[32,8,128]{2,1,0:T(8,128)(2,1)S(1)}, u32[]{:S(2)}, u32[]{:S(2)}) collective-permute-start(bf16[32,8,128]{2,1,0:T(8,128)(2,1)S(1)} %all_to_all.55.refs_3_.refs_7_.segment), channel_id=1, source_target_pairs={{0,4},{4,0},{8,12},{12,8},{16,20},{20,16},{24,28},{28,24},{32,36},... | collective-permute-start | bytes 196616 | tf_op jit(solution)/shard_map/ppermute | solution.py:286
  29.1 1.1 collective-permute-start.7
  30.1 2.2 %collective-permute-start.6 = (bf16[2304,128]{1,0:T(8,128)(2,1)S(1)}, bf16[2304,128]{1,0:T(8,128)(2,1)S(1)}, u32[]{:S(2)}, u32[]{:S(2)}) collective-permute-start(bf16[2304,128]{1,0:T(8,128)(2,1)S(1)} %after.1.refs_3_.refs_5_), channel_id=1, source_target_pairs={{0,3},{1,2},{2,1},{3,0},{4,7},{5,6},{6,5},{7,4},{8,11},{9,10},{10,... | collective-permute-start | bytes 1769480 | tf_op jit(solution)/shard_map/ppermute | solution.py:311
  32.8 1.2 forward_second.1
  34.1 11.8 %all_to_all.56.refs_9_.refs_2_.refs_4_ = bf16[32,8,128]{2,1,0:T(8,128)(2,1)S(1)} all-to-all(bf16[32,8,128]{2,1,0:T(8,128)(2,1)S(1)} %get-tuple-element.36), channel_id=1, replica_groups={{0,8,16,24,32,40,48,56,64,72,80,88,96,104,112,120,128,136,144,152,160,1..., dimensions={0} | all-to-all | bytes 131072 | tf_op jit(solution)/shard_map/all_to_all | solution.py:291
  45.9 2.2 %collective-permute-start.4 = (bf16[32,8,128]{2,1,0:T(8,128)(2,1)S(1)}, bf16[32,8,128]{2,1,0:T(8,128)(2,1)S(1)}, u32[]{:S(2)}, u32[]{:S(2)}) collective-permute-start(bf16[32,8,128]{2,1,0:T(8,128)(2,1)S(1)} %all_to_all.56.refs_9_.refs_2_.refs_4_), channel_id=1, source_target_pairs={{0,4},{4,0},{8,12},{12,8},{16,20},{20,16},{24,28},{28,24},{32,36},... | collective-permute-start | bytes 196616 | tf_op jit(solution)/shard_map/ppermute | solution.py:286
  48.0 0.9 collective-permute-done.4.refs_10_
  49.3 11.9 %all_to_all.57.refs_11_.refs_2_.refs_5_ = bf16[32,8,128]{2,1,0:T(8,128)(2,1)S(1)} all-to-all(bf16[32,8,128]{2,1,0:T(8,128)(2,1)S(1)} %forward_level_2.1), channel_id=1, replica_groups={{0,8,16,24,32,40,48,56,64,72,80,88,96,104,112,120,128,136,144,152,160,1..., dimensions={0} | all-to-all | bytes 131072 | tf_op jit(solution)/shard_map/all_to_all | solution.py:291
  61.3 1.6 collective-permute-start.8
  64.2 11.9 %all_to_all.58.refs_13_.refs_2_.refs_6_ = bf16[32,8,128]{2,1,0:T(8,128)(2,1)S(1)} all-to-all(bf16[32,8,128]{2,1,0:T(8,128)(2,1)S(1)} %forward_level_3.1), channel_id=1, replica_groups={{0,8,16,24,32,40,48,56,64,72,80,88,96,104,112,120,128,136,144,152,160,1..., dimensions={0} | all-to-all | bytes 131072 | tf_op jit(solution)/shard_map/all_to_all | solution.py:291
  76.1 1.6 collective-permute-start.9
  77.7 0.9 collective-permute-done.9.refs_14_
  79.0 11.9 %all_to_all.59.refs_15_.refs_2_.refs_7_ = bf16[32,8,128]{2,1,0:T(8,128)(2,1)S(1)} all-to-all(bf16[32,8,128]{2,1,0:T(8,128)(2,1)S(1)} %forward_level_4.1), channel_id=1, replica_groups={{0,8,16,24,32,40,48,56,64,72,80,88,96,104,112,120,128,136,144,152,160,1..., dimensions={0} | all-to-all | bytes 131072 | tf_op jit(solution)/shard_map/all_to_all | solution.py:291
  90.9 1.6 collective-permute-start.10
  92.5 0.9 collective-permute-done.10.refs_16_
  93.4 1.0 turn_level.1
  94.9 0.9 collective-permute-done.11.other
  95.8 11.8 %all_to_all.60.refs_3_ = bf16[32,8,128]{2,1,0:T(8,128)(2,1)S(1)} all-to-all(bf16[32,8,128]{2,1,0:T(8,128)(2,1)S(1)} %add_other.5), channel_id=1, replica_groups={{0,8,16,24,32,40,48,56,64,72,80,88,96,104,112,120,128,136,144,152,160,1..., dimensions={0} | all-to-all | bytes 131072 | tf_op jit(solution)/shard_map/all_to_all | solution.py:291
  108.1 1.7 collective-permute-start.12
  109.8 0.9 collective-permute-done.12.other
  110.7 11.8 %all_to_all.61.refs_3_ = bf16[32,8,128]{2,1,0:T(8,128)(2,1)S(1)} all-to-all(bf16[32,8,128]{2,1,0:T(8,128)(2,1)S(1)} %add_other.6), channel_id=1, replica_groups={{0,8,16,24,32,40,48,56,64,72,80,88,96,104,112,120,128,136,144,152,160,1..., dimensions={0} | all-to-all | bytes 131072 | tf_op jit(solution)/shard_map/all_to_all | solution.py:291
  122.9 1.8 %collective-permute-start.13 = (bf16[32,8,128]{2,1,0:T(8,128)(2,1)S(1)}, bf16[32,8,128]{2,1,0:T(8,128)(2,1)S(1)}, u32[]{:S(2)}, u32[]{:S(2)}) collective-permute-start(bf16[32,8,128]{2,1,0:T(8,128)(2,1)S(1)} %get-tuple-element.45), channel_id=1, source_target_pairs={{0,4},{4,0},{8,12},{12,8},{16,20},{20,16},{24,28},{28,24},{32,36},... | collective-permute-start | bytes 196616 | tf_op jit(solution)/shard_map/ppermute | solution.py:286
  125.7 11.8 %all_to_all.62.refs_3_ = bf16[32,8,128]{2,1,0:T(8,128)(2,1)S(1)} all-to-all(bf16[32,8,128]{2,1,0:T(8,128)(2,1)S(1)} %add_other.7), channel_id=1, replica_groups={{0,8,16,24,32,40,48,56,64,72,80,88,96,104,112,120,128,136,144,152,160,1..., dimensions={0} | all-to-all | bytes 131072 | tf_op jit(solution)/shard_map/all_to_all | solution.py:291
  138.0 1.7 collective-permute-start.14
  140.6 11.8 %all_to_all.63.refs_3_ = bf16[32,8,128]{2,1,0:T(8,128)(2,1)S(1)} all-to-all(bf16[32,8,128]{2,1,0:T(8,128)(2,1)S(1)} %add_other.8), channel_id=1, replica_groups={{0,8,16,24,32,40,48,56,64,72,80,88,96,104,112,120,128,136,144,152,160,1..., dimensions={0} | all-to-all | bytes 131072 | tf_op jit(solution)/shard_map/all_to_all | solution.py:291
  152.8 1.7 collective-permute-start.15
  155.4 11.8 %all_to_all.64.refs_2_ = bf16[32,8,128]{2,1,0:T(8,128)(2,1)S(1)} all-to-all(bf16[32,8,128]{2,1,0:T(8,128)(2,1)S(1)} %add_other.9), channel_id=1, replica_groups={{0,8,16,24,32,40,48,56,64,72,80,88,96,104,112,120,128,136,144,152,160,1..., dimensions={0} | all-to-all | bytes 131072 | tf_op jit(solution)/shard_map/all_to_all | solution.py:291
  167.4 8.0 %all_to_all.65 = bf16[4,8,8,128]{3,2,1,0:T(8,128)(2,1)S(1)} all-to-all(bf16[4,8,8,128]{3,2,1,0:T(8,128)(2,1)S(1)} %finish.1), channel_id=1, replica_groups=mesh['chain'=64,'col'=4] {'col'}, dimensions={0} | all-to-all | bytes 131072 | tf_op jit(solution)/shard_map/all_to_all | solution.py:436
  (30 shorter events, 9.0 us)
Async XLA Ops:
  2.0 30.3 %collective-permute-start.3 = (bf16[1552,128]{1,0:T(8,128)(2,1)S(1)}, bf16[1552,128]{1,0:T(8,128)(2,1)S(1)}, u32[]{:S(2)}, u32[]{:S(2)}) collective-permute-start(bf16[1552,128]{1,0:T(8,128)(2,1)S(1)} %get-tuple-element.34.refs_5_.refs_3_), channel_id=1, source_target_pairs={{0,1},{1,0},{2,3},{3,2},{4,5},{5,4},{6,7},{7,6},{8,9},{9,8},{10,11... | collective-permute-start | bytes 1191944 | tf_op jit(solution)/shard_map/ppermute | solution.py:311
  4.1 28.7 %collective-permute-start.2 = (bf16[1552,128]{1,0:T(8,128)(2,1)S(1)}, bf16[1552,128]{1,0:T(8,128)(2,1)S(1)}, u32[]{:S(2)}, u32[]{:S(2)}) collective-permute-start(bf16[1552,128]{1,0:T(8,128)(2,1)S(1)} %get-tuple-element.34.refs_5_.refs_3_), channel_id=1, source_target_pairs={{0,3},{1,2},{2,1},{3,0},{4,7},{5,6},{6,5},{7,4},{8,11},{9,10},{10,... | collective-permute-start | bytes 1191944 | tf_op jit(solution)/shard_map/ppermute | solution.py:311
  5.9 26.9 %collective-permute-start.1 = (bf16[1552,128]{1,0:T(8,128)(2,1)S(1)}, bf16[1552,128]{1,0:T(8,128)(2,1)S(1)}, u32[]{:S(2)}, u32[]{:S(2)}) collective-permute-start(bf16[1552,128]{1,0:T(8,128)(2,1)S(1)} %get-tuple-element.34.refs_5_.refs_3_), channel_id=1, source_target_pairs={{0,2},{1,3},{2,0},{3,1},{4,6},{5,7},{6,4},{7,5},{8,10},{9,11},{10,... | collective-permute-start | bytes 1191944 | tf_op jit(solution)/shard_map/ppermute | solution.py:311
  26.4 3.7 %collective-permute-start = (bf16[32,8,128]{2,1,0:T(8,128)(2,1)S(1)}, bf16[32,8,128]{2,1,0:T(8,128)(2,1)S(1)}, u32[]{:S(2)}, u32[]{:S(2)}) collective-permute-start(bf16[32,8,128]{2,1,0:T(8,128)(2,1)S(1)} %all_to_all.55.refs_3_.refs_7_.segment), channel_id=1, source_target_pairs={{0,4},{4,0},{8,12},{12,8},{16,20},{20,16},{24,28},{28,24},{32,36},... | collective-permute-start | bytes 196616 | tf_op jit(solution)/shard_map/ppermute | solution.py:286
  29.1 33.8 %collective-permute-start.7 = (bf16[2304,128]{1,0:T(8,128)(2,1)S(1)}, bf16[2304,128]{1,0:T(8,128)(2,1)S(1)}, u32[]{:S(2)}, u32[]{:S(2)}) collective-permute-start(bf16[2304,128]{1,0:T(8,128)(2,1)S(1)} %after.1.refs_3_.refs_5_), channel_id=1, source_target_pairs={{0,1},{1,0},{2,3},{3,2},{4,5},{5,4},{6,7},{7,6},{8,9},{9,8},{10,11... | collective-permute-start | bytes 1769480 | tf_op jit(solution)/shard_map/ppermute | solution.py:311
  30.1 32.7 %collective-permute-start.6 = (bf16[2304,128]{1,0:T(8,128)(2,1)S(1)}, bf16[2304,128]{1,0:T(8,128)(2,1)S(1)}, u32[]{:S(2)}, u32[]{:S(2)}) collective-permute-start(bf16[2304,128]{1,0:T(8,128)(2,1)S(1)} %after.1.refs_3_.refs_5_), channel_id=1, source_target_pairs={{0,3},{1,2},{2,1},{3,0},{4,7},{5,6},{6,5},{7,4},{8,11},{9,10},{10,... | collective-permute-start | bytes 1769480 | tf_op jit(solution)/shard_map/ppermute | solution.py:311
  32.3 30.6 %collective-permute-start.5 = (bf16[2304,128]{1,0:T(8,128)(2,1)S(1)}, bf16[2304,128]{1,0:T(8,128)(2,1)S(1)}, u32[]{:S(2)}, u32[]{:S(2)}) collective-permute-start(bf16[2304,128]{1,0:T(8,128)(2,1)S(1)} %after.1.refs_3_.refs_5_), channel_id=1, source_target_pairs={{0,2},{1,3},{2,0},{3,1},{4,6},{5,7},{6,4},{7,5},{8,10},{9,11},{10,... | collective-permute-start | bytes 1769480 | tf_op jit(solution)/shard_map/ppermute | solution.py:311
  45.9 3.1 %collective-permute-start.4 = (bf16[32,8,128]{2,1,0:T(8,128)(2,1)S(1)}, bf16[32,8,128]{2,1,0:T(8,128)(2,1)S(1)}, u32[]{:S(2)}, u32[]{:S(2)}) collective-permute-start(bf16[32,8,128]{2,1,0:T(8,128)(2,1)S(1)} %all_to_all.56.refs_9_.refs_2_.refs_4_), channel_id=1, source_target_pairs={{0,4},{4,0},{8,12},{12,8},{16,20},{20,16},{24,28},{28,24},{32,36},... | collective-permute-start | bytes 196616 | tf_op jit(solution)/shard_map/ppermute | solution.py:286
  61.3 2.5 %collective-permute-start.8 = (bf16[32,8,128]{2,1,0:T(8,128)(2,1)S(1)}, bf16[32,8,128]{2,1,0:T(8,128)(2,1)S(1)}, u32[]{:S(2)}, u32[]{:S(2)}) collective-permute-start(bf16[32,8,128]{2,1,0:T(8,128)(2,1)S(1)} %all_to_all.57.refs_11_.refs_2_.refs_5_), channel_id=1, source_target_pairs={{0,4},{4,0},{8,12},{12,8},{16,20},{20,16},{24,28},{28,24},{32,36},... | collective-permute-start | bytes 196616 | tf_op jit(solution)/shard_map/ppermute | solution.py:286
  76.1 2.5 %collective-permute-start.9 = (bf16[32,8,128]{2,1,0:T(8,128)(2,1)S(1)}, bf16[32,8,128]{2,1,0:T(8,128)(2,1)S(1)}, u32[]{:S(2)}, u32[]{:S(2)}) collective-permute-start(bf16[32,8,128]{2,1,0:T(8,128)(2,1)S(1)} %all_to_all.58.refs_13_.refs_2_.refs_6_), channel_id=1, source_target_pairs={{0,4},{4,0},{8,12},{12,8},{16,20},{20,16},{24,28},{28,24},{32,36},... | collective-permute-start | bytes 196616 | tf_op jit(solution)/shard_map/ppermute | solution.py:286
  90.9 2.5 %collective-permute-start.10 = (bf16[32,8,128]{2,1,0:T(8,128)(2,1)S(1)}, bf16[32,8,128]{2,1,0:T(8,128)(2,1)S(1)}, u32[]{:S(2)}, u32[]{:S(2)}) collective-permute-start(bf16[32,8,128]{2,1,0:T(8,128)(2,1)S(1)} %all_to_all.59.refs_15_.refs_2_.refs_7_), channel_id=1, source_target_pairs={{0,4},{4,0},{8,12},{12,8},{16,20},{20,16},{24,28},{28,24},{32,36},... | collective-permute-start | bytes 196616 | tf_op jit(solution)/shard_map/ppermute | solution.py:286
  94.4 1.3 collective-permute-start.11
  108.1 2.6 %collective-permute-start.12 = (bf16[32,8,128]{2,1,0:T(8,128)(2,1)S(1)}, bf16[32,8,128]{2,1,0:T(8,128)(2,1)S(1)}, u32[]{:S(2)}, u32[]{:S(2)}) collective-permute-start(bf16[32,8,128]{2,1,0:T(8,128)(2,1)S(1)} %get-tuple-element.42), channel_id=1, source_target_pairs={{0,4},{4,0},{8,12},{12,8},{16,20},{20,16},{24,28},{28,24},{32,36},... | collective-permute-start | bytes 196616 | tf_op jit(solution)/shard_map/ppermute | solution.py:286
  122.9 2.7 %collective-permute-start.13 = (bf16[32,8,128]{2,1,0:T(8,128)(2,1)S(1)}, bf16[32,8,128]{2,1,0:T(8,128)(2,1)S(1)}, u32[]{:S(2)}, u32[]{:S(2)}) collective-permute-start(bf16[32,8,128]{2,1,0:T(8,128)(2,1)S(1)} %get-tuple-element.45), channel_id=1, source_target_pairs={{0,4},{4,0},{8,12},{12,8},{16,20},{20,16},{24,28},{28,24},{32,36},... | collective-permute-start | bytes 196616 | tf_op jit(solution)/shard_map/ppermute | solution.py:286
  138.0 2.6 %collective-permute-start.14 = (bf16[32,8,128]{2,1,0:T(8,128)(2,1)S(1)}, bf16[32,8,128]{2,1,0:T(8,128)(2,1)S(1)}, u32[]{:S(2)}, u32[]{:S(2)}) collective-permute-start(bf16[32,8,128]{2,1,0:T(8,128)(2,1)S(1)} %get-tuple-element.48), channel_id=1, source_target_pairs={{0,4},{4,0},{8,12},{12,8},{16,20},{20,16},{24,28},{28,24},{32,36},... | collective-permute-start | bytes 196616 | tf_op jit(solution)/shard_map/ppermute | solution.py:286
  152.8 2.6 %collective-permute-start.15 = (bf16[32,8,128]{2,1,0:T(8,128)(2,1)S(1)}, bf16[32,8,128]{2,1,0:T(8,128)(2,1)S(1)}, u32[]{:S(2)}, u32[]{:S(2)}) collective-permute-start(bf16[32,8,128]{2,1,0:T(8,128)(2,1)S(1)} %get-tuple-element.51), channel_id=1, source_target_pairs={{0,4},{4,0},{8,12},{12,8},{16,20},{20,16},{24,28},{28,24},{32,36},... | collective-permute-start | bytes 196616 | tf_op jit(solution)/shard_map/ppermute | solution.py:286

commit v12 on v11

--- a/solution.py
+++ b/solution.py
@@ -199,13 +199,17 @@
     out[...] = jnp.broadcast_to(segment[None], out.shape)
 
 
+def clear(front, acc):
+    acc[...] = jnp.zeros(acc.shape, F32)
+
+
 def turn_level(plan, level, *refs):
     table, right, inverse = refs[:3]
     sources = refs[3 : 3 + plan.cols]
     earlier = refs[3 + plan.cols : 3 + plan.cols + PAIR * level]
+    refs = refs[1:]
     half, solved, acc, own, other, store = refs[3 + plan.cols + PAIR * level :]
     gather_store(plan, level, earlier, store)
-    acc[...] = jnp.zeros(acc.shape, F32)
     segment = half_segment(plan, level, table, right, inverse, sources, store)
     half[...] = segment
     segment = lax.dot_general(
@@ -393,15 +397,24 @@
 
     last = levels - 1
     acc_shape = pltpu.VMEM((last * lanes + 1, share, width), F32)
+    cleared = pl.pallas_call(
+        clear,
+        out_shape=acc_shape,
+        in_specs=[vmem],
+        out_specs=vmem,
+        compiler_params=params,
+        name="clear",
+    )(fronts[PAIR * (last - 1)])
     half_last, solved, acc, *terms = pl.pallas_call(
         functools.partial(turn_level, plan, last),
         out_shape=(segment_shape, segment_shape, acc_shape, own_shape, front_shape),
-        in_specs=[smem] + [vmem] * (2 + cols + PAIR * last),
+        in_specs=[smem] + [vmem] * (3 + cols + PAIR * last),
         out_specs=(vmem,) * 5,
+        input_output_aliases={3 + cols + PAIR * last: 2},
         scratch_shapes=[store(last)],
         compiler_params=params,
         name="turn_level",
-    )(table, rights, inverses, *sources(last), *fronts)
+    )(table, rights, inverses, *sources(last), *fronts, held(cleared))
     done = [held(solved)]
     for k in range(last - 1, 0, -1):
         solved, acc, *terms = pl.pallas_call(

time: 177 us -> 177 us (level)
  no operation moved by 1% of the time
where the time goes in v12:
time: 177 us; the launch traced here: 176 us
  blocking collectives  135 us (76%)
  starting transfers between devices  25.3 us (14%)
  waiting for transfers between devices  8.04 us (5%)
  Pallas kernels  6.84 us (4%)
    all_to_all x10, blocking collectives, among(): lax.all_to_all(x, 'chain', 0, 0, tiled=True, axis_index_groups=groups)  127 us
    ppermute x10, starting transfers between devices, across(): return held(lax.ppermute(x, 'chain', [(i, i ^ 1) for i in range(lanes)]))  16.9 us
    ppermute x6, starting transfers between devices, around(): lax.ppermute(x, 'col', [(i, i ^ s) for i in range(cols)])  8.33 us
    ppermute x10, waiting for transfers between devices, across(): return held(lax.ppermute(x, 'chain', [(i, i ^ 1) for i in range(lanes)]))  8.02 us
    all_to_all x1, blocking collectives, per_device(): whole = lax.all_to_all(shares, 'col', 0, 0, tiled=True)  7.98 us
  transfers between devices with their start and end apart: 16, of which 9 were waited for; matrix products, arithmetic and copies ran while one was open for 0% of the time, Pallas kernels for 1%

profile of v12, /device:TPU:1, one launch (start us, length us, event | category | flops | bytes accessed | tf_op | source)
XLA Modules:
  0.0 176.0 jit_solution(10346479422968510805)
XLA Ops:
  0.6 1.3 forward_first.1
  2.0 2.1 %collective-permute-start.3 = (bf16[1552,128]{1,0:T(8,128)(2,1)S(1)}, bf16[1552,128]{1,0:T(8,128)(2,1)S(1)}, u32[]{:S(2)}, u32[]{:S(2)}) collective-permute-start(bf16[1552,128]{1,0:T(8,128)(2,1)S(1)} %get-tuple-element.34.refs_5_.refs_3_), channel_id=1, source_target_pairs={{0,1},{1,0},{2,3},{3,2},{4,5},{5,4},{6,7},{7,6},{8,9},{9,8},{10,11... | collective-permute-start | bytes 1191944 | tf_op jit(solution)/shard_map/ppermute | solution.py:315
  4.1 1.8 %collective-permute-start.2 = (bf16[1552,128]{1,0:T(8,128)(2,1)S(1)}, bf16[1552,128]{1,0:T(8,128)(2,1)S(1)}, u32[]{:S(2)}, u32[]{:S(2)}) collective-permute-start(bf16[1552,128]{1,0:T(8,128)(2,1)S(1)} %get-tuple-element.34.refs_5_.refs_3_), channel_id=1, source_target_pairs={{0,3},{1,2},{2,1},{3,0},{4,7},{5,6},{6,5},{7,4},{8,11},{9,10},{10,... | collective-permute-start | bytes 1191944 | tf_op jit(solution)/shard_map/ppermute | solution.py:315
  6.6 19.8 %all_to_all.55.refs_3_.refs_7_.segment = bf16[32,8,128]{2,1,0:T(8,128)(2,1)S(1)} all-to-all(bf16[32,8,128]{2,1,0:T(8,128)(2,1)S(1)} %get-tuple-element.33), channel_id=1, replica_groups={{0,8,16,24,32,40,48,56,64,72,80,88,96,104,112,120,128,136,144,152,160,1..., dimensions={0} | all-to-all | bytes 131072 | tf_op jit(solution)/shard_map/all_to_all | solution.py:295
  26.4 2.7 %collective-permute-start = (bf16[32,8,128]{2,1,0:T(8,128)(2,1)S(1)}, bf16[32,8,128]{2,1,0:T(8,128)(2,1)S(1)}, u32[]{:S(2)}, u32[]{:S(2)}) collective-permute-start(bf16[32,8,128]{2,1,0:T(8,128)(2,1)S(1)} %all_to_all.55.refs_3_.refs_7_.segment), channel_id=1, source_target_pairs={{0,4},{4,0},{8,12},{12,8},{16,20},{20,16},{24,28},{28,24},{32,36},... | collective-permute-start | bytes 196616 | tf_op jit(solution)/shard_map/ppermute | solution.py:290
  29.1 1.1 collective-permute-start.7
  30.1 2.2 %collective-permute-start.6 = (bf16[2304,128]{1,0:T(8,128)(2,1)S(1)}, bf16[2304,128]{1,0:T(8,128)(2,1)S(1)}, u32[]{:S(2)}, u32[]{:S(2)}) collective-permute-start(bf16[2304,128]{1,0:T(8,128)(2,1)S(1)} %after.1.refs_3_.refs_5_), channel_id=1, source_target_pairs={{0,3},{1,2},{2,1},{3,0},{4,7},{5,6},{6,5},{7,4},{8,11},{9,10},{10,... | collective-permute-start | bytes 1769480 | tf_op jit(solution)/shard_map/ppermute | solution.py:315
  32.8 1.2 forward_second.1
  34.1 11.8 %all_to_all.56.refs_9_.refs_2_.refs_4_ = bf16[32,8,128]{2,1,0:T(8,128)(2,1)S(1)} all-to-all(bf16[32,8,128]{2,1,0:T(8,128)(2,1)S(1)} %get-tuple-element.36), channel_id=1, replica_groups={{0,8,16,24,32,40,48,56,64,72,80,88,96,104,112,120,128,136,144,152,160,1..., dimensions={0} | all-to-all | bytes 131072 | tf_op jit(solution)/shard_map/all_to_all | solution.py:295
  45.9 2.2 %collective-permute-start.4 = (bf16[32,8,128]{2,1,0:T(8,128)(2,1)S(1)}, bf16[32,8,128]{2,1,0:T(8,128)(2,1)S(1)}, u32[]{:S(2)}, u32[]{:S(2)}) collective-permute-start(bf16[32,8,128]{2,1,0:T(8,128)(2,1)S(1)} %all_to_all.56.refs_9_.refs_2_.refs_4_), channel_id=1, source_target_pairs={{0,4},{4,0},{8,12},{12,8},{16,20},{20,16},{24,28},{28,24},{32,36},... | collective-permute-start | bytes 196616 | tf_op jit(solution)/shard_map/ppermute | solution.py:290
  48.0 0.9 collective-permute-done.4.refs_10_
  49.4 11.9 %all_to_all.57.refs_11_.refs_2_.refs_5_ = bf16[32,8,128]{2,1,0:T(8,128)(2,1)S(1)} all-to-all(bf16[32,8,128]{2,1,0:T(8,128)(2,1)S(1)} %forward_level_2.1), channel_id=1, replica_groups={{0,8,16,24,32,40,48,56,64,72,80,88,96,104,112,120,128,136,144,152,160,1..., dimensions={0} | all-to-all | bytes 131072 | tf_op jit(solution)/shard_map/all_to_all | solution.py:295
  61.3 1.6 collective-permute-start.8
  64.2 11.9 %all_to_all.58.refs_13_.refs_2_.refs_6_ = bf16[32,8,128]{2,1,0:T(8,128)(2,1)S(1)} all-to-all(bf16[32,8,128]{2,1,0:T(8,128)(2,1)S(1)} %forward_level_3.1), channel_id=1, replica_groups={{0,8,16,24,32,40,48,56,64,72,80,88,96,104,112,120,128,136,144,152,160,1..., dimensions={0} | all-to-all | bytes 131072 | tf_op jit(solution)/shard_map/all_to_all | solution.py:295
  76.1 1.6 collective-permute-start.9
  77.7 0.9 collective-permute-done.9.refs_14_
  79.0 11.9 %all_to_all.59.front.refs_15_.refs_2_.refs_7_ = bf16[32,8,128]{2,1,0:T(8,128)(2,1)S(1)} all-to-all(bf16[32,8,128]{2,1,0:T(8,128)(2,1)S(1)} %forward_level_4.1), channel_id=1, replica_groups={{0,8,16,24,32,40,48,56,64,72,80,88,96,104,112,120,128,136,144,152,160,1..., dimensions={0} | all-to-all | bytes 131072 | tf_op jit(solution)/shard_map/all_to_all | solution.py:295
  90.9 1.6 collective-permute-start.10
  93.4 1.0 turn_level.1
  94.8 0.9 collective-permute-done.11.other
  95.8 11.8 %all_to_all.60.refs_3_ = bf16[32,8,128]{2,1,0:T(8,128)(2,1)S(1)} all-to-all(bf16[32,8,128]{2,1,0:T(8,128)(2,1)S(1)} %add_other.5), channel_id=1, replica_groups={{0,8,16,24,32,40,48,56,64,72,80,88,96,104,112,120,128,136,144,152,160,1..., dimensions={0} | all-to-all | bytes 131072 | tf_op jit(solution)/shard_map/all_to_all | solution.py:295
  108.1 1.7 collective-permute-start.12
  109.7 0.9 collective-permute-done.12.other
  110.7 11.8 %all_to_all.61.refs_3_ = bf16[32,8,128]{2,1,0:T(8,128)(2,1)S(1)} all-to-all(bf16[32,8,128]{2,1,0:T(8,128)(2,1)S(1)} %add_other.6), channel_id=1, replica_groups={{0,8,16,24,32,40,48,56,64,72,80,88,96,104,112,120,128,136,144,152,160,1..., dimensions={0} | all-to-all | bytes 131072 | tf_op jit(solution)/shard_map/all_to_all | solution.py:295
  122.9 1.8 %collective-permute-start.13 = (bf16[32,8,128]{2,1,0:T(8,128)(2,1)S(1)}, bf16[32,8,128]{2,1,0:T(8,128)(2,1)S(1)}, u32[]{:S(2)}, u32[]{:S(2)}) collective-permute-start(bf16[32,8,128]{2,1,0:T(8,128)(2,1)S(1)} %get-tuple-element.45), channel_id=1, source_target_pairs={{0,4},{4,0},{8,12},{12,8},{16,20},{20,16},{24,28},{28,24},{32,36},... | collective-permute-start | bytes 196616 | tf_op jit(solution)/shard_map/ppermute | solution.py:290
  124.7 0.9 collective-permute-done.13.other
  125.6 11.8 %all_to_all.62.refs_3_ = bf16[32,8,128]{2,1,0:T(8,128)(2,1)S(1)} all-to-all(bf16[32,8,128]{2,1,0:T(8,128)(2,1)S(1)} %add_other.7), channel_id=1, replica_groups={{0,8,16,24,32,40,48,56,64,72,80,88,96,104,112,120,128,136,144,152,160,1..., dimensions={0} | all-to-all | bytes 131072 | tf_op jit(solution)/shard_map/all_to_all | solution.py:295
  137.9 1.7 collective-permute-start.14
  140.6 11.8 %all_to_all.63.refs_3_ = bf16[32,8,128]{2,1,0:T(8,128)(2,1)S(1)} all-to-all(bf16[32,8,128]{2,1,0:T(8,128)(2,1)S(1)} %add_other.8), channel_id=1, replica_groups={{0,8,16,24,32,40,48,56,64,72,80,88,96,104,112,120,128,136,144,152,160,1..., dimensions={0} | all-to-all | bytes 131072 | tf_op jit(solution)/shard_map/all_to_all | solution.py:295
  152.8 1.7 collective-permute-start.15
  155.4 11.8 %all_to_all.64.refs_2_ = bf16[32,8,128]{2,1,0:T(8,128)(2,1)S(1)} all-to-all(bf16[32,8,128]{2,1,0:T(8,128)(2,1)S(1)} %add_other.9), channel_id=1, replica_groups={{0,8,16,24,32,40,48,56,64,72,80,88,96,104,112,120,128,136,144,152,160,1..., dimensions={0} | all-to-all | bytes 131072 | tf_op jit(solution)/shard_map/all_to_all | solution.py:295
  167.4 8.0 %all_to_all.65 = bf16[4,8,8,128]{3,2,1,0:T(8,128)(2,1)S(1)} all-to-all(bf16[4,8,8,128]{3,2,1,0:T(8,128)(2,1)S(1)} %finish.1), channel_id=1, replica_groups=mesh['chain'=64,'col'=4] {'col'}, dimensions={0} | all-to-all | bytes 131072 | tf_op jit(solution)/shard_map/all_to_all | solution.py:449
  (31 shorter events, 9.0 us)
Async XLA Ops:
  2.0 30.3 %collective-permute-start.3 = (bf16[1552,128]{1,0:T(8,128)(2,1)S(1)}, bf16[1552,128]{1,0:T(8,128)(2,1)S(1)}, u32[]{:S(2)}, u32[]{:S(2)}) collective-permute-start(bf16[1552,128]{1,0:T(8,128)(2,1)S(1)} %get-tuple-element.34.refs_5_.refs_3_), channel_id=1, source_target_pairs={{0,1},{1,0},{2,3},{3,2},{4,5},{5,4},{6,7},{7,6},{8,9},{9,8},{10,11... | collective-permute-start | bytes 1191944 | tf_op jit(solution)/shard_map/ppermute | solution.py:315
  4.1 28.7 %collective-permute-start.2 = (bf16[1552,128]{1,0:T(8,128)(2,1)S(1)}, bf16[1552,128]{1,0:T(8,128)(2,1)S(1)}, u32[]{:S(2)}, u32[]{:S(2)}) collective-permute-start(bf16[1552,128]{1,0:T(8,128)(2,1)S(1)} %get-tuple-element.34.refs_5_.refs_3_), channel_id=1, source_target_pairs={{0,3},{1,2},{2,1},{3,0},{4,7},{5,6},{6,5},{7,4},{8,11},{9,10},{10,... | collective-permute-start | bytes 1191944 | tf_op jit(solution)/shard_map/ppermute | solution.py:315
  5.9 26.9 %collective-permute-start.1 = (bf16[1552,128]{1,0:T(8,128)(2,1)S(1)}, bf16[1552,128]{1,0:T(8,128)(2,1)S(1)}, u32[]{:S(2)}, u32[]{:S(2)}) collective-permute-start(bf16[1552,128]{1,0:T(8,128)(2,1)S(1)} %get-tuple-element.34.refs_5_.refs_3_), channel_id=1, source_target_pairs={{0,2},{1,3},{2,0},{3,1},{4,6},{5,7},{6,4},{7,5},{8,10},{9,11},{10,... | collective-permute-start | bytes 1191944 | tf_op jit(solution)/shard_map/ppermute | solution.py:315
  26.4 3.7 %collective-permute-start = (bf16[32,8,128]{2,1,0:T(8,128)(2,1)S(1)}, bf16[32,8,128]{2,1,0:T(8,128)(2,1)S(1)}, u32[]{:S(2)}, u32[]{:S(2)}) collective-permute-start(bf16[32,8,128]{2,1,0:T(8,128)(2,1)S(1)} %all_to_all.55.refs_3_.refs_7_.segment), channel_id=1, source_target_pairs={{0,4},{4,0},{8,12},{12,8},{16,20},{20,16},{24,28},{28,24},{32,36},... | collective-permute-start | bytes 196616 | tf_op jit(solution)/shard_map/ppermute | solution.py:290
  29.1 33.8 %collective-permute-start.7 = (bf16[2304,128]{1,0:T(8,128)(2,1)S(1)}, bf16[2304,128]{1,0:T(8,128)(2,1)S(1)}, u32[]{:S(2)}, u32[]{:S(2)}) collective-permute-start(bf16[2304,128]{1,0:T(8,128)(2,1)S(1)} %after.1.refs_3_.refs_5_), channel_id=1, source_target_pairs={{0,1},{1,0},{2,3},{3,2},{4,5},{5,4},{6,7},{7,6},{8,9},{9,8},{10,11... | collective-permute-start | bytes 1769480 | tf_op jit(solution)/shard_map/ppermute | solution.py:315
  30.1 32.7 %collective-permute-start.6 = (bf16[2304,128]{1,0:T(8,128)(2,1)S(1)}, bf16[2304,128]{1,0:T(8,128)(2,1)S(1)}, u32[]{:S(2)}, u32[]{:S(2)}) collective-permute-start(bf16[2304,128]{1,0:T(8,128)(2,1)S(1)} %after.1.refs_3_.refs_5_), channel_id=1, source_target_pairs={{0,3},{1,2},{2,1},{3,0},{4,7},{5,6},{6,5},{7,4},{8,11},{9,10},{10,... | collective-permute-start | bytes 1769480 | tf_op jit(solution)/shard_map/ppermute | solution.py:315
  32.3 30.6 %collective-permute-start.5 = (bf16[2304,128]{1,0:T(8,128)(2,1)S(1)}, bf16[2304,128]{1,0:T(8,128)(2,1)S(1)}, u32[]{:S(2)}, u32[]{:S(2)}) collective-permute-start(bf16[2304,128]{1,0:T(8,128)(2,1)S(1)} %after.1.refs_3_.refs_5_), channel_id=1, source_target_pairs={{0,2},{1,3},{2,0},{3,1},{4,6},{5,7},{6,4},{7,5},{8,10},{9,11},{10,... | collective-permute-start | bytes 1769480 | tf_op jit(solution)/shard_map/ppermute | solution.py:315
  45.9 3.1 %collective-permute-start.4 = (bf16[32,8,128]{2,1,0:T(8,128)(2,1)S(1)}, bf16[32,8,128]{2,1,0:T(8,128)(2,1)S(1)}, u32[]{:S(2)}, u32[]{:S(2)}) collective-permute-start(bf16[32,8,128]{2,1,0:T(8,128)(2,1)S(1)} %all_to_all.56.refs_9_.refs_2_.refs_4_), channel_id=1, source_target_pairs={{0,4},{4,0},{8,12},{12,8},{16,20},{20,16},{24,28},{28,24},{32,36},... | collective-permute-start | bytes 196616 | tf_op jit(solution)/shard_map/ppermute | solution.py:290
  61.3 2.5 %collective-permute-start.8 = (bf16[32,8,128]{2,1,0:T(8,128)(2,1)S(1)}, bf16[32,8,128]{2,1,0:T(8,128)(2,1)S(1)}, u32[]{:S(2)}, u32[]{:S(2)}) collective-permute-start(bf16[32,8,128]{2,1,0:T(8,128)(2,1)S(1)} %all_to_all.57.refs_11_.refs_2_.refs_5_), channel_id=1, source_target_pairs={{0,4},{4,0},{8,12},{12,8},{16,20},{20,16},{24,28},{28,24},{32,36},... | collective-permute-start | bytes 196616 | tf_op jit(solution)/shard_map/ppermute | solution.py:290
  76.1 2.5 %collective-permute-start.9 = (bf16[32,8,128]{2,1,0:T(8,128)(2,1)S(1)}, bf16[32,8,128]{2,1,0:T(8,128)(2,1)S(1)}, u32[]{:S(2)}, u32[]{:S(2)}) collective-permute-start(bf16[32,8,128]{2,1,0:T(8,128)(2,1)S(1)} %all_to_all.58.refs_13_.refs_2_.refs_6_), channel_id=1, source_target_pairs={{0,4},{4,0},{8,12},{12,8},{16,20},{20,16},{24,28},{28,24},{32,36},... | collective-permute-start | bytes 196616 | tf_op jit(solution)/shard_map/ppermute | solution.py:290
  90.9 2.5 %collective-permute-start.10 = (bf16[32,8,128]{2,1,0:T(8,128)(2,1)S(1)}, bf16[32,8,128]{2,1,0:T(8,128)(2,1)S(1)}, u32[]{:S(2)}, u32[]{:S(2)}) collective-permute-start(bf16[32,8,128]{2,1,0:T(8,128)(2,1)S(1)} %all_to_all.59.front.refs_15_.refs_2_.refs_7_), channel_id=1, source_target_pairs={{0,4},{4,0},{8,12},{12,8},{16,20},{20,16},{24,28},{28,24},{32,36},... | collective-permute-start | bytes 196616 | tf_op jit(solution)/shard_map/ppermute | solution.py:290
  94.4 1.3 collective-permute-start.11
  108.1 2.6 %collective-permute-start.12 = (bf16[32,8,128]{2,1,0:T(8,128)(2,1)S(1)}, bf16[32,8,128]{2,1,0:T(8,128)(2,1)S(1)}, u32[]{:S(2)}, u32[]{:S(2)}) collective-permute-start(bf16[32,8,128]{2,1,0:T(8,128)(2,1)S(1)} %get-tuple-element.42), channel_id=1, source_target_pairs={{0,4},{4,0},{8,12},{12,8},{16,20},{20,16},{24,28},{28,24},{32,36},... | collective-permute-start | bytes 196616 | tf_op jit(solution)/shard_map/ppermute | solution.py:290
  122.9 2.7 %collective-permute-start.13 = (bf16[32,8,128]{2,1,0:T(8,128)(2,1)S(1)}, bf16[32,8,128]{2,1,0:T(8,128)(2,1)S(1)}, u32[]{:S(2)}, u32[]{:S(2)}) collective-permute-start(bf16[32,8,128]{2,1,0:T(8,128)(2,1)S(1)} %get-tuple-element.45), channel_id=1, source_target_pairs={{0,4},{4,0},{8,12},{12,8},{16,20},{20,16},{24,28},{28,24},{32,36},... | collective-permute-start | bytes 196616 | tf_op jit(solution)/shard_map/ppermute | solution.py:290
  137.9 2.6 %collective-permute-start.14 = (bf16[32,8,128]{2,1,0:T(8,128)(2,1)S(1)}, bf16[32,8,128]{2,1,0:T(8,128)(2,1)S(1)}, u32[]{:S(2)}, u32[]{:S(2)}) collective-permute-start(bf16[32,8,128]{2,1,0:T(8,128)(2,1)S(1)} %get-tuple-element.48), channel_id=1, source_target_pairs={{0,4},{4,0},{8,12},{12,8},{16,20},{20,16},{24,28},{28,24},{32,36},... | collective-permute-start | bytes 196616 | tf_op jit(solution)/shard_map/ppermute | solution.py:290
  152.8 2.6 %collective-permute-start.15 = (bf16[32,8,128]{2,1,0:T(8,128)(2,1)S(1)}, bf16[32,8,128]{2,1,0:T(8,128)(2,1)S(1)}, u32[]{:S(2)}, u32[]{:S(2)}) collective-permute-start(bf16[32,8,128]{2,1,0:T(8,128)(2,1)S(1)} %get-tuple-element.51), channel_id=1, source_target_pairs={{0,4},{4,0},{8,12},{12,8},{16,20},{20,16},{24,28},{28,24},{32,36},... | collective-permute-start | bytes 196616 | tf_op jit(solution)/shard_map/ppermute | solution.py:290

commit v13 on v12

--- a/solution.py
+++ b/solution.py
@@ -313,7 +313,7 @@
     def around(x):
         return [held(x)] + [
             held(lax.ppermute(x, "col", [(i, i ^ s) for i in range(cols)]))
-            for s in (2, 3, 1)
+            for s in (2, 1, 3)
         ]
 
     factor = far_off(factor.reshape(rows * plan.entries * width, width))

time: 177 us -> 178 us (level)
  no operation moved by 1% of the time
where the time goes in v13:
time: 178 us; the launch traced here: 177 us
  blocking collectives  134 us (75%)
  starting transfers between devices  26.5 us (15%)
  waiting for transfers between devices  8.04 us (5%)
  Pallas kernels  6.82 us (4%)
    all_to_all x10, blocking collectives, among(): lax.all_to_all(x, 'chain', 0, 0, tiled=True, axis_index_groups=groups)  127 us
    ppermute x10, starting transfers between devices, across(): return held(lax.ppermute(x, 'chain', [(i, i ^ 1) for i in range(lanes)]))  17.3 us
    ppermute x6, starting transfers between devices, around(): lax.ppermute(x, 'col', [(i, i ^ s) for i in range(cols)])  9.23 us
    ppermute x10, waiting for transfers between devices, across(): return held(lax.ppermute(x, 'chain', [(i, i ^ 1) for i in range(lanes)]))  8.02 us
    all_to_all x1, blocking collectives, per_device(): whole = lax.all_to_all(shares, 'col', 0, 0, tiled=True)  7.23 us
  transfers between devices with their start and end apart: 16, of which 9 were waited for; matrix products, arithmetic and copies ran while one was open for 0% of the time, Pallas kernels for 1%

profile of v13, /device:TPU:1, one launch (start us, length us, event | category | flops | bytes accessed | tf_op | source)
XLA Modules:
  0.0 176.6 jit_solution(12353364703517200600)
XLA Ops:
  0.6 1.3 forward_first.1
  2.0 3.4 %collective-permute-start.3 = (bf16[1552,128]{1,0:T(8,128)(2,1)S(1)}, bf16[1552,128]{1,0:T(8,128)(2,1)S(1)}, u32[]{:S(2)}, u32[]{:S(2)}) collective-permute-start(bf16[1552,128]{1,0:T(8,128)(2,1)S(1)} %get-tuple-element.34.refs_5_.refs_3_), channel_id=1, source_target_pairs={{0,3},{1,2},{2,1},{3,0},{4,7},{5,6},{6,5},{7,4},{8,11},{9,10},{10,... | collective-permute-start | bytes 1191944 | tf_op jit(solution)/shard_map/ppermute | solution.py:315
  5.4 1.3 collective-permute-start.1
  6.7 19.9 %all_to_all.55.refs_3_.refs_7_.segment = bf16[32,8,128]{2,1,0:T(8,128)(2,1)S(1)} all-to-all(bf16[32,8,128]{2,1,0:T(8,128)(2,1)S(1)} %get-tuple-element.33), channel_id=1, replica_groups={{0,8,16,24,32,40,48,56,64,72,80,88,96,104,112,120,128,136,144,152,160,1..., dimensions={0} | all-to-all | bytes 131072 | tf_op jit(solution)/shard_map/all_to_all | solution.py:295
  26.6 2.9 %collective-permute-start = (bf16[32,8,128]{2,1,0:T(8,128)(2,1)S(1)}, bf16[32,8,128]{2,1,0:T(8,128)(2,1)S(1)}, u32[]{:S(2)}, u32[]{:S(2)}) collective-permute-start(bf16[32,8,128]{2,1,0:T(8,128)(2,1)S(1)} %all_to_all.55.refs_3_.refs_7_.segment), channel_id=1, source_target_pairs={{0,4},{4,0},{8,12},{12,8},{16,20},{20,16},{24,28},{28,24},{32,36},... | collective-permute-start | bytes 196616 | tf_op jit(solution)/shard_map/ppermute | solution.py:290
  29.5 2.5 %collective-permute-start.7 = (bf16[2304,128]{1,0:T(8,128)(2,1)S(1)}, bf16[2304,128]{1,0:T(8,128)(2,1)S(1)}, u32[]{:S(2)}, u32[]{:S(2)}) collective-permute-start(bf16[2304,128]{1,0:T(8,128)(2,1)S(1)} %after.1.refs_3_.refs_5_), channel_id=1, source_target_pairs={{0,3},{1,2},{2,1},{3,0},{4,7},{5,6},{6,5},{7,4},{8,11},{9,10},{10,... | collective-permute-start | bytes 1769480 | tf_op jit(solution)/shard_map/ppermute | solution.py:315
  32.0 2.1 %collective-permute-start.5 = (bf16[2304,128]{1,0:T(8,128)(2,1)S(1)}, bf16[2304,128]{1,0:T(8,128)(2,1)S(1)}, u32[]{:S(2)}, u32[]{:S(2)}) collective-permute-start(bf16[2304,128]{1,0:T(8,128)(2,1)S(1)} %after.1.refs_3_.refs_5_), channel_id=1, source_target_pairs={{0,2},{1,3},{2,0},{3,1},{4,6},{5,7},{6,4},{7,5},{8,10},{9,11},{10,... | collective-permute-start | bytes 1769480 | tf_op jit(solution)/shard_map/ppermute | solution.py:315
  34.1 1.2 forward_second.1
  35.3 11.8 %all_to_all.56.refs_9_.refs_2_.refs_4_ = bf16[32,8,128]{2,1,0:T(8,128)(2,1)S(1)} all-to-all(bf16[32,8,128]{2,1,0:T(8,128)(2,1)S(1)} %get-tuple-element.36), channel_id=1, replica_groups={{0,8,16,24,32,40,48,56,64,72,80,88,96,104,112,120,128,136,144,152,160,1..., dimensions={0} | all-to-all | bytes 131072 | tf_op jit(solution)/shard_map/all_to_all | solution.py:295
  47.2 2.2 %collective-permute-start.4 = (bf16[32,8,128]{2,1,0:T(8,128)(2,1)S(1)}, bf16[32,8,128]{2,1,0:T(8,128)(2,1)S(1)}, u32[]{:S(2)}, u32[]{:S(2)}) collective-permute-start(bf16[32,8,128]{2,1,0:T(8,128)(2,1)S(1)} %all_to_all.56.refs_9_.refs_2_.refs_4_), channel_id=1, source_target_pairs={{0,4},{4,0},{8,12},{12,8},{16,20},{20,16},{24,28},{28,24},{32,36},... | collective-permute-start | bytes 196616 | tf_op jit(solution)/shard_map/ppermute | solution.py:290
  49.3 0.9 collective-permute-done.4.refs_10_
  50.6 11.9 %all_to_all.57.refs_11_.refs_2_.refs_5_ = bf16[32,8,128]{2,1,0:T(8,128)(2,1)S(1)} all-to-all(bf16[32,8,128]{2,1,0:T(8,128)(2,1)S(1)} %forward_level_2.1), channel_id=1, replica_groups={{0,8,16,24,32,40,48,56,64,72,80,88,96,104,112,120,128,136,144,152,160,1..., dimensions={0} | all-to-all | bytes 131072 | tf_op jit(solution)/shard_map/all_to_all | solution.py:295
  62.5 1.6 collective-permute-start.8
  65.4 11.9 %all_to_all.58.refs_13_.refs_2_.refs_6_ = bf16[32,8,128]{2,1,0:T(8,128)(2,1)S(1)} all-to-all(bf16[32,8,128]{2,1,0:T(8,128)(2,1)S(1)} %forward_level_3.1), channel_id=1, replica_groups={{0,8,16,24,32,40,48,56,64,72,80,88,96,104,112,120,128,136,144,152,160,1..., dimensions={0} | all-to-all | bytes 131072 | tf_op jit(solution)/shard_map/all_to_all | solution.py:295
  77.3 1.6 collective-permute-start.9
  78.9 0.9 collective-permute-done.9.refs_14_
  80.2 11.9 %all_to_all.59.front.refs_15_.refs_2_.refs_7_ = bf16[32,8,128]{2,1,0:T(8,128)(2,1)S(1)} all-to-all(bf16[32,8,128]{2,1,0:T(8,128)(2,1)S(1)} %forward_level_4.1), channel_id=1, replica_groups={{0,8,16,24,32,40,48,56,64,72,80,88,96,104,112,120,128,136,144,152,160,1..., dimensions={0} | all-to-all | bytes 131072 | tf_op jit(solution)/shard_map/all_to_all | solution.py:295
  92.2 1.6 collective-permute-start.10
  94.6 1.0 turn_level.1
  96.1 0.9 collective-permute-done.11.other
  97.1 11.8 %all_to_all.60.refs_3_ = bf16[32,8,128]{2,1,0:T(8,128)(2,1)S(1)} all-to-all(bf16[32,8,128]{2,1,0:T(8,128)(2,1)S(1)} %add_other.5), channel_id=1, replica_groups={{0,8,16,24,32,40,48,56,64,72,80,88,96,104,112,120,128,136,144,152,160,1..., dimensions={0} | all-to-all | bytes 131072 | tf_op jit(solution)/shard_map/all_to_all | solution.py:295
  109.3 1.7 collective-permute-start.12
  111.0 0.9 collective-permute-done.12.other
  111.9 11.8 %all_to_all.61.refs_3_ = bf16[32,8,128]{2,1,0:T(8,128)(2,1)S(1)} all-to-all(bf16[32,8,128]{2,1,0:T(8,128)(2,1)S(1)} %add_other.6), channel_id=1, replica_groups={{0,8,16,24,32,40,48,56,64,72,80,88,96,104,112,120,128,136,144,152,160,1..., dimensions={0} | all-to-all | bytes 131072 | tf_op jit(solution)/shard_map/all_to_all | solution.py:295
  124.2 1.9 %collective-permute-start.13 = (bf16[32,8,128]{2,1,0:T(8,128)(2,1)S(1)}, bf16[32,8,128]{2,1,0:T(8,128)(2,1)S(1)}, u32[]{:S(2)}, u32[]{:S(2)}) collective-permute-start(bf16[32,8,128]{2,1,0:T(8,128)(2,1)S(1)} %get-tuple-element.45), channel_id=1, source_target_pairs={{0,4},{4,0},{8,12},{12,8},{16,20},{20,16},{24,28},{28,24},{32,36},... | collective-permute-start | bytes 196616 | tf_op jit(solution)/shard_map/ppermute | solution.py:290
  126.1 0.9 collective-permute-done.13.other
  127.0 11.8 %all_to_all.62.refs_3_ = bf16[32,8,128]{2,1,0:T(8,128)(2,1)S(1)} all-to-all(bf16[32,8,128]{2,1,0:T(8,128)(2,1)S(1)} %add_other.7), channel_id=1, replica_groups={{0,8,16,24,32,40,48,56,64,72,80,88,96,104,112,120,128,136,144,152,160,1..., dimensions={0} | all-to-all | bytes 131072 | tf_op jit(solution)/shard_map/all_to_all | solution.py:295
  139.2 1.7 collective-permute-start.14
  141.8 11.8 %all_to_all.63.refs_3_ = bf16[32,8,128]{2,1,0:T(8,128)(2,1)S(1)} all-to-all(bf16[32,8,128]{2,1,0:T(8,128)(2,1)S(1)} %add_other.8), channel_id=1, replica_groups={{0,8,16,24,32,40,48,56,64,72,80,88,96,104,112,120,128,136,144,152,160,1..., dimensions={0} | all-to-all | bytes 131072 | tf_op jit(solution)/shard_map/all_to_all | solution.py:295
  154.1 1.7 collective-permute-start.15
  156.7 11.8 %all_to_all.64.refs_2_ = bf16[32,8,128]{2,1,0:T(8,128)(2,1)S(1)} all-to-all(bf16[32,8,128]{2,1,0:T(8,128)(2,1)S(1)} %add_other.9), channel_id=1, replica_groups={{0,8,16,24,32,40,48,56,64,72,80,88,96,104,112,120,128,136,144,152,160,1..., dimensions={0} | all-to-all | bytes 131072 | tf_op jit(solution)/shard_map/all_to_all | solution.py:295
  168.7 7.2 %all_to_all.65 = bf16[4,8,8,128]{3,2,1,0:T(8,128)(2,1)S(1)} all-to-all(bf16[4,8,8,128]{3,2,1,0:T(8,128)(2,1)S(1)} %finish.1), channel_id=1, replica_groups=mesh['chain'=64,'col'=4] {'col'}, dimensions={0} | all-to-all | bytes 131072 | tf_op jit(solution)/shard_map/all_to_all | solution.py:449
  (31 shorter events, 7.8 us)
Async XLA Ops:
  2.0 30.0 %collective-permute-start.3 = (bf16[1552,128]{1,0:T(8,128)(2,1)S(1)}, bf16[1552,128]{1,0:T(8,128)(2,1)S(1)}, u32[]{:S(2)}, u32[]{:S(2)}) collective-permute-start(bf16[1552,128]{1,0:T(8,128)(2,1)S(1)} %get-tuple-element.34.refs_5_.refs_3_), channel_id=1, source_target_pairs={{0,3},{1,2},{2,1},{3,0},{4,7},{5,6},{6,5},{7,4},{8,11},{9,10},{10,... | collective-permute-start | bytes 1191944 | tf_op jit(solution)/shard_map/ppermute | solution.py:315
  5.4 28.7 %collective-permute-start.2 = (bf16[1552,128]{1,0:T(8,128)(2,1)S(1)}, bf16[1552,128]{1,0:T(8,128)(2,1)S(1)}, u32[]{:S(2)}, u32[]{:S(2)}) collective-permute-start(bf16[1552,128]{1,0:T(8,128)(2,1)S(1)} %get-tuple-element.34.refs_5_.refs_3_), channel_id=1, source_target_pairs={{0,1},{1,0},{2,3},{3,2},{4,5},{5,4},{6,7},{7,6},{8,9},{9,8},{10,11... | collective-permute-start | bytes 1191944 | tf_op jit(solution)/shard_map/ppermute | solution.py:315
  5.4 28.7 %collective-permute-start.1 = (bf16[1552,128]{1,0:T(8,128)(2,1)S(1)}, bf16[1552,128]{1,0:T(8,128)(2,1)S(1)}, u32[]{:S(2)}, u32[]{:S(2)}) collective-permute-start(bf16[1552,128]{1,0:T(8,128)(2,1)S(1)} %get-tuple-element.34.refs_5_.refs_3_), channel_id=1, source_target_pairs={{0,2},{1,3},{2,0},{3,1},{4,6},{5,7},{6,4},{7,5},{8,10},{9,11},{10,... | collective-permute-start | bytes 1191944 | tf_op jit(solution)/shard_map/ppermute | solution.py:315
  26.6 5.4 %collective-permute-start = (bf16[32,8,128]{2,1,0:T(8,128)(2,1)S(1)}, bf16[32,8,128]{2,1,0:T(8,128)(2,1)S(1)}, u32[]{:S(2)}, u32[]{:S(2)}) collective-permute-start(bf16[32,8,128]{2,1,0:T(8,128)(2,1)S(1)} %all_to_all.55.refs_3_.refs_7_.segment), channel_id=1, source_target_pairs={{0,4},{4,0},{8,12},{12,8},{16,20},{20,16},{24,28},{28,24},{32,36},... | collective-permute-start | bytes 196616 | tf_op jit(solution)/shard_map/ppermute | solution.py:290
  29.5 34.6 %collective-permute-start.7 = (bf16[2304,128]{1,0:T(8,128)(2,1)S(1)}, bf16[2304,128]{1,0:T(8,128)(2,1)S(1)}, u32[]{:S(2)}, u32[]{:S(2)}) collective-permute-start(bf16[2304,128]{1,0:T(8,128)(2,1)S(1)} %after.1.refs_3_.refs_5_), channel_id=1, source_target_pairs={{0,3},{1,2},{2,1},{3,0},{4,7},{5,6},{6,5},{7,4},{8,11},{9,10},{10,... | collective-permute-start | bytes 1769480 | tf_op jit(solution)/shard_map/ppermute | solution.py:315
  32.0 32.1 %collective-permute-start.6 = (bf16[2304,128]{1,0:T(8,128)(2,1)S(1)}, bf16[2304,128]{1,0:T(8,128)(2,1)S(1)}, u32[]{:S(2)}, u32[]{:S(2)}) collective-permute-start(bf16[2304,128]{1,0:T(8,128)(2,1)S(1)} %after.1.refs_3_.refs_5_), channel_id=1, source_target_pairs={{0,1},{1,0},{2,3},{3,2},{4,5},{5,4},{6,7},{7,6},{8,9},{9,8},{10,11... | collective-permute-start | bytes 1769480 | tf_op jit(solution)/shard_map/ppermute | solution.py:315
  32.0 32.1 %collective-permute-start.5 = (bf16[2304,128]{1,0:T(8,128)(2,1)S(1)}, bf16[2304,128]{1,0:T(8,128)(2,1)S(1)}, u32[]{:S(2)}, u32[]{:S(2)}) collective-permute-start(bf16[2304,128]{1,0:T(8,128)(2,1)S(1)} %after.1.refs_3_.refs_5_), channel_id=1, source_target_pairs={{0,2},{1,3},{2,0},{3,1},{4,6},{5,7},{6,4},{7,5},{8,10},{9,11},{10,... | collective-permute-start | bytes 1769480 | tf_op jit(solution)/shard_map/ppermute | solution.py:315
  47.2 3.1 %collective-permute-start.4 = (bf16[32,8,128]{2,1,0:T(8,128)(2,1)S(1)}, bf16[32,8,128]{2,1,0:T(8,128)(2,1)S(1)}, u32[]{:S(2)}, u32[]{:S(2)}) collective-permute-start(bf16[32,8,128]{2,1,0:T(8,128)(2,1)S(1)} %all_to_all.56.refs_9_.refs_2_.refs_4_), channel_id=1, source_target_pairs={{0,4},{4,0},{8,12},{12,8},{16,20},{20,16},{24,28},{28,24},{32,36},... | collective-permute-start | bytes 196616 | tf_op jit(solution)/shard_map/ppermute | solution.py:290
  62.5 2.5 %collective-permute-start.8 = (bf16[32,8,128]{2,1,0:T(8,128)(2,1)S(1)}, bf16[32,8,128]{2,1,0:T(8,128)(2,1)S(1)}, u32[]{:S(2)}, u32[]{:S(2)}) collective-permute-start(bf16[32,8,128]{2,1,0:T(8,128)(2,1)S(1)} %all_to_all.57.refs_11_.refs_2_.refs_5_), channel_id=1, source_target_pairs={{0,4},{4,0},{8,12},{12,8},{16,20},{20,16},{24,28},{28,24},{32,36},... | collective-permute-start | bytes 196616 | tf_op jit(solution)/shard_map/ppermute | solution.py:290
  77.3 2.5 %collective-permute-start.9 = (bf16[32,8,128]{2,1,0:T(8,128)(2,1)S(1)}, bf16[32,8,128]{2,1,0:T(8,128)(2,1)S(1)}, u32[]{:S(2)}, u32[]{:S(2)}) collective-permute-start(bf16[32,8,128]{2,1,0:T(8,128)(2,1)S(1)} %all_to_all.58.refs_13_.refs_2_.refs_6_), channel_id=1, source_target_pairs={{0,4},{4,0},{8,12},{12,8},{16,20},{20,16},{24,28},{28,24},{32,36},... | collective-permute-start | bytes 196616 | tf_op jit(solution)/shard_map/ppermute | solution.py:290
  92.2 2.5 %collective-permute-start.10 = (bf16[32,8,128]{2,1,0:T(8,128)(2,1)S(1)}, bf16[32,8,128]{2,1,0:T(8,128)(2,1)S(1)}, u32[]{:S(2)}, u32[]{:S(2)}) collective-permute-start(bf16[32,8,128]{2,1,0:T(8,128)(2,1)S(1)} %all_to_all.59.front.refs_15_.refs_2_.refs_7_), channel_id=1, source_target_pairs={{0,4},{4,0},{8,12},{12,8},{16,20},{20,16},{24,28},{28,24},{32,36},... | collective-permute-start | bytes 196616 | tf_op jit(solution)/shard_map/ppermute | solution.py:290
  95.7 1.3 collective-permute-start.11
  109.3 2.6 %collective-permute-start.12 = (bf16[32,8,128]{2,1,0:T(8,128)(2,1)S(1)}, bf16[32,8,128]{2,1,0:T(8,128)(2,1)S(1)}, u32[]{:S(2)}, u32[]{:S(2)}) collective-permute-start(bf16[32,8,128]{2,1,0:T(8,128)(2,1)S(1)} %get-tuple-element.42), channel_id=1, source_target_pairs={{0,4},{4,0},{8,12},{12,8},{16,20},{20,16},{24,28},{28,24},{32,36},... | collective-permute-start | bytes 196616 | tf_op jit(solution)/shard_map/ppermute | solution.py:290
  124.2 2.8 %collective-permute-start.13 = (bf16[32,8,128]{2,1,0:T(8,128)(2,1)S(1)}, bf16[32,8,128]{2,1,0:T(8,128)(2,1)S(1)}, u32[]{:S(2)}, u32[]{:S(2)}) collective-permute-start(bf16[32,8,128]{2,1,0:T(8,128)(2,1)S(1)} %get-tuple-element.45), channel_id=1, source_target_pairs={{0,4},{4,0},{8,12},{12,8},{16,20},{20,16},{24,28},{28,24},{32,36},... | collective-permute-start | bytes 196616 | tf_op jit(solution)/shard_map/ppermute | solution.py:290
  139.2 2.6 %collective-permute-start.14 = (bf16[32,8,128]{2,1,0:T(8,128)(2,1)S(1)}, bf16[32,8,128]{2,1,0:T(8,128)(2,1)S(1)}, u32[]{:S(2)}, u32[]{:S(2)}) collective-permute-start(bf16[32,8,128]{2,1,0:T(8,128)(2,1)S(1)} %get-tuple-element.48), channel_id=1, source_target_pairs={{0,4},{4,0},{8,12},{12,8},{16,20},{20,16},{24,28},{28,24},{32,36},... | collective-permute-start | bytes 196616 | tf_op jit(solution)/shard_map/ppermute | solution.py:290
  154.1 2.6 %collective-permute-start.15 = (bf16[32,8,128]{2,1,0:T(8,128)(2,1)S(1)}, bf16[32,8,128]{2,1,0:T(8,128)(2,1)S(1)}, u32[]{:S(2)}, u32[]{:S(2)}) collective-permute-start(bf16[32,8,128]{2,1,0:T(8,128)(2,1)S(1)} %get-tuple-element.51), channel_id=1, source_target_pairs={{0,4},{4,0},{8,12},{12,8},{16,20},{20,16},{24,28},{28,24},{32,36},... | collective-permute-start | bytes 196616 | tf_op jit(solution)/shard_map/ppermute | solution.py:290

commit v14 on v13

--- a/solution.py
+++ b/solution.py
@@ -310,11 +310,12 @@
         )(held(own), across(other))
         return among(whole)
 
-    def around(x):
-        return [held(x)] + [
-            held(lax.ppermute(x, "col", [(i, i ^ s) for i in range(cols)]))
-            for s in (2, 1, 3)
-        ]
+    def around(x, order):
+        got = {
+            s: held(lax.ppermute(x, "col", [(i, i ^ s) for i in range(cols)]))
+            for s in order
+        }
+        return [held(x), got[2], got[3], got[1]]
 
     factor = far_off(factor.reshape(rows * plan.entries * width, width))
     far_shape = pltpu.VMEM((len(plan.far) * plan.deep, width), BF16)
@@ -348,7 +349,7 @@
         far_off(inverse.reshape(rows, width, width)),
     )
     rights, inverses, sizes = held(rights), held(inverses), scalars(sizes)
-    near = around(own)
+    near = around(own, (2, 3, 1))
     fronts = exchange(first)
     later = pl.pallas_call(
         after,
@@ -359,7 +360,7 @@
         compiler_params=params,
         name="after",
     )(held(later), fronts[0])
-    far = around(later)
+    far = around(later, (1, 3, 2))
 
     mine, table = pl.pallas_call(
         functools.partial(forward_second, plan),

time: 178 us -> 177 us (level)
  no operation moved by 1% of the time
where the time goes in v14:
time: 177 us; the launch traced here: 176 us
  blocking collectives  135 us (76%)
  starting transfers between devices  25.3 us (14%)
  waiting for transfers between devices  8.04 us (5%)
  Pallas kernels  6.8 us (4%)
    all_to_all x10, blocking collectives, among(): lax.all_to_all(x, 'chain', 0, 0, tiled=True, axis_index_groups=groups)  127 us
    ppermute x10, starting transfers between devices, across(): return held(lax.ppermute(x, 'chain', [(i, i ^ 1) for i in range(lanes)]))  17 us
    ppermute x6, starting transfers between devices, around(): lax.ppermute(x, 'col', [(i, i ^ s) for i in range(cols)])  8.33 us
    ppermute x10, waiting for transfers between devices, across(): return held(lax.ppermute(x, 'chain', [(i, i ^ 1) for i in range(lanes)]))  8.02 us
    all_to_all x1, blocking collectives, per_device(): whole = lax.all_to_all(shares, 'col', 0, 0, tiled=True)  8 us
  transfers between devices with their start and end apart: 16, of which 9 were waited for; matrix products, arithmetic and copies ran while one was open for 0% of the time, Pallas kernels for 1%

profile of v14, /device:TPU:1, one launch (start us, length us, event | category | flops | bytes accessed | tf_op | source)
XLA Modules:
  0.0 176.1 jit_solution(10346479422968510805)
XLA Ops:
  0.6 1.3 forward_first.1
  2.0 2.1 %collective-permute-start.3 = (bf16[1552,128]{1,0:T(8,128)(2,1)S(1)}, bf16[1552,128]{1,0:T(8,128)(2,1)S(1)}, u32[]{:S(2)}, u32[]{:S(2)}) collective-permute-start(bf16[1552,128]{1,0:T(8,128)(2,1)S(1)} %get-tuple-element.34.refs_5_.refs_3_), channel_id=1, source_target_pairs={{0,1},{1,0},{2,3},{3,2},{4,5},{5,4},{6,7},{7,6},{8,9},{9,8},{10,11... | collective-permute-start | bytes 1191944 | tf_op jit(solution)/shard_map/ppermute | solution.py:315
  4.1 1.8 %collective-permute-start.2 = (bf16[1552,128]{1,0:T(8,128)(2,1)S(1)}, bf16[1552,128]{1,0:T(8,128)(2,1)S(1)}, u32[]{:S(2)}, u32[]{:S(2)}) collective-permute-start(bf16[1552,128]{1,0:T(8,128)(2,1)S(1)} %get-tuple-element.34.refs_5_.refs_3_), channel_id=1, source_target_pairs={{0,3},{1,2},{2,1},{3,0},{4,7},{5,6},{6,5},{7,4},{8,11},{9,10},{10,... | collective-permute-start | bytes 1191944 | tf_op jit(solution)/shard_map/ppermute | solution.py:315
  6.6 19.8 %all_to_all.55.refs_3_.refs_7_.segment = bf16[32,8,128]{2,1,0:T(8,128)(2,1)S(1)} all-to-all(bf16[32,8,128]{2,1,0:T(8,128)(2,1)S(1)} %get-tuple-element.33), channel_id=1, replica_groups={{0,8,16,24,32,40,48,56,64,72,80,88,96,104,112,120,128,136,144,152,160,1..., dimensions={0} | all-to-all | bytes 131072 | tf_op jit(solution)/shard_map/all_to_all | solution.py:295
  26.4 2.7 %collective-permute-start = (bf16[32,8,128]{2,1,0:T(8,128)(2,1)S(1)}, bf16[32,8,128]{2,1,0:T(8,128)(2,1)S(1)}, u32[]{:S(2)}, u32[]{:S(2)}) collective-permute-start(bf16[32,8,128]{2,1,0:T(8,128)(2,1)S(1)} %all_to_all.55.refs_3_.refs_7_.segment), channel_id=1, source_target_pairs={{0,4},{4,0},{8,12},{12,8},{16,20},{20,16},{24,28},{28,24},{32,36},... | collective-permute-start | bytes 196616 | tf_op jit(solution)/shard_map/ppermute | solution.py:290
  29.1 1.1 collective-permute-start.7
  30.1 2.2 %collective-permute-start.6 = (bf16[2304,128]{1,0:T(8,128)(2,1)S(1)}, bf16[2304,128]{1,0:T(8,128)(2,1)S(1)}, u32[]{:S(2)}, u32[]{:S(2)}) collective-permute-start(bf16[2304,128]{1,0:T(8,128)(2,1)S(1)} %after.1.refs_3_.refs_5_), channel_id=1, source_target_pairs={{0,3},{1,2},{2,1},{3,0},{4,7},{5,6},{6,5},{7,4},{8,11},{9,10},{10,... | collective-permute-start | bytes 1769480 | tf_op jit(solution)/shard_map/ppermute | solution.py:315
  32.8 1.2 forward_second.1
  34.0 11.8 %all_to_all.56.refs_9_.refs_2_.refs_4_ = bf16[32,8,128]{2,1,0:T(8,128)(2,1)S(1)} all-to-all(bf16[32,8,128]{2,1,0:T(8,128)(2,1)S(1)} %get-tuple-element.36), channel_id=1, replica_groups={{0,8,16,24,32,40,48,56,64,72,80,88,96,104,112,120,128,136,144,152,160,1..., dimensions={0} | all-to-all | bytes 131072 | tf_op jit(solution)/shard_map/all_to_all | solution.py:295
  45.9 2.2 %collective-permute-start.4 = (bf16[32,8,128]{2,1,0:T(8,128)(2,1)S(1)}, bf16[32,8,128]{2,1,0:T(8,128)(2,1)S(1)}, u32[]{:S(2)}, u32[]{:S(2)}) collective-permute-start(bf16[32,8,128]{2,1,0:T(8,128)(2,1)S(1)} %all_to_all.56.refs_9_.refs_2_.refs_4_), channel_id=1, source_target_pairs={{0,4},{4,0},{8,12},{12,8},{16,20},{20,16},{24,28},{28,24},{32,36},... | collective-permute-start | bytes 196616 | tf_op jit(solution)/shard_map/ppermute | solution.py:290
  48.0 0.9 collective-permute-done.4.refs_10_
  49.4 11.9 %all_to_all.57.refs_11_.refs_2_.refs_5_ = bf16[32,8,128]{2,1,0:T(8,128)(2,1)S(1)} all-to-all(bf16[32,8,128]{2,1,0:T(8,128)(2,1)S(1)} %forward_level_2.1), channel_id=1, replica_groups={{0,8,16,24,32,40,48,56,64,72,80,88,96,104,112,120,128,136,144,152,160,1..., dimensions={0} | all-to-all | bytes 131072 | tf_op jit(solution)/shard_map/all_to_all | solution.py:295
  61.3 1.6 collective-permute-start.8
  64.2 11.9 %all_to_all.58.refs_13_.refs_2_.refs_6_ = bf16[32,8,128]{2,1,0:T(8,128)(2,1)S(1)} all-to-all(bf16[32,8,128]{2,1,0:T(8,128)(2,1)S(1)} %forward_level_3.1), channel_id=1, replica_groups={{0,8,16,24,32,40,48,56,64,72,80,88,96,104,112,120,128,136,144,152,160,1..., dimensions={0} | all-to-all | bytes 131072 | tf_op jit(solution)/shard_map/all_to_all | solution.py:295
  76.1 1.6 collective-permute-start.9
  77.7 0.9 collective-permute-done.9.refs_14_
  79.0 11.9 %all_to_all.59.front.refs_15_.refs_2_.refs_7_ = bf16[32,8,128]{2,1,0:T(8,128)(2,1)S(1)} all-to-all(bf16[32,8,128]{2,1,0:T(8,128)(2,1)S(1)} %forward_level_4.1), channel_id=1, replica_groups={{0,8,16,24,32,40,48,56,64,72,80,88,96,104,112,120,128,136,144,152,160,1..., dimensions={0} | all-to-all | bytes 131072 | tf_op jit(solution)/shard_map/all_to_all | solution.py:295
  90.9 1.6 collective-permute-start.10
  93.4 1.0 turn_level.1
  94.9 0.9 collective-permute-done.11.other
  95.8 11.8 %all_to_all.60.refs_3_ = bf16[32,8,128]{2,1,0:T(8,128)(2,1)S(1)} all-to-all(bf16[32,8,128]{2,1,0:T(8,128)(2,1)S(1)} %add_other.5), channel_id=1, replica_groups={{0,8,16,24,32,40,48,56,64,72,80,88,96,104,112,120,128,136,144,152,160,1..., dimensions={0} | all-to-all | bytes 131072 | tf_op jit(solution)/shard_map/all_to_all | solution.py:295
  108.0 1.7 collective-permute-start.12
  109.7 0.9 collective-permute-done.12.other
  110.6 11.8 %all_to_all.61.refs_3_ = bf16[32,8,128]{2,1,0:T(8,128)(2,1)S(1)} all-to-all(bf16[32,8,128]{2,1,0:T(8,128)(2,1)S(1)} %add_other.6), channel_id=1, replica_groups={{0,8,16,24,32,40,48,56,64,72,80,88,96,104,112,120,128,136,144,152,160,1..., dimensions={0} | all-to-all | bytes 131072 | tf_op jit(solution)/shard_map/all_to_all | solution.py:295
  122.9 1.9 %collective-permute-start.13 = (bf16[32,8,128]{2,1,0:T(8,128)(2,1)S(1)}, bf16[32,8,128]{2,1,0:T(8,128)(2,1)S(1)}, u32[]{:S(2)}, u32[]{:S(2)}) collective-permute-start(bf16[32,8,128]{2,1,0:T(8,128)(2,1)S(1)} %get-tuple-element.45), channel_id=1, source_target_pairs={{0,4},{4,0},{8,12},{12,8},{16,20},{20,16},{24,28},{28,24},{32,36},... | collective-permute-start | bytes 196616 | tf_op jit(solution)/shard_map/ppermute | solution.py:290
  125.7 11.8 %all_to_all.62.refs_3_ = bf16[32,8,128]{2,1,0:T(8,128)(2,1)S(1)} all-to-all(bf16[32,8,128]{2,1,0:T(8,128)(2,1)S(1)} %add_other.7), channel_id=1, replica_groups={{0,8,16,24,32,40,48,56,64,72,80,88,96,104,112,120,128,136,144,152,160,1..., dimensions={0} | all-to-all | bytes 131072 | tf_op jit(solution)/shard_map/all_to_all | solution.py:295
  137.9 1.7 collective-permute-start.14
  140.6 11.8 %all_to_all.63.refs_3_ = bf16[32,8,128]{2,1,0:T(8,128)(2,1)S(1)} all-to-all(bf16[32,8,128]{2,1,0:T(8,128)(2,1)S(1)} %add_other.8), channel_id=1, replica_groups={{0,8,16,24,32,40,48,56,64,72,80,88,96,104,112,120,128,136,144,152,160,1..., dimensions={0} | all-to-all | bytes 131072 | tf_op jit(solution)/shard_map/all_to_all | solution.py:295
  152.8 1.6 collective-permute-start.15
  154.5 0.9 collective-permute-done.15.other
  155.4 11.8 %all_to_all.64.refs_2_ = bf16[32,8,128]{2,1,0:T(8,128)(2,1)S(1)} all-to-all(bf16[32,8,128]{2,1,0:T(8,128)(2,1)S(1)} %add_other.9), channel_id=1, replica_groups={{0,8,16,24,32,40,48,56,64,72,80,88,96,104,112,120,128,136,144,152,160,1..., dimensions={0} | all-to-all | bytes 131072 | tf_op jit(solution)/shard_map/all_to_all | solution.py:295
  167.4 8.0 %all_to_all.65 = bf16[4,8,8,128]{3,2,1,0:T(8,128)(2,1)S(1)} all-to-all(bf16[4,8,8,128]{3,2,1,0:T(8,128)(2,1)S(1)} %finish.1), channel_id=1, replica_groups=mesh['chain'=64,'col'=4] {'col'}, dimensions={0} | all-to-all | bytes 131072 | tf_op jit(solution)/shard_map/all_to_all | solution.py:450
  (31 shorter events, 9.0 us)
Async XLA Ops:
  2.0 30.3 %collective-permute-start.3 = (bf16[1552,128]{1,0:T(8,128)(2,1)S(1)}, bf16[1552,128]{1,0:T(8,128)(2,1)S(1)}, u32[]{:S(2)}, u32[]{:S(2)}) collective-permute-start(bf16[1552,128]{1,0:T(8,128)(2,1)S(1)} %get-tuple-element.34.refs_5_.refs_3_), channel_id=1, source_target_pairs={{0,1},{1,0},{2,3},{3,2},{4,5},{5,4},{6,7},{7,6},{8,9},{9,8},{10,11... | collective-permute-start | bytes 1191944 | tf_op jit(solution)/shard_map/ppermute | solution.py:315
  4.1 28.7 %collective-permute-start.2 = (bf16[1552,128]{1,0:T(8,128)(2,1)S(1)}, bf16[1552,128]{1,0:T(8,128)(2,1)S(1)}, u32[]{:S(2)}, u32[]{:S(2)}) collective-permute-start(bf16[1552,128]{1,0:T(8,128)(2,1)S(1)} %get-tuple-element.34.refs_5_.refs_3_), channel_id=1, source_target_pairs={{0,3},{1,2},{2,1},{3,0},{4,7},{5,6},{6,5},{7,4},{8,11},{9,10},{10,... | collective-permute-start | bytes 1191944 | tf_op jit(solution)/shard_map/ppermute | solution.py:315
  5.9 26.9 %collective-permute-start.1 = (bf16[1552,128]{1,0:T(8,128)(2,1)S(1)}, bf16[1552,128]{1,0:T(8,128)(2,1)S(1)}, u32[]{:S(2)}, u32[]{:S(2)}) collective-permute-start(bf16[1552,128]{1,0:T(8,128)(2,1)S(1)} %get-tuple-element.34.refs_5_.refs_3_), channel_id=1, source_target_pairs={{0,2},{1,3},{2,0},{3,1},{4,6},{5,7},{6,4},{7,5},{8,10},{9,11},{10,... | collective-permute-start | bytes 1191944 | tf_op jit(solution)/shard_map/ppermute | solution.py:315
  26.4 3.7 %collective-permute-start = (bf16[32,8,128]{2,1,0:T(8,128)(2,1)S(1)}, bf16[32,8,128]{2,1,0:T(8,128)(2,1)S(1)}, u32[]{:S(2)}, u32[]{:S(2)}) collective-permute-start(bf16[32,8,128]{2,1,0:T(8,128)(2,1)S(1)} %all_to_all.55.refs_3_.refs_7_.segment), channel_id=1, source_target_pairs={{0,4},{4,0},{8,12},{12,8},{16,20},{20,16},{24,28},{28,24},{32,36},... | collective-permute-start | bytes 196616 | tf_op jit(solution)/shard_map/ppermute | solution.py:290
  29.1 33.8 %collective-permute-start.7 = (bf16[2304,128]{1,0:T(8,128)(2,1)S(1)}, bf16[2304,128]{1,0:T(8,128)(2,1)S(1)}, u32[]{:S(2)}, u32[]{:S(2)}) collective-permute-start(bf16[2304,128]{1,0:T(8,128)(2,1)S(1)} %after.1.refs_3_.refs_5_), channel_id=1, source_target_pairs={{0,1},{1,0},{2,3},{3,2},{4,5},{5,4},{6,7},{7,6},{8,9},{9,8},{10,11... | collective-permute-start | bytes 1769480 | tf_op jit(solution)/shard_map/ppermute | solution.py:315
  30.1 32.7 %collective-permute-start.6 = (bf16[2304,128]{1,0:T(8,128)(2,1)S(1)}, bf16[2304,128]{1,0:T(8,128)(2,1)S(1)}, u32[]{:S(2)}, u32[]{:S(2)}) collective-permute-start(bf16[2304,128]{1,0:T(8,128)(2,1)S(1)} %after.1.refs_3_.refs_5_), channel_id=1, source_target_pairs={{0,3},{1,2},{2,1},{3,0},{4,7},{5,6},{6,5},{7,4},{8,11},{9,10},{10,... | collective-permute-start | bytes 1769480 | tf_op jit(solution)/shard_map/ppermute | solution.py:315
  32.3 30.6 %collective-permute-start.5 = (bf16[2304,128]{1,0:T(8,128)(2,1)S(1)}, bf16[2304,128]{1,0:T(8,128)(2,1)S(1)}, u32[]{:S(2)}, u32[]{:S(2)}) collective-permute-start(bf16[2304,128]{1,0:T(8,128)(2,1)S(1)} %after.1.refs_3_.refs_5_), channel_id=1, source_target_pairs={{0,2},{1,3},{2,0},{3,1},{4,6},{5,7},{6,4},{7,5},{8,10},{9,11},{10,... | collective-permute-start | bytes 1769480 | tf_op jit(solution)/shard_map/ppermute | solution.py:315
  45.9 3.1 %collective-permute-start.4 = (bf16[32,8,128]{2,1,0:T(8,128)(2,1)S(1)}, bf16[32,8,128]{2,1,0:T(8,128)(2,1)S(1)}, u32[]{:S(2)}, u32[]{:S(2)}) collective-permute-start(bf16[32,8,128]{2,1,0:T(8,128)(2,1)S(1)} %all_to_all.56.refs_9_.refs_2_.refs_4_), channel_id=1, source_target_pairs={{0,4},{4,0},{8,12},{12,8},{16,20},{20,16},{24,28},{28,24},{32,36},... | collective-permute-start | bytes 196616 | tf_op jit(solution)/shard_map/ppermute | solution.py:290
  61.3 2.5 %collective-permute-start.8 = (bf16[32,8,128]{2,1,0:T(8,128)(2,1)S(1)}, bf16[32,8,128]{2,1,0:T(8,128)(2,1)S(1)}, u32[]{:S(2)}, u32[]{:S(2)}) collective-permute-start(bf16[32,8,128]{2,1,0:T(8,128)(2,1)S(1)} %all_to_all.57.refs_11_.refs_2_.refs_5_), channel_id=1, source_target_pairs={{0,4},{4,0},{8,12},{12,8},{16,20},{20,16},{24,28},{28,24},{32,36},... | collective-permute-start | bytes 196616 | tf_op jit(solution)/shard_map/ppermute | solution.py:290
  76.1 2.5 %collective-permute-start.9 = (bf16[32,8,128]{2,1,0:T(8,128)(2,1)S(1)}, bf16[32,8,128]{2,1,0:T(8,128)(2,1)S(1)}, u32[]{:S(2)}, u32[]{:S(2)}) collective-permute-start(bf16[32,8,128]{2,1,0:T(8,128)(2,1)S(1)} %all_to_all.58.refs_13_.refs_2_.refs_6_), channel_id=1, source_target_pairs={{0,4},{4,0},{8,12},{12,8},{16,20},{20,16},{24,28},{28,24},{32,36},... | collective-permute-start | bytes 196616 | tf_op jit(solution)/shard_map/ppermute | solution.py:290
  90.9 2.5 %collective-permute-start.10 = (bf16[32,8,128]{2,1,0:T(8,128)(2,1)S(1)}, bf16[32,8,128]{2,1,0:T(8,128)(2,1)S(1)}, u32[]{:S(2)}, u32[]{:S(2)}) collective-permute-start(bf16[32,8,128]{2,1,0:T(8,128)(2,1)S(1)} %all_to_all.59.front.refs_15_.refs_2_.refs_7_), channel_id=1, source_target_pairs={{0,4},{4,0},{8,12},{12,8},{16,20},{20,16},{24,28},{28,24},{32,36},... | collective-permute-start | bytes 196616 | tf_op jit(solution)/shard_map/ppermute | solution.py:290
  94.4 1.3 collective-permute-start.11
  108.0 2.6 %collective-permute-start.12 = (bf16[32,8,128]{2,1,0:T(8,128)(2,1)S(1)}, bf16[32,8,128]{2,1,0:T(8,128)(2,1)S(1)}, u32[]{:S(2)}, u32[]{:S(2)}) collective-permute-start(bf16[32,8,128]{2,1,0:T(8,128)(2,1)S(1)} %get-tuple-element.42), channel_id=1, source_target_pairs={{0,4},{4,0},{8,12},{12,8},{16,20},{20,16},{24,28},{28,24},{32,36},... | collective-permute-start | bytes 196616 | tf_op jit(solution)/shard_map/ppermute | solution.py:290
  122.9 2.8 %collective-permute-start.13 = (bf16[32,8,128]{2,1,0:T(8,128)(2,1)S(1)}, bf16[32,8,128]{2,1,0:T(8,128)(2,1)S(1)}, u32[]{:S(2)}, u32[]{:S(2)}) collective-permute-start(bf16[32,8,128]{2,1,0:T(8,128)(2,1)S(1)} %get-tuple-element.45), channel_id=1, source_target_pairs={{0,4},{4,0},{8,12},{12,8},{16,20},{20,16},{24,28},{28,24},{32,36},... | collective-permute-start | bytes 196616 | tf_op jit(solution)/shard_map/ppermute | solution.py:290
  137.9 2.6 %collective-permute-start.14 = (bf16[32,8,128]{2,1,0:T(8,128)(2,1)S(1)}, bf16[32,8,128]{2,1,0:T(8,128)(2,1)S(1)}, u32[]{:S(2)}, u32[]{:S(2)}) collective-permute-start(bf16[32,8,128]{2,1,0:T(8,128)(2,1)S(1)} %get-tuple-element.48), channel_id=1, source_target_pairs={{0,4},{4,0},{8,12},{12,8},{16,20},{20,16},{24,28},{28,24},{32,36},... | collective-permute-start | bytes 196616 | tf_op jit(solution)/shard_map/ppermute | solution.py:290
  152.8 2.5 %collective-permute-start.15 = (bf16[32,8,128]{2,1,0:T(8,128)(2,1)S(1)}, bf16[32,8,128]{2,1,0:T(8,128)(2,1)S(1)}, u32[]{:S(2)}, u32[]{:S(2)}) collective-permute-start(bf16[32,8,128]{2,1,0:T(8,128)(2,1)S(1)} %get-tuple-element.51), channel_id=1, source_target_pairs={{0,4},{4,0},{8,12},{12,8},{16,20},{20,16},{24,28},{28,24},{32,36},... | collective-permute-start | bytes 196616 | tf_op jit(solution)/shard_map/ppermute | solution.py:290

commit v15 on v12

--- a/solution.py
+++ b/solution.py
@@ -99,9 +99,9 @@
     col = lax.axis_index("col")
     loads = [
         (level_size, sizes),
+        (factor, blocks),
         (inverse, diagonal),
         (right.at[:, col], sides),
-        (factor, blocks),
         (pattern, pats),
     ]
     copies = [
@@ -113,8 +113,8 @@
     wide[...] = jnp.zeros(wide.shape, F32)
     copies[0].wait()
     slots = [locate(plan, k, sizes)[0] for k in range(plan.levels)]
-    copies[1].wait()
     copies[2].wait()
+    copies[3].wait()
     segment = lax.dot_general(
         sides[0], diagonal[0], NT, preferred_element_type=F32
     ).astype(BF16)
@@ -122,7 +122,7 @@
     for k in range(plan.levels):
         rights[k] = sides[slots[k]]
         inverses[k] = diagonal[slots[k]]
-    copies[3].wait()
+    copies[1].wait()
     copies[4].wait()
     for target, levels in ((near, plan.near), (far, plan.far)):
         for i, k in enumerate(levels):

time: 177 us -> 177 us (level)
  no operation moved by 1% of the time
where the time goes in v15:
time: 177 us; the launch traced here: 176 us
  blocking collectives  135 us (76%)
  starting transfers between devices  25.3 us (14%)
  waiting for transfers between devices  8.04 us (5%)
  Pallas kernels  6.91 us (4%)
    all_to_all x10, blocking collectives, among(): lax.all_to_all(x, 'chain', 0, 0, tiled=True, axis_index_groups=groups)  127 us
    ppermute x10, starting transfers between devices, across(): return held(lax.ppermute(x, 'chain', [(i, i ^ 1) for i in range(lanes)]))  17 us
    ppermute x6, starting transfers between devices, around(): lax.ppermute(x, 'col', [(i, i ^ s) for i in range(cols)])  8.33 us
    ppermute x10, waiting for transfers between devices, across(): return held(lax.ppermute(x, 'chain', [(i, i ^ 1) for i in range(lanes)]))  8.02 us
    all_to_all x1, blocking collectives, per_device(): whole = lax.all_to_all(shares, 'col', 0, 0, tiled=True)  7.98 us
  transfers between devices with their start and end apart: 16, of which 9 were waited for; matrix products, arithmetic and copies ran while one was open for 0% of the time, Pallas kernels for 1%

profile of v15, /device:TPU:1, one launch (start us, length us, event | category | flops | bytes accessed | tf_op | source)
XLA Modules:
  0.0 176.2 jit_solution(12036924553996690757)
XLA Ops:
  0.6 1.4 forward_first.1
  2.1 2.1 %collective-permute-start.3 = (bf16[1552,128]{1,0:T(8,128)(2,1)S(1)}, bf16[1552,128]{1,0:T(8,128)(2,1)S(1)}, u32[]{:S(2)}, u32[]{:S(2)}) collective-permute-start(bf16[1552,128]{1,0:T(8,128)(2,1)S(1)} %get-tuple-element.34.refs_5_.refs_3_), channel_id=1, source_target_pairs={{0,1},{1,0},{2,3},{3,2},{4,5},{5,4},{6,7},{7,6},{8,9},{9,8},{10,11... | collective-permute-start | bytes 1191944 | tf_op jit(solution)/shard_map/ppermute | solution.py:315
  4.2 1.8 %collective-permute-start.2 = (bf16[1552,128]{1,0:T(8,128)(2,1)S(1)}, bf16[1552,128]{1,0:T(8,128)(2,1)S(1)}, u32[]{:S(2)}, u32[]{:S(2)}) collective-permute-start(bf16[1552,128]{1,0:T(8,128)(2,1)S(1)} %get-tuple-element.34.refs_5_.refs_3_), channel_id=1, source_target_pairs={{0,3},{1,2},{2,1},{3,0},{4,7},{5,6},{6,5},{7,4},{8,11},{9,10},{10,... | collective-permute-start | bytes 1191944 | tf_op jit(solution)/shard_map/ppermute | solution.py:315
  6.6 19.8 %all_to_all.55.refs_3_.refs_7_.segment = bf16[32,8,128]{2,1,0:T(8,128)(2,1)S(1)} all-to-all(bf16[32,8,128]{2,1,0:T(8,128)(2,1)S(1)} %get-tuple-element.33), channel_id=1, replica_groups={{0,8,16,24,32,40,48,56,64,72,80,88,96,104,112,120,128,136,144,152,160,1..., dimensions={0} | all-to-all | bytes 131072 | tf_op jit(solution)/shard_map/all_to_all | solution.py:295
  26.5 2.7 %collective-permute-start = (bf16[32,8,128]{2,1,0:T(8,128)(2,1)S(1)}, bf16[32,8,128]{2,1,0:T(8,128)(2,1)S(1)}, u32[]{:S(2)}, u32[]{:S(2)}) collective-permute-start(bf16[32,8,128]{2,1,0:T(8,128)(2,1)S(1)} %all_to_all.55.refs_3_.refs_7_.segment), channel_id=1, source_target_pairs={{0,4},{4,0},{8,12},{12,8},{16,20},{20,16},{24,28},{28,24},{32,36},... | collective-permute-start | bytes 196616 | tf_op jit(solution)/shard_map/ppermute | solution.py:290
  29.1 1.1 collective-permute-start.7
  30.2 2.2 %collective-permute-start.6 = (bf16[2304,128]{1,0:T(8,128)(2,1)S(1)}, bf16[2304,128]{1,0:T(8,128)(2,1)S(1)}, u32[]{:S(2)}, u32[]{:S(2)}) collective-permute-start(bf16[2304,128]{1,0:T(8,128)(2,1)S(1)} %after.1.refs_3_.refs_5_), channel_id=1, source_target_pairs={{0,3},{1,2},{2,1},{3,0},{4,7},{5,6},{6,5},{7,4},{8,11},{9,10},{10,... | collective-permute-start | bytes 1769480 | tf_op jit(solution)/shard_map/ppermute | solution.py:315
  32.9 1.2 forward_second.1
  34.1 11.8 %all_to_all.56.refs_9_.refs_2_.refs_4_ = bf16[32,8,128]{2,1,0:T(8,128)(2,1)S(1)} all-to-all(bf16[32,8,128]{2,1,0:T(8,128)(2,1)S(1)} %get-tuple-element.36), channel_id=1, replica_groups={{0,8,16,24,32,40,48,56,64,72,80,88,96,104,112,120,128,136,144,152,160,1..., dimensions={0} | all-to-all | bytes 131072 | tf_op jit(solution)/shard_map/all_to_all | solution.py:295
  46.0 2.2 %collective-permute-start.4 = (bf16[32,8,128]{2,1,0:T(8,128)(2,1)S(1)}, bf16[32,8,128]{2,1,0:T(8,128)(2,1)S(1)}, u32[]{:S(2)}, u32[]{:S(2)}) collective-permute-start(bf16[32,8,128]{2,1,0:T(8,128)(2,1)S(1)} %all_to_all.56.refs_9_.refs_2_.refs_4_), channel_id=1, source_target_pairs={{0,4},{4,0},{8,12},{12,8},{16,20},{20,16},{24,28},{28,24},{32,36},... | collective-permute-start | bytes 196616 | tf_op jit(solution)/shard_map/ppermute | solution.py:290
  48.1 0.9 collective-permute-done.4.refs_10_
  49.4 11.9 %all_to_all.57.refs_11_.refs_2_.refs_5_ = bf16[32,8,128]{2,1,0:T(8,128)(2,1)S(1)} all-to-all(bf16[32,8,128]{2,1,0:T(8,128)(2,1)S(1)} %forward_level_2.1), channel_id=1, replica_groups={{0,8,16,24,32,40,48,56,64,72,80,88,96,104,112,120,128,136,144,152,160,1..., dimensions={0} | all-to-all | bytes 131072 | tf_op jit(solution)/shard_map/all_to_all | solution.py:295
  61.3 1.6 collective-permute-start.8
  64.2 11.9 %all_to_all.58.refs_13_.refs_2_.refs_6_ = bf16[32,8,128]{2,1,0:T(8,128)(2,1)S(1)} all-to-all(bf16[32,8,128]{2,1,0:T(8,128)(2,1)S(1)} %forward_level_3.1), channel_id=1, replica_groups={{0,8,16,24,32,40,48,56,64,72,80,88,96,104,112,120,128,136,144,152,160,1..., dimensions={0} | all-to-all | bytes 131072 | tf_op jit(solution)/shard_map/all_to_all | solution.py:295
  76.1 1.6 collective-permute-start.9
  77.7 0.9 collective-permute-done.9.refs_14_
  79.1 11.9 %all_to_all.59.front.refs_15_.refs_2_.refs_7_ = bf16[32,8,128]{2,1,0:T(8,128)(2,1)S(1)} all-to-all(bf16[32,8,128]{2,1,0:T(8,128)(2,1)S(1)} %forward_level_4.1), channel_id=1, replica_groups={{0,8,16,24,32,40,48,56,64,72,80,88,96,104,112,120,128,136,144,152,160,1..., dimensions={0} | all-to-all | bytes 131072 | tf_op jit(solution)/shard_map/all_to_all | solution.py:295
  91.0 1.6 collective-permute-start.10
  93.4 1.0 turn_level.1
  94.9 0.9 collective-permute-done.11.other
  95.8 11.8 %all_to_all.60.refs_3_ = bf16[32,8,128]{2,1,0:T(8,128)(2,1)S(1)} all-to-all(bf16[32,8,128]{2,1,0:T(8,128)(2,1)S(1)} %add_other.5), channel_id=1, replica_groups={{0,8,16,24,32,40,48,56,64,72,80,88,96,104,112,120,128,136,144,152,160,1..., dimensions={0} | all-to-all | bytes 131072 | tf_op jit(solution)/shard_map/all_to_all | solution.py:295
  108.1 1.7 collective-permute-start.12
  109.8 0.9 collective-permute-done.12.other
  110.7 11.8 %all_to_all.61.refs_3_ = bf16[32,8,128]{2,1,0:T(8,128)(2,1)S(1)} all-to-all(bf16[32,8,128]{2,1,0:T(8,128)(2,1)S(1)} %add_other.6), channel_id=1, replica_groups={{0,8,16,24,32,40,48,56,64,72,80,88,96,104,112,120,128,136,144,152,160,1..., dimensions={0} | all-to-all | bytes 131072 | tf_op jit(solution)/shard_map/all_to_all | solution.py:295
  123.0 1.8 %collective-permute-start.13 = (bf16[32,8,128]{2,1,0:T(8,128)(2,1)S(1)}, bf16[32,8,128]{2,1,0:T(8,128)(2,1)S(1)}, u32[]{:S(2)}, u32[]{:S(2)}) collective-permute-start(bf16[32,8,128]{2,1,0:T(8,128)(2,1)S(1)} %get-tuple-element.45), channel_id=1, source_target_pairs={{0,4},{4,0},{8,12},{12,8},{16,20},{20,16},{24,28},{28,24},{32,36},... | collective-permute-start | bytes 196616 | tf_op jit(solution)/shard_map/ppermute | solution.py:290
  124.8 0.9 collective-permute-done.13.other
  125.7 11.8 %all_to_all.62.refs_3_ = bf16[32,8,128]{2,1,0:T(8,128)(2,1)S(1)} all-to-all(bf16[32,8,128]{2,1,0:T(8,128)(2,1)S(1)} %add_other.7), channel_id=1, replica_groups={{0,8,16,24,32,40,48,56,64,72,80,88,96,104,112,120,128,136,144,152,160,1..., dimensions={0} | all-to-all | bytes 131072 | tf_op jit(solution)/shard_map/all_to_all | solution.py:295
  138.0 1.7 collective-permute-start.14
  140.7 11.8 %all_to_all.63.refs_3_ = bf16[32,8,128]{2,1,0:T(8,128)(2,1)S(1)} all-to-all(bf16[32,8,128]{2,1,0:T(8,128)(2,1)S(1)} %add_other.8), channel_id=1, replica_groups={{0,8,16,24,32,40,48,56,64,72,80,88,96,104,112,120,128,136,144,152,160,1..., dimensions={0} | all-to-all | bytes 131072 | tf_op jit(solution)/shard_map/all_to_all | solution.py:295
  152.9 1.7 collective-permute-start.15
  155.5 11.8 %all_to_all.64.refs_2_ = bf16[32,8,128]{2,1,0:T(8,128)(2,1)S(1)} all-to-all(bf16[32,8,128]{2,1,0:T(8,128)(2,1)S(1)} %add_other.9), channel_id=1, replica_groups={{0,8,16,24,32,40,48,56,64,72,80,88,96,104,112,120,128,136,144,152,160,1..., dimensions={0} | all-to-all | bytes 131072 | tf_op jit(solution)/shard_map/all_to_all | solution.py:295
  167.5 8.0 %all_to_all.65 = bf16[4,8,8,128]{3,2,1,0:T(8,128)(2,1)S(1)} all-to-all(bf16[4,8,8,128]{3,2,1,0:T(8,128)(2,1)S(1)} %finish.1), channel_id=1, replica_groups=mesh['chain'=64,'col'=4] {'col'}, dimensions={0} | all-to-all | bytes 131072 | tf_op jit(solution)/shard_map/all_to_all | solution.py:449
  (31 shorter events, 9.0 us)
Async XLA Ops:
  2.1 30.3 %collective-permute-start.3 = (bf16[1552,128]{1,0:T(8,128)(2,1)S(1)}, bf16[1552,128]{1,0:T(8,128)(2,1)S(1)}, u32[]{:S(2)}, u32[]{:S(2)}) collective-permute-start(bf16[1552,128]{1,0:T(8,128)(2,1)S(1)} %get-tuple-element.34.refs_5_.refs_3_), channel_id=1, source_target_pairs={{0,1},{1,0},{2,3},{3,2},{4,5},{5,4},{6,7},{7,6},{8,9},{9,8},{10,11... | collective-permute-start | bytes 1191944 | tf_op jit(solution)/shard_map/ppermute | solution.py:315
  4.2 28.7 %collective-permute-start.2 = (bf16[1552,128]{1,0:T(8,128)(2,1)S(1)}, bf16[1552,128]{1,0:T(8,128)(2,1)S(1)}, u32[]{:S(2)}, u32[]{:S(2)}) collective-permute-start(bf16[1552,128]{1,0:T(8,128)(2,1)S(1)} %get-tuple-element.34.refs_5_.refs_3_), channel_id=1, source_target_pairs={{0,3},{1,2},{2,1},{3,0},{4,7},{5,6},{6,5},{7,4},{8,11},{9,10},{10,... | collective-permute-start | bytes 1191944 | tf_op jit(solution)/shard_map/ppermute | solution.py:315
  6.0 26.9 %collective-permute-start.1 = (bf16[1552,128]{1,0:T(8,128)(2,1)S(1)}, bf16[1552,128]{1,0:T(8,128)(2,1)S(1)}, u32[]{:S(2)}, u32[]{:S(2)}) collective-permute-start(bf16[1552,128]{1,0:T(8,128)(2,1)S(1)} %get-tuple-element.34.refs_5_.refs_3_), channel_id=1, source_target_pairs={{0,2},{1,3},{2,0},{3,1},{4,6},{5,7},{6,4},{7,5},{8,10},{9,11},{10,... | collective-permute-start | bytes 1191944 | tf_op jit(solution)/shard_map/ppermute | solution.py:315
  26.5 3.7 %collective-permute-start = (bf16[32,8,128]{2,1,0:T(8,128)(2,1)S(1)}, bf16[32,8,128]{2,1,0:T(8,128)(2,1)S(1)}, u32[]{:S(2)}, u32[]{:S(2)}) collective-permute-start(bf16[32,8,128]{2,1,0:T(8,128)(2,1)S(1)} %all_to_all.55.refs_3_.refs_7_.segment), channel_id=1, source_target_pairs={{0,4},{4,0},{8,12},{12,8},{16,20},{20,16},{24,28},{28,24},{32,36},... | collective-permute-start | bytes 196616 | tf_op jit(solution)/shard_map/ppermute | solution.py:290
  29.1 33.8 %collective-permute-start.7 = (bf16[2304,128]{1,0:T(8,128)(2,1)S(1)}, bf16[2304,128]{1,0:T(8,128)(2,1)S(1)}, u32[]{:S(2)}, u32[]{:S(2)}) collective-permute-start(bf16[2304,128]{1,0:T(8,128)(2,1)S(1)} %after.1.refs_3_.refs_5_), channel_id=1, source_target_pairs={{0,1},{1,0},{2,3},{3,2},{4,5},{5,4},{6,7},{7,6},{8,9},{9,8},{10,11... | collective-permute-start | bytes 1769480 | tf_op jit(solution)/shard_map/ppermute | solution.py:315
  30.2 32.7 %collective-permute-start.6 = (bf16[2304,128]{1,0:T(8,128)(2,1)S(1)}, bf16[2304,128]{1,0:T(8,128)(2,1)S(1)}, u32[]{:S(2)}, u32[]{:S(2)}) collective-permute-start(bf16[2304,128]{1,0:T(8,128)(2,1)S(1)} %after.1.refs_3_.refs_5_), channel_id=1, source_target_pairs={{0,3},{1,2},{2,1},{3,0},{4,7},{5,6},{6,5},{7,4},{8,11},{9,10},{10,... | collective-permute-start | bytes 1769480 | tf_op jit(solution)/shard_map/ppermute | solution.py:315
  32.4 30.6 %collective-permute-start.5 = (bf16[2304,128]{1,0:T(8,128)(2,1)S(1)}, bf16[2304,128]{1,0:T(8,128)(2,1)S(1)}, u32[]{:S(2)}, u32[]{:S(2)}) collective-permute-start(bf16[2304,128]{1,0:T(8,128)(2,1)S(1)} %after.1.refs_3_.refs_5_), channel_id=1, source_target_pairs={{0,2},{1,3},{2,0},{3,1},{4,6},{5,7},{6,4},{7,5},{8,10},{9,11},{10,... | collective-permute-start | bytes 1769480 | tf_op jit(solution)/shard_map/ppermute | solution.py:315
  46.0 3.1 %collective-permute-start.4 = (bf16[32,8,128]{2,1,0:T(8,128)(2,1)S(1)}, bf16[32,8,128]{2,1,0:T(8,128)(2,1)S(1)}, u32[]{:S(2)}, u32[]{:S(2)}) collective-permute-start(bf16[32,8,128]{2,1,0:T(8,128)(2,1)S(1)} %all_to_all.56.refs_9_.refs_2_.refs_4_), channel_id=1, source_target_pairs={{0,4},{4,0},{8,12},{12,8},{16,20},{20,16},{24,28},{28,24},{32,36},... | collective-permute-start | bytes 196616 | tf_op jit(solution)/shard_map/ppermute | solution.py:290
  61.3 2.5 %collective-permute-start.8 = (bf16[32,8,128]{2,1,0:T(8,128)(2,1)S(1)}, bf16[32,8,128]{2,1,0:T(8,128)(2,1)S(1)}, u32[]{:S(2)}, u32[]{:S(2)}) collective-permute-start(bf16[32,8,128]{2,1,0:T(8,128)(2,1)S(1)} %all_to_all.57.refs_11_.refs_2_.refs_5_), channel_id=1, source_target_pairs={{0,4},{4,0},{8,12},{12,8},{16,20},{20,16},{24,28},{28,24},{32,36},... | collective-permute-start | bytes 196616 | tf_op jit(solution)/shard_map/ppermute | solution.py:290
  76.1 2.5 %collective-permute-start.9 = (bf16[32,8,128]{2,1,0:T(8,128)(2,1)S(1)}, bf16[32,8,128]{2,1,0:T(8,128)(2,1)S(1)}, u32[]{:S(2)}, u32[]{:S(2)}) collective-permute-start(bf16[32,8,128]{2,1,0:T(8,128)(2,1)S(1)} %all_to_all.58.refs_13_.refs_2_.refs_6_), channel_id=1, source_target_pairs={{0,4},{4,0},{8,12},{12,8},{16,20},{20,16},{24,28},{28,24},{32,36},... | collective-permute-start | bytes 196616 | tf_op jit(solution)/shard_map/ppermute | solution.py:290
  91.0 2.5 %collective-permute-start.10 = (bf16[32,8,128]{2,1,0:T(8,128)(2,1)S(1)}, bf16[32,8,128]{2,1,0:T(8,128)(2,1)S(1)}, u32[]{:S(2)}, u32[]{:S(2)}) collective-permute-start(bf16[32,8,128]{2,1,0:T(8,128)(2,1)S(1)} %all_to_all.59.front.refs_15_.refs_2_.refs_7_), channel_id=1, source_target_pairs={{0,4},{4,0},{8,12},{12,8},{16,20},{20,16},{24,28},{28,24},{32,36},... | collective-permute-start | bytes 196616 | tf_op jit(solution)/shard_map/ppermute | solution.py:290
  94.5 1.3 collective-permute-start.11
  108.1 2.6 %collective-permute-start.12 = (bf16[32,8,128]{2,1,0:T(8,128)(2,1)S(1)}, bf16[32,8,128]{2,1,0:T(8,128)(2,1)S(1)}, u32[]{:S(2)}, u32[]{:S(2)}) collective-permute-start(bf16[32,8,128]{2,1,0:T(8,128)(2,1)S(1)} %get-tuple-element.42), channel_id=1, source_target_pairs={{0,4},{4,0},{8,12},{12,8},{16,20},{20,16},{24,28},{28,24},{32,36},... | collective-permute-start | bytes 196616 | tf_op jit(solution)/shard_map/ppermute | solution.py:290
  123.0 2.7 %collective-permute-start.13 = (bf16[32,8,128]{2,1,0:T(8,128)(2,1)S(1)}, bf16[32,8,128]{2,1,0:T(8,128)(2,1)S(1)}, u32[]{:S(2)}, u32[]{:S(2)}) collective-permute-start(bf16[32,8,128]{2,1,0:T(8,128)(2,1)S(1)} %get-tuple-element.45), channel_id=1, source_target_pairs={{0,4},{4,0},{8,12},{12,8},{16,20},{20,16},{24,28},{28,24},{32,36},... | collective-permute-start | bytes 196616 | tf_op jit(solution)/shard_map/ppermute | solution.py:290
  138.0 2.7 %collective-permute-start.14 = (bf16[32,8,128]{2,1,0:T(8,128)(2,1)S(1)}, bf16[32,8,128]{2,1,0:T(8,128)(2,1)S(1)}, u32[]{:S(2)}, u32[]{:S(2)}) collective-permute-start(bf16[32,8,128]{2,1,0:T(8,128)(2,1)S(1)} %get-tuple-element.48), channel_id=1, source_target_pairs={{0,4},{4,0},{8,12},{12,8},{16,20},{20,16},{24,28},{28,24},{32,36},... | collective-permute-start | bytes 196616 | tf_op jit(solution)/shard_map/ppermute | solution.py:290
  152.9 2.6 %collective-permute-start.15 = (bf16[32,8,128]{2,1,0:T(8,128)(2,1)S(1)}, bf16[32,8,128]{2,1,0:T(8,128)(2,1)S(1)}, u32[]{:S(2)}, u32[]{:S(2)}) collective-permute-start(bf16[32,8,128]{2,1,0:T(8,128)(2,1)S(1)} %get-tuple-element.51), channel_id=1, source_target_pairs={{0,4},{4,0},{8,12},{12,8},{16,20},{20,16},{24,28},{28,24},{32,36},... | collective-permute-start | bytes 196616 | tf_op jit(solution)/shard_map/ppermute | solution.py:290
